TPU v7x, 256 devices: a whole 4x4x8 slice. The times are simulated.
256 devices in a mesh: cols: 64 (over x, z, core), lat: 4 (over y).
Axes of the slice: x: 4, y: 4, z: 8, core: 2. Of those that a mesh axis runs over, the one named last changes fastest.
Arguments:
- adjoint: float32 [10, 131072], P(None, ('cols', 'lat')), may hold values from -6 to 6
- impl_tiles: bfloat16 [1024, 7, 128, 128], P(('cols', 'lat')), may hold values from -0.1875 to 0.1875
- expl_tiles: bfloat16 [1024, 7, 128, 128], P(('cols', 'lat')), may hold values from -0.1875 to 0.1875
- impl_dest: int32 [1024, 4], P(('cols', 'lat')), may hold values from 0 to 63, all different within a row; in each aligned block of 4 rows (0 to 3, 4 to 7, ...) at most 2 rows name the same one
- impl_local: int32 [1024, 4], P(('cols', 'lat')), may hold values from 0 to 3
- expl_dest: int32 [1024, 4], P(('cols', 'lat')), may hold values from 0 to 63, all different within a row; in each aligned block of 4 rows (0 to 3, 4 to 7, ...) at most 2 rows name the same one
- expl_local: int32 [1024, 4], P(('cols', 'lat')), may hold values from 0 to 3
- column_depth: int32 [2048], P(('cols', 'lat')), may hold values from 4 to 64
- newton: int32 [2048], P(('cols', 'lat')), may hold values from 2 to 4
- jacobian: bfloat16 [10, 10, 131072], P(None, None, ('cols', 'lat')), may hold values from -0.41 to 0.21
- newton_inverse: bfloat16 [30, 30, 131072], P(None, None, ('cols', 'lat')), may hold values from -0.45 to 1.45
Outputs:
- sensitivity: float32 [10, 131072], P(None, ('cols', 'lat'))
Inputs may be any that keep to these rules, and one draw needn't show every extreme that they name: `impl_dest`: the 4 band blocks of a row block have different cols indices; the row blocks of one device name one cols index at most 2 times, and exactly 2 times on some devices. `expl_dest`: as for impl_dest.
All inputs are finite; a program needn't handle non-finite values.
Results may differ from a plain program's by a relative error of at most 0.0056.
Values sent between devices are 32-bit elements; how exact they have to be, the bound alone decides.
No kernel may reach another device: no remote copies, remote signals or barrier semaphores. Data moves between devices by JAX's collectives and lax.ppermute only.
A program may use at most 64 MiB of HBM per device.

v0:
```python
import math

import jax
import jax.numpy as jnp
from jax import lax
from jax.sharding import PartitionSpec as P

NEWT = 4
STEPS = 2


def shifted(value, axis, steps):
    count = lax.axis_size(axis)
    initial, last = (max(0, -steps), min(count, count - steps))
    return lax.ppermute(value, axis, [(source, source + steps) for source in range(initial, last)])


def radau_coef():
    root = math.sqrt(6.0)
    return jnp.array(
        [
            [
                (88.0 - 7.0 * root) / 360.0,
                (296.0 - 169.0 * root) / 1800.0,
                (-2.0 + 3.0 * root) / 225.0,
            ],
            [
                (296.0 + 169.0 * root) / 1800.0,
                (88.0 + 7.0 * root) / 360.0,
                (-2.0 - 3.0 * root) / 225.0,
            ],
            [(16.0 - root) / 36.0, (16.0 + root) / 36.0, 1.0 / 9.0],
        ],
        jnp.float32,
    )


def column_adjoint(forcing_in, jacobian, inverse, sweeps):
    highest = lax.Precision.HIGHEST
    coef = radau_coef()
    tracers, boxes = forcing_in.shape
    section_count = inverse.shape[0] // tracers
    forcing = (
        jnp.zeros((section_count, tracers, boxes), jnp.float32)
        .at[section_count - 1]
        .set(forcing_in)
    )
    sections = jnp.zeros((section_count, tracers, boxes), jnp.float32)
    for sweep in range(NEWT):
        mixed_term = jnp.einsum(
            "ijb,sib->sjb",
            jacobian,
            sections,
            precision=highest,
            preferred_element_type=jnp.float32,
        )
        image_term = sections - jnp.einsum("rs,rjb->sjb", coef, mixed_term, precision=highest)
        residual = (forcing - image_term).reshape(section_count * tracers, boxes)
        update = jnp.einsum(
            "qpb,qb->pb", inverse, residual, precision=highest, preferred_element_type=jnp.float32
        )
        sections = jnp.where(
            sweep < sweeps, sections + update.reshape(section_count, tracers, boxes), sections
        )
    return jnp.sum(sections, axis=0)


def body(
    adjoint,
    impl_tiles,
    expl_tiles,
    impl_dest,
    impl_local,
    expl_dest,
    expl_local,
    column_depth,
    newton,
    jacobian,
    newton_inverse,
):
    tracers, box_count = adjoint.shape
    row_blocks = impl_tiles.shape[0]
    block_len = impl_tiles.shape[2]
    band_count = impl_dest.shape[1]
    col_count = lax.axis_size("cols")
    columns = column_depth.shape[0]
    levels = box_count // columns
    level_ids = jnp.arange(levels, dtype=jnp.int32)
    wet_mask = (level_ids[None, :] < column_depth[:, None]).astype(jnp.float32).reshape(box_count)
    sweeps = jnp.broadcast_to(newton[:, None], (columns, levels)).reshape(box_count)

    def transport_transpose(field, tiles, dest, local):
        field_bf = field.astype(jnp.bfloat16).reshape(tracers, row_blocks, block_len)
        terms_all = jnp.einsum(
            "cri,rtij->rtcj", field_bf, tiles, preferred_element_type=jnp.float32
        )
        own_term = terms_all[:, 0]
        band_terms = terms_all[:, 1 : 1 + band_count].reshape(
            row_blocks * band_count, tracers * block_len
        )
        north_term = terms_all[:, band_count + 1]
        south_term = terms_all[:, band_count + 2]
        dest_flat = dest.reshape(-1)
        local_flat = local.reshape(-1)
        dense_target = dest_flat * row_blocks + local_flat
        dense_terms = jax.ops.segment_sum(
            band_terms, dense_target, num_segments=col_count * row_blocks
        )
        dense_terms = dense_terms.reshape(col_count, row_blocks, tracers, block_len)
        arrived = lax.psum_scatter(dense_terms, "cols", scatter_dimension=0, tiled=True).reshape(
            row_blocks, tracers, block_len
        )
        from_below = shifted(north_term, "lat", 1)
        from_above = shifted(south_term, "lat", -1)
        summed = own_term + arrived + from_below + from_above
        return summed.transpose(1, 0, 2).reshape(tracers, box_count)

    adjoint_now = adjoint
    for step_index in range(STEPS):
        transported = wet_mask * transport_transpose(adjoint_now, impl_tiles, impl_dest, impl_local)
        reacted = column_adjoint(transported, jacobian, newton_inverse, sweeps)
        adjoint_now = wet_mask * transport_transpose(reacted, expl_tiles, expl_dest, expl_local)
    return adjoint_now


def solution(mesh):
    return jax.shard_map(
        body,
        mesh=mesh,
        in_specs=(
            P(None, ("cols", "lat")),
            P(("cols", "lat"), None, None, None),
            P(("cols", "lat"), None, None, None),
            P(("cols", "lat"), None),
            P(("cols", "lat"), None),
            P(("cols", "lat"), None),
            P(("cols", "lat"), None),
            P(("cols", "lat")),
            P(("cols", "lat")),
            P(None, None, ("cols", "lat")),
            P(None, None, ("cols", "lat")),
        ),
        out_specs=P(None, ("cols", "lat")),
        check_vma=False,
    )
```

profile of v0, /device:TPU:24, one launch (start us, length us, event | category | flops | bytes accessed | tf_op | source)
XLA Modules:
  0.0 652.6 jit_solution(13809270490110483959)
XLA Ops:
  6.5 0.8 convert_element_type.40
  8.0 0.7 multiply_add_fusion.1
  8.8 1.1 scatter_custom_fusion
  9.9 1.6 reshape.300
  11.6 0.6 slice_bitcast_fusion.10
  12.2 1.3 collective-permute-start
  13.5 4.5 collective-permute-start.1
  18.0 2.1 copy.57
  20.2 2.8 fusion.23
  23.1 1.5 copy.58
  24.7 0.7 gt.39
  25.5 0.6 gt.37
  26.1 0.7 gt.35
  26.9 0.7 gt.33
  27.5 0.7 reshape.341
  28.2 127.0 %reduce-scatter.5.cloned.1.call-done = f32[1,4,10,128]{3,2,1,0:T(8,128)} async-done(((f32[64,4,10,128]{3,2,1,0:T(8,128)}), f32[1,4,10,128]{3,2,1,0:T(8,128)}) %reduce-scatter.5.cloned.1.call-update) | async-done | bytes 20496 | tf_op jit(solution)/shard_map/reduce_scatter | solution.py:110
  155.2 0.8 fusion.58
  156.4 1.4 fusion
  157.9 1.4 copy.65
  159.2 4.0 fusion.67
  163.3 1.5 copy.66
  165.2 1.4 fusion.1
  166.7 1.4 copy.73
  168.1 4.0 fusion.68
  172.1 1.5 copy.74
  174.0 1.4 fusion.2
  175.6 1.4 copy.81
  176.9 4.0 fusion.69
  181.0 1.5 copy.82
  182.9 1.4 fusion.3
  184.4 1.4 convolution_bitcast_fusion.2
  185.9 2.0 scatter_custom_fusion.1
  187.9 2.7 reshape.312
  190.9 1.3 collective-permute-start.2
  192.2 5.2 collective-permute-start.3
  198.4 131.2 %reduce-scatter.7.cloned.1.call-done = f32[1,4,10,128]{3,2,1,0:T(8,128)} async-done(((f32[64,4,10,128]{3,2,1,0:T(8,128)}), f32[1,4,10,128]{3,2,1,0:T(8,128)}) %reduce-scatter.7.cloned.1.call-update) | async-done | bytes 20496 | tf_op jit(solution)/shard_map/reduce_scatter | solution.py:110
  329.6 1.0 convolution_bitcast_fusion.1
  330.7 2.0 scatter_custom_fusion.2
  332.6 2.7 reshape.315
  335.4 1.3 collective-permute-start.4
  336.7 4.5 collective-permute-start.5
  341.2 1.6 collective-permute-done.5
  342.8 131.7 %reduce-scatter.9.cloned.1.call-done = f32[1,4,10,128]{3,2,1,0:T(8,128)} async-done(((f32[64,4,10,128]{3,2,1,0:T(8,128)}), f32[1,4,10,128]{3,2,1,0:T(8,128)}) %reduce-scatter.9.cloned.1.call-update) | async-done | bytes 20496 | tf_op jit(solution)/shard_map/reduce_scatter | solution.py:110
  474.5 0.8 fusion.49
  475.4 1.4 fusion.4
  476.9 1.4 copy.97
  478.3 4.1 fusion.70
  482.3 1.5 copy.98
  484.2 1.4 fusion.5
  485.8 1.4 copy.105
  487.1 4.0 fusion.71
  491.2 1.5 copy.106
  493.1 1.4 fusion.6
  494.6 1.4 copy.113
  496.0 4.0 fusion.72
  500.0 1.7 copy.114
  502.7 1.2 scatter_custom_fusion.3
  503.9 1.6 reshape.327
  505.6 1.3 collective-permute-start.6
  506.9 4.5 collective-permute-start.7
  511.4 1.6 collective-permute-done.7
  513.0 131.6 %reduce-scatter.11.cloned.1.call-done = f32[1,4,10,128]{3,2,1,0:T(8,128)} async-done(((f32[64,4,10,128]{3,2,1,0:T(8,128)}), f32[1,4,10,128]{3,2,1,0:T(8,128)}) %reduce-scatter.11.cloned.1.call-update) | async-done | bytes 20496 | tf_op jit(solution)/shard_map/reduce_scatter | solution.py:110
  644.6 0.8 fusion.45
  645.4 0.6 broadcast_multiply_fusion
  (133 shorter events, 6.5 us)
Async XLA Ops:
  6.5 1.2 copy-start
  6.5 148.6 %reduce-scatter.5.cloned.1.call-start = ((), (), s32[]{:S(2)}) async-start(), calls=%async_computation.4 | async-start | bytes 2129920 | tf_op jit(solution)/shard_map/reduce_scatter | solution.py:110
  8.8 2.7 copy-start.21
  11.5 6.6 %copy-start.3 = (bf16[10,10,512]{2,1,0:T(8,128)(2,1)S(1)}, bf16[10,10,512]{2,1,0:T(8,128)(2,1)}, u32[]{:S(2)}) copy-start(bf16[10,10,512]{2,1,0:T(8,128)(2,1)} %param.26) | copy-start | bytes 307204
  11.5 8.6 %copy-start.18 = (s32[8]{0:T(128)S(1)}, s32[8]{0:T(128)}, u32[]{:S(2)}) copy-start(s32[8]{0:T(128)} %param.24) | copy-start | bytes 100
  11.5 8.7 %copy-start.16 = (s32[4,4]{1,0:T(4,128)S(1)}, s32[4,4]{1,0:T(4,128)}, u32[]{:S(2)}) copy-start(s32[4,4]{1,0:T(4,128)} %param.23) | copy-start | bytes 196
  11.5 8.7 %copy-start.17 = (s32[4,4]{1,0:T(4,128)S(1)}, s32[4,4]{1,0:T(4,128)}, u32[]{:S(2)}) copy-start(s32[4,4]{1,0:T(4,128)} %param.22) | copy-start | bytes 196
  11.5 318.1 %reduce-scatter.7.cloned.1.call-start = ((), (), s32[]{:S(2)}) async-start(), calls=%async_computation.5 | async-start | bytes 2129920 | tf_op jit(solution)/shard_map/reduce_scatter | solution.py:110
  12.2 16.0 %collective-permute-start = (f32[4,10,128]{2,1,0:T(8,128)}, f32[4,10,128]{2,1,0:T(8,128)S(1)}, u32[]{:S(2)}, u32[]{:S(2)}) collective-permute-start(f32[4,10,128]{2,1,0:T(8,128)} %get-tuple-element.35), channel_id=1, source_target_pairs={{0,1},{1,2},{2,3},{4,5},{5,6},{6,7},{8,9},{9,10},{10,11},{12,13},{... | collective-permute-start | bytes 61448 | tf_op jit(solution)/shard_map/ppermute | solution.py:15
  13.5 14.7 %collective-permute-start.1 = (f32[4,10,128]{2,1,0:T(8,128)S(1)}, f32[4,10,128]{2,1,0:T(8,128)S(1)}, u32[]{:S(2)}, u32[]{:S(2)}) collective-permute-start(f32[4,10,128]{2,1,0:T(8,128)S(1)} %get-tuple-element.36), channel_id=1, source_target_pairs={{1,0},{2,1},{3,2},{5,4},{6,5},{7,6},{9,8},{10,9},{11,10},{13,12},{... | collective-permute-start | bytes 61448 | tf_op jit(solution)/shard_map/ppermute | solution.py:15
  20.1 2.9 copy-start.20
  20.2 135.8 %copy-start.4 = (f32[3,3,1]{0,1,2:T(4,128)S(1)}, f32[3,3,1]{0,1,2:T(4,128)}, u32[]{:S(2)}) copy-start(f32[3,3,1]{0,1,2:T(4,128)} %constant.82) | copy-start | bytes 112
  23.1 132.9 %copy-start.6 = (f32[512]{0:T(512)}, f32[512]{0:T(512)S(1)}, u32[]{:S(2)}) copy-start(f32[512]{0:T(512)S(1)} %reshape.330) | copy-start | bytes 6148
  156.0 1.9 copy-start.8
  163.3 3.4 copy-start.14
  172.1 3.4 copy-start.12
  181.0 3.4 copy-start.10
  187.9 2.7 copy-start.19
  190.6 283.9 %reduce-scatter.9.cloned.1.call-start = ((), (), s32[]{:S(2)}) async-start(), calls=%async_computation.6 | async-start | bytes 2129920 | tf_op jit(solution)/shard_map/reduce_scatter | solution.py:110
  190.9 7.0 %collective-permute-start.2 = (f32[4,10,128]{2,1,0:T(8,128)S(1)}, f32[4,10,128]{2,1,0:T(8,128)}, u32[]{:S(2)}, u32[]{:S(2)}) collective-permute-start(f32[4,10,128]{2,1,0:T(8,128)S(1)} %get-tuple-element.33), channel_id=1, source_target_pairs={{0,1},{1,2},{2,3},{4,5},{5,6},{6,7},{8,9},{9,10},{10,11},{12,13},{... | collective-permute-start | bytes 61448 | tf_op jit(solution)/shard_map/ppermute | solution.py:15
  192.2 6.1 collective-permute-start.3
  335.3 140.0 %copy-start.7 = (f32[512]{0:T(512)S(1)}, f32[512]{0:T(512)}, u32[]{:S(2)}) copy-start(f32[512]{0:T(512)} %copy-done.6) | copy-start | bytes 6148
  335.3 141.6 %copy-start.9 = (pred[512]{0:T(512)(128)(4,1)S(1)}, pred[512]{0:T(512)(128)(4,1)}, u32[]{:S(2)}) copy-start(pred[512]{0:T(512)(128)(4,1)} %gt.39) | copy-start | bytes 1540
  335.3 309.3 %reduce-scatter.11.cloned.1.call-start = ((), (), s32[]{:S(2)}) async-start(), calls=%async_computation.7 | async-start | bytes 2129920 | tf_op jit(solution)/shard_map/reduce_scatter | solution.py:110
  335.4 5.9 collective-permute-start.4
  336.7 6.1 collective-permute-start.5
  478.3 5.6 copy-start.5
  482.3 3.4 copy-start.15
  491.2 3.4 copy-start.13
  500.0 2.0 copy-start.1
  500.0 2.3 copy-start.11
  500.0 2.4 copy-start.2
  505.6 5.9 collective-permute-start.6
  506.9 6.1 collective-permute-start.7
Sparse Core Ops, SparseCore 0:
  11.6 143.5 reduce-scatter.4
  190.7 138.8 reduce-scatter.6
  335.4 138.9 reduce-scatter.8
  505.7 138.8 reduce-scatter.10
where the time goes:
time: 654 us; the launch traced here: 653 us
  waiting for transfers between devices  525 us (80%)
  local copies, waits for them, and re-layouts  35.3 us (5%)
  matrix products  32.1 us (5%)
  starting transfers between devices  24.1 us (4%)
  other arithmetic  22.3 us (3%)
  between operations  13.8 us (2%)
    reduce_scatter x4, waiting for transfers between devices, transport_transpose(): lax.psum_scatter(dense_terms, 'cols', scatter_dimension=0, tiled=True)  521 us
    dot_general x7, matrix products, column_adjoint(): jnp.einsum('ijb,sib->sjb', jacobian, sections, precision=highest, preferr...  27 us
    ppermute x8, starting transfers between devices, shifted(): lax.ppermute(value, axis, [(source, source + steps) for source in range(i...  23.9 us
  transfers between devices with their start and end apart: 12, of which 7 were waited for; matrix products, arithmetic and copies ran while one was open for 2% of the time, Pallas kernels for 0%

commit v1 on v0

v1 whole, which is shorter than its diff:
```python
import math

import jax
import jax.numpy as jnp
from jax import lax
from jax.experimental import pallas as pl
from jax.experimental.pallas import tpu as pltpu
from jax.sharding import PartitionSpec as P

NEWT = 4
STEPS = 2
TR = 10
SECTIONS = 3
BLK = 128
NBAND = 4
NB = 7
LEV = 64
RB = 4
NX, NZ, NCORE = 4, 8, 2
N_LAT = 4
TERMS = RB * NBAND
SLAB = RB * TR
F32 = jnp.float32

ROOT = math.sqrt(6.0)
COEF = [
    [(88.0 - 7.0 * ROOT) / 360.0, (296.0 - 169.0 * ROOT) / 1800.0, (-2.0 + 3.0 * ROOT) / 225.0],
    [(296.0 + 169.0 * ROOT) / 1800.0, (88.0 + 7.0 * ROOT) / 360.0, (-2.0 - 3.0 * ROOT) / 225.0],
    [(16.0 - ROOT) / 36.0, (16.0 + ROOT) / 36.0, 1.0 / 9.0],
]

VMEM = pl.BlockSpec(memory_space=pltpu.VMEM)
SMEM = pl.BlockSpec(memory_space=pltpu.SMEM)


def cols_id(x, z, core):
    return (x * NZ + z) * NCORE + core


def shift_x(value, steps):
    pairs = [
        (cols_id(x, z, c), cols_id((x + steps) % NX, z, c))
        for x in range(NX)
        for z in range(NZ)
        for c in range(NCORE)
    ]
    return lax.ppermute(value, "cols", pairs)


def swap_core(value):
    return lax.ppermute(value, "cols", [(i, i ^ 1) for i in range(NX * NZ * NCORE)])


def ring_lat(value, steps):
    return lax.ppermute(value, "lat", [(i, (i + steps) % N_LAT) for i in range(N_LAT)])


def exchange_z(value):
    groups = [[cols_id(x, z, c) for z in range(NZ)] for x in range(NX) for c in range(NCORE)]
    return lax.all_to_all(value, "cols", 0, 0, axis_index_groups=groups, tiled=True)


def emit_terms(blocks, tiles_ref, raw_ref, own_ref, north_ref, south_ref):
    for r in range(RB):
        padded = jnp.concatenate([blocks[r], jnp.zeros((16 - TR, BLK), F32)], axis=0)
        left = padded.astype(jnp.bfloat16)
        for t in range(NB):
            term = jnp.dot(left, tiles_ref[r, t], preferred_element_type=F32)[:TR]
            if t == 0:
                own_ref[r * TR : (r + 1) * TR, :] = term
            elif t <= NBAND:
                k = r * NBAND + t - 1
                raw_ref[k * TR : (k + 1) * TR, :] = term
            elif t == NBAND + 1:
                north_ref[r * TR : (r + 1) * TR, :] = term
            else:
                south_ref[r * TR : (r + 1) * TR, :] = term


def first_kernel(field_ref, tiles_ref, raw_ref, own_ref, north_ref, south_ref):
    blocks = [field_ref[:, r * BLK : (r + 1) * BLK] for r in range(RB)]
    emit_terms(blocks, tiles_ref, raw_ref, own_ref, north_ref, south_ref)


def merge_kernel(slot_ref, raw0, raw1, raw2, raw3, mine_ref, other_ref, acc):
    acc[...] = jnp.zeros_like(acc)
    for source, raw in enumerate((raw0, raw1, raw2, raw3)):
        for k in range(TERMS):
            slot = slot_ref[source, k]
            acc[slot] = acc[slot] + raw[k * TR : (k + 1) * TR, :]
    for slot in range(NZ * RB):
        mine_ref[slot * TR : (slot + 1) * TR, :] = acc[slot]
        other_ref[slot * TR : (slot + 1) * TR, :] = acc[NZ * RB + slot]


def arrived_blocks(edge_ref, slabs_ref, own_ref, below_ref, above_ref, wet_ref):
    total = own_ref[...]
    for z in range(NZ):
        total = total + slabs_ref[z]
    total = total + jnp.where(edge_ref[0] > 0, below_ref[...], 0.0)
    total = total + jnp.where(edge_ref[1] > 0, above_ref[...], 0.0)
    return [total[r * TR : (r + 1) * TR, :] * wet_ref[r : r + 1, :] for r in range(RB)]


def column_block(forcing, r, jac_ref, inv_ref, sweeps):
    lanes = slice(r * BLK, (r + 1) * BLK)

    def image_update(rows):
        total = None
        for q, row in rows:
            part = inv_ref[q, :, lanes].astype(F32) * row
            total = part if total is None else total + part
        return total

    rows = [(2 * TR + i, forcing[i : i + 1, :]) for i in range(TR)]
    update = jnp.where(0 < sweeps, image_update(rows), 0.0)
    z = [update[s * TR : (s + 1) * TR, :] for s in range(SECTIONS)]
    for sweep in range(1, NEWT):
        mixed = [None] * SECTIONS
        for i in range(TR):
            jac = jac_ref[i, :, lanes].astype(F32)
            for s in range(SECTIONS):
                part = jac * z[s][i : i + 1, :]
                mixed[s] = part if mixed[s] is None else mixed[s] + part
        rows = []
        for s in range(SECTIONS):
            mix = COEF[0][s] * mixed[0] + COEF[1][s] * mixed[1] + COEF[2][s] * mixed[2]
            residual = mix - z[s]
            if s == SECTIONS - 1:
                residual = residual + forcing
            rows += [(s * TR + i, residual[i : i + 1, :]) for i in range(TR)]
        update = jnp.where(sweep < sweeps, image_update(rows), 0.0)
        z = [z[s] + update[s * TR : (s + 1) * TR, :] for s in range(SECTIONS)]
    return z[0] + z[1] + z[2]


def react_kernel(
    edge_ref, slabs_ref, own_in, below_ref, above_ref, wet_ref, sweeps_ref, jac_ref, inv_ref,
    tiles_ref, raw_ref, own_ref, north_ref, south_ref,
):
    blocks = arrived_blocks(edge_ref, slabs_ref, own_in, below_ref, above_ref, wet_ref)
    blocks = [
        column_block(blocks[r], r, jac_ref, inv_ref, sweeps_ref[r : r + 1, :]) for r in range(RB)
    ]
    emit_terms(blocks, tiles_ref, raw_ref, own_ref, north_ref, south_ref)


def step_kernel(
    edge_ref, slabs_ref, own_in, below_ref, above_ref, wet_ref,
    tiles_ref, raw_ref, own_ref, north_ref, south_ref,
):
    blocks = arrived_blocks(edge_ref, slabs_ref, own_in, below_ref, above_ref, wet_ref)
    emit_terms(blocks, tiles_ref, raw_ref, own_ref, north_ref, south_ref)


def last_kernel(edge_ref, slabs_ref, own_in, below_ref, above_ref, wet_ref, out_ref):
    blocks = arrived_blocks(edge_ref, slabs_ref, own_in, below_ref, above_ref, wet_ref)
    for r in range(RB):
        out_ref[:, r * BLK : (r + 1) * BLK] = blocks[r]


def struct(*shape):
    return jax.ShapeDtypeStruct(shape, F32)


TERM_SHAPES = (
    struct(TERMS * TR, BLK),
    struct(SLAB, BLK),
    struct(SLAB, BLK),
    struct(SLAB, BLK),
)


def call(kernel, out_shape, operands, smem, name, scratch=(), flops=0):
    many = isinstance(out_shape, tuple)
    size = sum(a.size * a.dtype.itemsize for a in operands)
    return pl.pallas_call(
        kernel,
        out_shape=out_shape,
        in_specs=[SMEM] * smem + [VMEM] * (len(operands) - smem),
        out_specs=[VMEM] * len(out_shape) if many else VMEM,
        scratch_shapes=scratch,
        compiler_params=pltpu.CompilerParams(vmem_limit_bytes=32 * 1024 * 1024),
        cost_estimate=pl.CostEstimate(flops=flops, bytes_accessed=size, transcendentals=0),
        name=name,
    )(*operands)


def body(
    adjoint,
    impl_tiles,
    expl_tiles,
    impl_dest,
    impl_local,
    expl_dest,
    expl_local,
    column_depth,
    newton,
    jacobian,
    newton_inverse,
):
    cols = lax.axis_index("cols")
    lat = lax.axis_index("lat")
    my_x = cols // (NZ * NCORE)
    my_core = cols % NCORE
    edges = jnp.stack([lat > 0, lat < N_LAT - 1]).astype(jnp.int32)

    codes = jnp.stack([impl_dest * RB + impl_local, expl_dest * RB + expl_local])
    codes = codes.reshape(2, TERMS)
    gathered = jnp.stack([codes] + [shift_x(codes, k) for k in range(1, NX)], axis=1)
    owner, local = gathered // RB, gathered % RB
    place = (owner // NCORE) % NZ * RB + local
    place = place + jnp.where(owner % NCORE == my_core, 0, NZ * RB)
    slots = jnp.where(owner // (NZ * NCORE) == my_x, place, 2 * NZ * RB).astype(jnp.int32)

    level = jnp.arange(LEV, dtype=jnp.int32)
    wet = (level[None, :] < column_depth[:, None]).astype(F32).reshape(RB, BLK)
    sweeps = jnp.broadcast_to(newton[:, None], (newton.shape[0], LEV)).reshape(RB, BLK)

    def deliver(terms, slot):
        raw, own, north, south = terms
        raws = [raw] + [shift_x(raw, k) for k in range(1, NX)]
        mine, other = call(
            merge_kernel,
            (struct(NZ * SLAB, BLK), struct(NZ * SLAB, BLK)),
            [slot] + raws,
            1,
            "merge",
            [pltpu.VMEM((2 * NZ * RB + 1, TR, BLK), F32)],
        )
        dense = (mine + swap_core(other)).reshape(NZ, SLAB, BLK)
        slabs = exchange_z(dense)
        return [edges, slabs, own, ring_lat(north, 1), ring_lat(south, N_LAT - 1), wet]

    terms = call(first_kernel, TERM_SHAPES, [adjoint, impl_tiles], 0, "first")
    for step_index in range(STEPS):
        arrived = deliver(terms, slots[0])
        terms = call(
            react_kernel,
            TERM_SHAPES,
            arrived + [sweeps, jacobian, newton_inverse, expl_tiles],
            1,
            "react",
        )
        arrived = deliver(terms, slots[1])
        if step_index + 1 < STEPS:
            terms = call(step_kernel, TERM_SHAPES, arrived + [impl_tiles], 1, "step")
    return call(last_kernel, struct(TR, RB * BLK), arrived, 1, "last")


def solution(mesh):
    both = ("cols", "lat")
    return jax.shard_map(
        body,
        mesh=mesh,
        in_specs=(
            P(None, both),
            P(both, None, None, None),
            P(both, None, None, None),
            P(both, None),
            P(both, None),
            P(both, None),
            P(both, None),
            P(both),
            P(both),
            P(None, None, both),
            P(None, None, both),
        ),
        out_specs=P(None, both),
        check_vma=False,
    )
```

time: 654 us -> 122 us (0.19)
  waiting for transfers between devices: 525 us -> 58.8 us
  matrix products: 32.1 us -> 0 us
  local copies, waits for them, and re-layouts: 35.3 us -> 4.03 us
  starting transfers between devices: 24.1 us -> 44 us
  other arithmetic: 22.3 us -> 3.64 us
  between operations: 13.8 us -> 0.18 us
  Pallas kernels: 0 us -> 9.4 us
    reduce_scatter x4 -> x0, waiting for transfers between devices: 521 us -> none  [transport_transpose(): lax.psum_scatter(dense_terms, 'cols', scatter_dimension=0, tiled=True)]
    ppermute x8 -> x27, waiting for transfers between devices: 3.54 us -> 38.7 us  [the longest x15 21.3 us: shift_x(): return lax.ppermute(value, 'cols', pairs)]
    dot_general x18 -> x0, matrix products: 32.1 us -> none  [the longest x7 27 us: column_adjoint(): jnp.einsum('ijb,sib->sjb', jacobian, sections, precision=highest, preferr...]
    all_to_all x0 -> x4, waiting for transfers between devices: none -> 20.1 us  [exchange_z(): lax.all_to_all(value, 'cols', 0, 0, axis_index_groups=groups, tiled=True)]
    all_to_all x0 -> x4, starting transfers between devices: none -> 18.7 us  [exchange_z(): lax.all_to_all(value, 'cols', 0, 0, axis_index_groups=groups, tiled=True)]
    dot_general x7 -> x0, local copies, waits for them, and re-layouts: 11 us -> none  [column_adjoint(): jnp.einsum('ijb,sib->sjb', jacobian, sections, precision=highest, preferr...]
    dot_general x8 -> x0, other arithmetic: 10.2 us -> none  [column_adjoint(): jnp.einsum('qpb,qb->pb', inverse, residual, precision=highest, preferred_...]
    pallas_call x0 -> x9, Pallas kernels: none -> 9.4 us  [call(): pl.pallas_call(kernel, out_shape=out_shape, in_specs=[SMEM] * smem + [VME...]
  transfers between devices with their start and end apart: 12 -> 31, of which waited for: 7 -> 25; matrix products, arithmetic and copies ran while one was open for 2% -> 1% of each run, Pallas kernels for 0% -> 0%
where the time goes in v1:
time: 122 us; the launch traced here: 120 us
  waiting for transfers between devices  58.8 us (48%)
  starting transfers between devices  44 us (36%)
  Pallas kernels  9.4 us (8%)
  local copies, waits for them, and re-layouts  4.03 us (3%)
  other arithmetic  3.64 us (3%)
    ppermute x15, waiting for transfers between devices, shift_x(): return lax.ppermute(value, 'cols', pairs)  21.3 us
    all_to_all x4, waiting for transfers between devices, exchange_z(): lax.all_to_all(value, 'cols', 0, 0, axis_index_groups=groups, tiled=True)  20.1 us
    all_to_all x4, starting transfers between devices, exchange_z(): lax.all_to_all(value, 'cols', 0, 0, axis_index_groups=groups, tiled=True)  18.7 us
    ppermute x15, starting transfers between devices, shift_x(): return lax.ppermute(value, 'cols', pairs)  16.5 us
    ppermute x8, waiting for transfers between devices, ring_lat(): lax.ppermute(value, 'lat', [(i, (i + steps) % N_LAT) for i in range(N_LAT)])  13.3 us
    pallas_call x9, Pallas kernels, call(): pl.pallas_call(kernel, out_shape=out_shape, in_specs=[SMEM] * smem + [VME...  9.4 us
    ppermute x8, starting transfers between devices, ring_lat(): lax.ppermute(value, 'lat', [(i, (i + steps) % N_LAT) for i in range(N_LAT)])  8.41 us
    ppermute x4, waiting for transfers between devices, swap_core(): lax.ppermute(value, 'cols', [(i, i ^ 1) for i in range(NX * NZ * NCORE)])  4.15 us
  transfers between devices with their start and end apart: 31, of which 25 were waited for; matrix products, arithmetic and copies ran while one was open for 1% of the time, Pallas kernels for 0%

profile of v1, /device:TPU:24, one launch (start us, length us, event | category | flops | bytes accessed | tf_op | source)
XLA Modules:
  0.0 120.1 jit_solution(8696110329830531664)
XLA Ops:
  0.0 0.7 multiply_add_fusion.1
  0.8 0.6 copy-done.6
  1.5 2.8 %collective-permute-start.2 = (s32[2,16]{1,0:T(2,128)S(1)}, s32[2,16]{1,0:T(2,128)S(1)}, u32[]{:S(2)}, u32[]{:S(2)}) collective-permute-start(s32[2,16]{1,0:T(2,128)S(1)} %pad_add_fusion.1), channel_id=1, source_target_pairs={{0,192},{4,196},{8,200},{12,204},{16,208},{20,212},{24,216},{28,22... | collective-permute-start | bytes 392 | tf_op jit(solution)/shard_map/ppermute | solution.py:47
  4.4 0.8 collective-permute-start.1
  5.2 0.9 collective-permute-start
  6.1 1.2 copy-done.2
  7.2 0.8 copy-done.5
  8.3 2.4 %collective-permute-start.5 = (f32[160,128]{1,0:T(8,128)S(1)}, f32[160,128]{1,0:T(8,128)S(1)}, u32[]{:S(2)}, u32[]{:S(2)}) collective-permute-start(f32[160,128]{1,0:T(8,128)S(1)} %get-tuple-element.29.raw0), channel_id=1, source_target_pairs={{0,192},{4,196},{8,200},{12,204},{16,208},{20,212},{24,216},{28,22... | collective-permute-start | bytes 245768 | tf_op jit(solution)/shard_map/ppermute | solution.py:47
  10.7 1.5 %collective-permute-start.4 = (f32[160,128]{1,0:T(8,128)S(1)}, f32[160,128]{1,0:T(8,128)S(1)}, u32[]{:S(2)}, u32[]{:S(2)}) collective-permute-start(f32[160,128]{1,0:T(8,128)S(1)} %get-tuple-element.29.raw0), channel_id=1, source_target_pairs={{0,128},{4,132},{8,136},{12,140},{16,144},{20,148},{24,152},{28,15... | collective-permute-start | bytes 245768 | tf_op jit(solution)/shard_map/ppermute | solution.py:47
  12.6 1.1 collective-permute-done.5.raw3
  13.6 3.1 %collective-permute-done.4.raw2 = f32[160,128]{1,0:T(8,128)S(1)} collective-permute-done((f32[160,128]{1,0:T(8,128)S(1)}, f32[160,128]{1,0:T(8,128)S(1)}, u32[]{:S(2)}, u32[]{:S(2)}) %collective-permute-start.4) | collective-permute-done | bytes 81952 | tf_op jit(solution)/shard_map/ppermute | solution.py:47
  16.7 1.4 %collective-permute-done.3.raw1 = f32[160,128]{1,0:T(8,128)S(1)} collective-permute-done((f32[160,128]{1,0:T(8,128)S(1)}, f32[160,128]{1,0:T(8,128)S(1)}, u32[]{:S(2)}, u32[]{:S(2)}) %collective-permute-start.3) | collective-permute-done | bytes 81952 | tf_op jit(solution)/shard_map/ppermute | solution.py:47
  18.1 1.0 merge.4
  19.5 1.8 %collective-permute-start.8 = (f32[40,128]{1,0:T(8,128)S(1)}, f32[40,128]{1,0:T(8,128)S(1)}, u32[]{:S(2)}, u32[]{:S(2)}) collective-permute-start(f32[40,128]{1,0:T(8,128)S(1)} %get-tuple-element.34), channel_id=1, source_target_pairs={{0,3},{1,0},{2,1},{3,2},{4,7},{5,4},{6,5},{7,6},{8,11},{9,8},{10,9... | collective-permute-start | bytes 61448 | tf_op jit(solution)/shard_map/ppermute | solution.py:55
  21.6 0.7 add.54
  22.3 8.6 %all-to-all-start = ((f32[8,40,128]{2,1,0:T(8,128)}), f32[8,40,128]{2,1,0:T(8,128)S(1)}, u32[]{:S(2)}, u32[]{:S(2)}) async-start(f32[8,40,128]{2,1,0:T(8,128)} %bitcast.10), calls=%async_computation | async-start | bytes 327680 | tf_op jit(solution)/shard_map/all_to_all | solution.py:60
  31.0 0.6 copy-done.9
  31.8 8.9 %all-to-all-done.slabs_ref = f32[8,40,128]{2,1,0:T(8,128)S(1)} async-done(((f32[8,40,128]{2,1,0:T(8,128)}), f32[8,40,128]{2,1,0:T(8,128)S(1)}, u32[]{:S(2)}, u32[]{:S(2)}) %all-to-all-start) | async-done | bytes 163872 | tf_op jit(solution)/shard_map/all_to_all | solution.py:60
  40.7 1.6 %react.2 = (f32[160,128]{1,0:T(8,128)S(1)}, f32[40,128]{1,0:T(8,128)S(1)}, f32[40,128]{1,0:T(8,128)S(1)}, f32[40,128]{1,0:T(8,128)S(1)}) custom-call(s32[2]{0:T(128)S(1)} %add_convert_fusion.edge_ref, f32[8,40,128]{2,1,0:T(8,128)S(1)} %all-to-all-done.slabs_ref, f32[40,128]{1,0:T(8,128)S(1)} %get-tuple-element.32.own_in, ...), custom_call_target="tpu_custom_call" | custom-call | bytes 2170888 | tf_op jit(solution)/shard_map/react/pallas_call | solution.py:177
  42.5 1.5 %collective-permute-start.10 = (f32[160,128]{1,0:T(8,128)S(1)}, f32[160,128]{1,0:T(8,128)S(1)}, u32[]{:S(2)}, u32[]{:S(2)}) collective-permute-start(f32[160,128]{1,0:T(8,128)S(1)} %get-tuple-element.35.raw0), channel_id=1, source_target_pairs={{0,128},{4,132},{8,136},{12,140},{16,144},{20,148},{24,152},{28,15... | collective-permute-start | bytes 245768 | tf_op jit(solution)/shard_map/ppermute | solution.py:47
  44.0 0.8 collective-permute-start.9
  44.8 2.0 %collective-permute-done.11.raw3 = f32[160,128]{1,0:T(8,128)S(1)} collective-permute-done((f32[160,128]{1,0:T(8,128)S(1)}, f32[160,128]{1,0:T(8,128)S(1)}, u32[]{:S(2)}, u32[]{:S(2)}) %collective-permute-start.11) | collective-permute-done | bytes 81952 | tf_op jit(solution)/shard_map/ppermute | solution.py:47
  46.8 1.6 %collective-permute-done.10.raw2 = f32[160,128]{1,0:T(8,128)S(1)} collective-permute-done((f32[160,128]{1,0:T(8,128)S(1)}, f32[160,128]{1,0:T(8,128)S(1)}, u32[]{:S(2)}, u32[]{:S(2)}) %collective-permute-start.10) | collective-permute-done | bytes 81952 | tf_op jit(solution)/shard_map/ppermute | solution.py:47
  48.4 1.2 %collective-permute-done.9.raw1 = f32[160,128]{1,0:T(8,128)S(1)} collective-permute-done((f32[160,128]{1,0:T(8,128)S(1)}, f32[160,128]{1,0:T(8,128)S(1)}, u32[]{:S(2)}, u32[]{:S(2)}) %collective-permute-start.9) | collective-permute-done | bytes 81952 | tf_op jit(solution)/shard_map/ppermute | solution.py:47
  49.6 1.0 merge.5
  50.7 1.4 %collective-permute-done.12 = f32[320,128]{1,0:T(8,128)S(1)} collective-permute-done((f32[320,128]{1,0:T(8,128)S(1)}, f32[320,128]{1,0:T(8,128)S(1)}, u32[]{:S(2)}, u32[]{:S(2)}) %collective-permute-start.12) | collective-permute-done | bytes 163872 | tf_op jit(solution)/shard_map/ppermute | solution.py:51
  52.1 0.7 add.55
  52.7 3.4 %all-to-all-start.1 = ((f32[8,40,128]{2,1,0:T(8,128)}), f32[8,40,128]{2,1,0:T(8,128)S(1)}, u32[]{:S(2)}, u32[]{:S(2)}) async-start(f32[8,40,128]{2,1,0:T(8,128)} %bitcast.11), calls=%async_computation.1 | async-start | bytes 327680 | tf_op jit(solution)/shard_map/all_to_all | solution.py:60
  56.1 1.6 %collective-permute-start.13 = (f32[40,128]{1,0:T(8,128)S(1)}, f32[40,128]{1,0:T(8,128)S(1)}, u32[]{:S(2)}, u32[]{:S(2)}) collective-permute-start(f32[40,128]{1,0:T(8,128)S(1)} %get-tuple-element.39), channel_id=1, source_target_pairs={{0,1},{1,2},{2,3},{3,0},{4,5},{5,6},{6,7},{7,4},{8,9},{9,10},{10,1... | collective-permute-start | bytes 61448 | tf_op jit(solution)/shard_map/ppermute | solution.py:55
  58.2 1.8 %collective-permute-done.13.below_ref = f32[40,128]{1,0:T(8,128)S(1)} collective-permute-done((f32[40,128]{1,0:T(8,128)S(1)}, f32[40,128]{1,0:T(8,128)S(1)}, u32[]{:S(2)}, u32[]{:S(2)}) %collective-permute-start.13) | collective-permute-done | bytes 20512 | tf_op jit(solution)/shard_map/ppermute | solution.py:55
  60.0 2.7 %collective-permute-done.14.above_ref = f32[40,128]{1,0:T(8,128)S(1)} collective-permute-done((f32[40,128]{1,0:T(8,128)S(1)}, f32[40,128]{1,0:T(8,128)S(1)}, u32[]{:S(2)}, u32[]{:S(2)}) %collective-permute-start.14) | collective-permute-done | bytes 20512 | tf_op jit(solution)/shard_map/ppermute | solution.py:55
  62.7 3.7 %all-to-all-done.1.slabs_ref = f32[8,40,128]{2,1,0:T(8,128)S(1)} async-done(((f32[8,40,128]{2,1,0:T(8,128)}), f32[8,40,128]{2,1,0:T(8,128)S(1)}, u32[]{:S(2)}, u32[]{:S(2)}) %all-to-all-start.1) | async-done | bytes 163872 | tf_op jit(solution)/shard_map/all_to_all | solution.py:60
  66.4 0.9 step.1
  67.3 2.0 %collective-permute-start.17 = (f32[160,128]{1,0:T(8,128)S(1)}, f32[160,128]{1,0:T(8,128)S(1)}, u32[]{:S(2)}, u32[]{:S(2)}) collective-permute-start(f32[160,128]{1,0:T(8,128)S(1)} %get-tuple-element.41.raw0), channel_id=1, source_target_pairs={{0,192},{4,196},{8,200},{12,204},{16,208},{20,212},{24,216},{28,22... | collective-permute-start | bytes 245768 | tf_op jit(solution)/shard_map/ppermute | solution.py:47
  69.3 0.8 collective-permute-start.16
  70.2 1.9 %collective-permute-done.17.raw3 = f32[160,128]{1,0:T(8,128)S(1)} collective-permute-done((f32[160,128]{1,0:T(8,128)S(1)}, f32[160,128]{1,0:T(8,128)S(1)}, u32[]{:S(2)}, u32[]{:S(2)}) %collective-permute-start.17) | collective-permute-done | bytes 81952 | tf_op jit(solution)/shard_map/ppermute | solution.py:47
  72.1 3.1 %collective-permute-done.16.raw2 = f32[160,128]{1,0:T(8,128)S(1)} collective-permute-done((f32[160,128]{1,0:T(8,128)S(1)}, f32[160,128]{1,0:T(8,128)S(1)}, u32[]{:S(2)}, u32[]{:S(2)}) %collective-permute-start.16) | collective-permute-done | bytes 81952 | tf_op jit(solution)/shard_map/ppermute | solution.py:47
  75.2 0.8 collective-permute-done.15.raw1
  76.1 1.0 merge.6
  77.1 1.4 %collective-permute-done.18 = f32[320,128]{1,0:T(8,128)S(1)} collective-permute-done((f32[320,128]{1,0:T(8,128)S(1)}, f32[320,128]{1,0:T(8,128)S(1)}, u32[]{:S(2)}, u32[]{:S(2)}) %collective-permute-start.18) | collective-permute-done | bytes 163872 | tf_op jit(solution)/shard_map/ppermute | solution.py:51
  78.5 0.7 add.56
  79.2 3.4 %all-to-all-start.2 = ((f32[8,40,128]{2,1,0:T(8,128)}), f32[8,40,128]{2,1,0:T(8,128)S(1)}, u32[]{:S(2)}, u32[]{:S(2)}) async-start(f32[8,40,128]{2,1,0:T(8,128)} %bitcast.12), calls=%async_computation.2 | async-start | bytes 327680 | tf_op jit(solution)/shard_map/all_to_all | solution.py:60
  82.6 1.5 %collective-permute-start.19 = (f32[40,128]{1,0:T(8,128)S(1)}, f32[40,128]{1,0:T(8,128)S(1)}, u32[]{:S(2)}, u32[]{:S(2)}) collective-permute-start(f32[40,128]{1,0:T(8,128)S(1)} %get-tuple-element.45), channel_id=1, source_target_pairs={{0,1},{1,2},{2,3},{3,0},{4,5},{5,6},{6,7},{7,4},{8,9},{9,10},{10,1... | collective-permute-start | bytes 61448 | tf_op jit(solution)/shard_map/ppermute | solution.py:55
  84.1 0.6 collective-permute-start.20
  84.7 1.8 %collective-permute-done.19.below_ref = f32[40,128]{1,0:T(8,128)S(1)} collective-permute-done((f32[40,128]{1,0:T(8,128)S(1)}, f32[40,128]{1,0:T(8,128)S(1)}, u32[]{:S(2)}, u32[]{:S(2)}) %collective-permute-start.19) | collective-permute-done | bytes 20512 | tf_op jit(solution)/shard_map/ppermute | solution.py:55
  86.5 2.6 %collective-permute-done.20.above_ref = f32[40,128]{1,0:T(8,128)S(1)} collective-permute-done((f32[40,128]{1,0:T(8,128)S(1)}, f32[40,128]{1,0:T(8,128)S(1)}, u32[]{:S(2)}, u32[]{:S(2)}) %collective-permute-start.20) | collective-permute-done | bytes 20512 | tf_op jit(solution)/shard_map/ppermute | solution.py:55
  89.1 3.8 %all-to-all-done.2.slabs_ref = f32[8,40,128]{2,1,0:T(8,128)S(1)} async-done(((f32[8,40,128]{2,1,0:T(8,128)}), f32[8,40,128]{2,1,0:T(8,128)S(1)}, u32[]{:S(2)}, u32[]{:S(2)}) %all-to-all-start.2) | async-done | bytes 163872 | tf_op jit(solution)/shard_map/all_to_all | solution.py:60
  92.9 1.6 %react.3 = (f32[160,128]{1,0:T(8,128)S(1)}, f32[40,128]{1,0:T(8,128)S(1)}, f32[40,128]{1,0:T(8,128)S(1)}, f32[40,128]{1,0:T(8,128)S(1)}) custom-call(s32[2]{0:T(128)S(1)} %add_convert_fusion.edge_ref, f32[8,40,128]{2,1,0:T(8,128)S(1)} %all-to-all-done.2.slabs_ref, f32[40,128]{1,0:T(8,128)S(1)} %get-tuple-element.44.own_in, ...), custom_call_target="tpu_custom_call" | custom-call | bytes 2170888 | tf_op jit(solution)/shard_map/react/pallas_call | solution.py:177
  94.5 0.6 collective-permute-start.23
  95.1 0.9 collective-permute-start.22
  96.0 1.1 collective-permute-start.21
  97.1 1.9 %collective-permute-done.23.raw3 = f32[160,128]{1,0:T(8,128)S(1)} collective-permute-done((f32[160,128]{1,0:T(8,128)S(1)}, f32[160,128]{1,0:T(8,128)S(1)}, u32[]{:S(2)}, u32[]{:S(2)}) %collective-permute-start.23) | collective-permute-done | bytes 81952 | tf_op jit(solution)/shard_map/ppermute | solution.py:47
  99.0 2.5 %collective-permute-done.22.raw2 = f32[160,128]{1,0:T(8,128)S(1)} collective-permute-done((f32[160,128]{1,0:T(8,128)S(1)}, f32[160,128]{1,0:T(8,128)S(1)}, u32[]{:S(2)}, u32[]{:S(2)}) %collective-permute-start.22) | collective-permute-done | bytes 81952 | tf_op jit(solution)/shard_map/ppermute | solution.py:47
  101.5 0.7 collective-permute-done.21.raw1
  102.2 1.0 merge.7
  103.2 1.4 %collective-permute-done.24 = f32[320,128]{1,0:T(8,128)S(1)} collective-permute-done((f32[320,128]{1,0:T(8,128)S(1)}, f32[320,128]{1,0:T(8,128)S(1)}, u32[]{:S(2)}, u32[]{:S(2)}) %collective-permute-start.24) | collective-permute-done | bytes 163872 | tf_op jit(solution)/shard_map/ppermute | solution.py:51
  104.6 0.7 add.57
  105.3 3.4 %all-to-all-start.3 = ((f32[8,40,128]{2,1,0:T(8,128)}), f32[8,40,128]{2,1,0:T(8,128)S(1)}, u32[]{:S(2)}, u32[]{:S(2)}) async-start(f32[8,40,128]{2,1,0:T(8,128)} %bitcast.13), calls=%async_computation.3 | async-start | bytes 327680 | tf_op jit(solution)/shard_map/all_to_all | solution.py:60
  108.7 1.5 %collective-permute-start.25 = (f32[40,128]{1,0:T(8,128)S(1)}, f32[40,128]{1,0:T(8,128)S(1)}, u32[]{:S(2)}, u32[]{:S(2)}) collective-permute-start(f32[40,128]{1,0:T(8,128)S(1)} %get-tuple-element.51), channel_id=1, source_target_pairs={{0,1},{1,2},{2,3},{3,0},{4,5},{5,6},{6,7},{7,4},{8,9},{9,10},{10,1... | collective-permute-start | bytes 61448 | tf_op jit(solution)/shard_map/ppermute | solution.py:55
  110.2 0.6 collective-permute-start.26
  110.8 1.8 %collective-permute-done.25.below_ref = f32[40,128]{1,0:T(8,128)S(1)} collective-permute-done((f32[40,128]{1,0:T(8,128)S(1)}, f32[40,128]{1,0:T(8,128)S(1)}, u32[]{:S(2)}, u32[]{:S(2)}) %collective-permute-start.25) | collective-permute-done | bytes 20512 | tf_op jit(solution)/shard_map/ppermute | solution.py:55
  112.6 2.7 %collective-permute-done.26.above_ref = f32[40,128]{1,0:T(8,128)S(1)} collective-permute-done((f32[40,128]{1,0:T(8,128)S(1)}, f32[40,128]{1,0:T(8,128)S(1)}, u32[]{:S(2)}, u32[]{:S(2)}) %collective-permute-start.26) | collective-permute-done | bytes 20512 | tf_op jit(solution)/shard_map/ppermute | solution.py:55
  115.2 3.7 %all-to-all-done.3.slabs_ref = f32[8,40,128]{2,1,0:T(8,128)S(1)} async-done(((f32[8,40,128]{2,1,0:T(8,128)}), f32[8,40,128]{2,1,0:T(8,128)S(1)}, u32[]{:S(2)}, u32[]{:S(2)}) %all-to-all-start.3) | async-done | bytes 163872 | tf_op jit(solution)/shard_map/all_to_all | solution.py:60
  119.0 1.2 last.1
  (50 shorter events, 3.0 us)
Async XLA Ops:
  0.0 0.8 copy-start.7
  0.0 21.4 %copy-start.8 = (s32[8]{0:T(128)S(1)}, s32[8]{0:T(128)}, u32[]{:S(2)}) copy-start(s32[8]{0:T(128)} %param.18) | copy-start | bytes 100
  0.7 0.7 copy-start.6
  1.5 39.2 %copy-start = (bf16[30,30,512]{2,1,0:T(8,128)(2,1)S(1)}, bf16[30,30,512]{2,1,0:T(8,128)(2,1)}, u32[]{:S(2)}) copy-start(bf16[30,30,512]{2,1,0:T(8,128)(2,1)} %inv_ref.3) | copy-start | bytes 2764804
  1.5 39.2 %copy-start.1 = (bf16[4,7,128,128]{3,2,1,0:T(8,128)(2,1)S(1)}, bf16[4,7,128,128]{3,2,1,0:T(8,128)(2,1)}, u32[]{:S(2)}) copy-start(bf16[4,7,128,128]{3,2,1,0:T(8,128)(2,1)} %tiles_ref.7) | copy-start | bytes 2752516
  1.5 10.9 %collective-permute-start.2 = (s32[2,16]{1,0:T(2,128)S(1)}, s32[2,16]{1,0:T(2,128)S(1)}, u32[]{:S(2)}, u32[]{:S(2)}) collective-permute-start(s32[2,16]{1,0:T(2,128)S(1)} %pad_add_fusion.1), channel_id=1, source_target_pairs={{0,192},{4,196},{8,200},{12,204},{16,208},{20,212},{24,216},{28,22... | collective-permute-start | bytes 392 | tf_op jit(solution)/shard_map/ppermute | solution.py:47
  4.4 8.1 %collective-permute-start.1 = (s32[2,16]{1,0:T(2,128)S(1)}, s32[2,16]{1,0:T(2,128)S(1)}, u32[]{:S(2)}, u32[]{:S(2)}) collective-permute-start(s32[2,16]{1,0:T(2,128)S(1)} %pad_add_fusion.1), channel_id=1, source_target_pairs={{0,128},{4,132},{8,136},{12,140},{16,144},{20,148},{24,152},{28,15... | collective-permute-start | bytes 392 | tf_op jit(solution)/shard_map/ppermute | solution.py:47
  5.2 7.3 %collective-permute-start = (s32[2,16]{1,0:T(2,128)S(1)}, s32[2,16]{1,0:T(2,128)S(1)}, u32[]{:S(2)}, u32[]{:S(2)}) collective-permute-start(s32[2,16]{1,0:T(2,128)S(1)} %pad_add_fusion.1), channel_id=1, source_target_pairs={{0,64},{4,68},{8,72},{12,76},{16,80},{20,84},{24,88},{28,92},{32,9... | collective-permute-start | bytes 392 | tf_op jit(solution)/shard_map/ppermute | solution.py:47
  6.1 1.2 copy-start.2
  7.2 0.8 copy-start.5
  8.3 5.3 %collective-permute-start.5 = (f32[160,128]{1,0:T(8,128)S(1)}, f32[160,128]{1,0:T(8,128)S(1)}, u32[]{:S(2)}, u32[]{:S(2)}) collective-permute-start(f32[160,128]{1,0:T(8,128)S(1)} %get-tuple-element.29.raw0), channel_id=1, source_target_pairs={{0,192},{4,196},{8,200},{12,204},{16,208},{20,212},{24,216},{28,22... | collective-permute-start | bytes 245768 | tf_op jit(solution)/shard_map/ppermute | solution.py:47
  10.7 5.9 %collective-permute-start.4 = (f32[160,128]{1,0:T(8,128)S(1)}, f32[160,128]{1,0:T(8,128)S(1)}, u32[]{:S(2)}, u32[]{:S(2)}) collective-permute-start(f32[160,128]{1,0:T(8,128)S(1)} %get-tuple-element.29.raw0), channel_id=1, source_target_pairs={{0,128},{4,132},{8,136},{12,140},{16,144},{20,148},{24,152},{28,15... | collective-permute-start | bytes 245768 | tf_op jit(solution)/shard_map/ppermute | solution.py:47
  12.4 5.7 %collective-permute-start.3 = (f32[160,128]{1,0:T(8,128)S(1)}, f32[160,128]{1,0:T(8,128)S(1)}, u32[]{:S(2)}, u32[]{:S(2)}) collective-permute-start(f32[160,128]{1,0:T(8,128)S(1)} %get-tuple-element.29.raw0), channel_id=1, source_target_pairs={{0,64},{4,68},{8,72},{12,76},{16,80},{20,84},{24,88},{28,92},{32,9... | collective-permute-start | bytes 245768 | tf_op jit(solution)/shard_map/ppermute | solution.py:47
  19.1 2.5 %collective-permute-start.6 = (f32[320,128]{1,0:T(8,128)S(1)}, f32[320,128]{1,0:T(8,128)S(1)}, u32[]{:S(2)}, u32[]{:S(2)}) collective-permute-start(f32[320,128]{1,0:T(8,128)S(1)} %get-tuple-element.31), channel_id=1, source_target_pairs={{0,4},{4,0},{8,12},{12,8},{16,20},{20,16},{24,28},{28,24},{32,36},... | collective-permute-start | bytes 491528 | tf_op jit(solution)/shard_map/ppermute | solution.py:51
  19.2 12.6 %collective-permute-start.7 = (f32[40,128]{1,0:T(8,128)S(1)}, f32[40,128]{1,0:T(8,128)S(1)}, u32[]{:S(2)}, u32[]{:S(2)}) collective-permute-start(f32[40,128]{1,0:T(8,128)S(1)} %get-tuple-element.33), channel_id=1, source_target_pairs={{0,1},{1,2},{2,3},{3,0},{4,5},{5,6},{6,7},{7,4},{8,9},{9,10},{10,1... | collective-permute-start | bytes 61448 | tf_op jit(solution)/shard_map/ppermute | solution.py:55
  19.5 12.3 %collective-permute-start.8 = (f32[40,128]{1,0:T(8,128)S(1)}, f32[40,128]{1,0:T(8,128)S(1)}, u32[]{:S(2)}, u32[]{:S(2)}) collective-permute-start(f32[40,128]{1,0:T(8,128)S(1)} %get-tuple-element.34), channel_id=1, source_target_pairs={{0,3},{1,0},{2,1},{3,2},{4,7},{5,4},{6,5},{7,6},{8,11},{9,8},{10,9... | collective-permute-start | bytes 61448 | tf_op jit(solution)/shard_map/ppermute | solution.py:55
  22.3 18.4 %copy-start.4 = (bf16[10,10,512]{2,1,0:T(8,128)(2,1)S(1)}, bf16[10,10,512]{2,1,0:T(8,128)(2,1)}, u32[]{:S(2)}) copy-start(bf16[10,10,512]{2,1,0:T(8,128)(2,1)} %jac_ref.3) | copy-start | bytes 307204
  22.3 18.4 %all-to-all-start = ((f32[8,40,128]{2,1,0:T(8,128)}), f32[8,40,128]{2,1,0:T(8,128)S(1)}, u32[]{:S(2)}, u32[]{:S(2)}) async-start(f32[8,40,128]{2,1,0:T(8,128)} %bitcast.10), calls=%async_computation | async-start | bytes 327680 | tf_op jit(solution)/shard_map/all_to_all | solution.py:60
  30.9 0.7 copy-start.9
  42.3 24.1 %copy-start.3 = (bf16[4,7,128,128]{3,2,1,0:T(8,128)(2,1)S(1)}, bf16[4,7,128,128]{3,2,1,0:T(8,128)(2,1)}, u32[]{:S(2)}) copy-start(bf16[4,7,128,128]{3,2,1,0:T(8,128)(2,1)} %tiles_ref.6) | copy-start | bytes 2752516
  42.3 4.5 %collective-permute-start.11 = (f32[160,128]{1,0:T(8,128)S(1)}, f32[160,128]{1,0:T(8,128)S(1)}, u32[]{:S(2)}, u32[]{:S(2)}) collective-permute-start(f32[160,128]{1,0:T(8,128)S(1)} %get-tuple-element.35.raw0), channel_id=1, source_target_pairs={{0,192},{4,196},{8,200},{12,204},{16,208},{20,212},{24,216},{28,22... | collective-permute-start | bytes 245768 | tf_op jit(solution)/shard_map/ppermute | solution.py:47
  42.5 6.0 %collective-permute-start.10 = (f32[160,128]{1,0:T(8,128)S(1)}, f32[160,128]{1,0:T(8,128)S(1)}, u32[]{:S(2)}, u32[]{:S(2)}) collective-permute-start(f32[160,128]{1,0:T(8,128)S(1)} %get-tuple-element.35.raw0), channel_id=1, source_target_pairs={{0,128},{4,132},{8,136},{12,140},{16,144},{20,148},{24,152},{28,15... | collective-permute-start | bytes 245768 | tf_op jit(solution)/shard_map/ppermute | solution.py:47
  44.0 5.7 %collective-permute-start.9 = (f32[160,128]{1,0:T(8,128)S(1)}, f32[160,128]{1,0:T(8,128)S(1)}, u32[]{:S(2)}, u32[]{:S(2)}) collective-permute-start(f32[160,128]{1,0:T(8,128)S(1)} %get-tuple-element.35.raw0), channel_id=1, source_target_pairs={{0,64},{4,68},{8,72},{12,76},{16,80},{20,84},{24,88},{28,92},{32,9... | collective-permute-start | bytes 245768 | tf_op jit(solution)/shard_map/ppermute | solution.py:47
  50.6 1.5 %collective-permute-start.12 = (f32[320,128]{1,0:T(8,128)S(1)}, f32[320,128]{1,0:T(8,128)S(1)}, u32[]{:S(2)}, u32[]{:S(2)}) collective-permute-start(f32[320,128]{1,0:T(8,128)S(1)} %get-tuple-element.37), channel_id=1, source_target_pairs={{0,4},{4,0},{8,12},{12,8},{16,20},{20,16},{24,28},{28,24},{32,36},... | collective-permute-start | bytes 491528 | tf_op jit(solution)/shard_map/ppermute | solution.py:51
  52.7 13.7 %all-to-all-start.1 = ((f32[8,40,128]{2,1,0:T(8,128)}), f32[8,40,128]{2,1,0:T(8,128)S(1)}, u32[]{:S(2)}, u32[]{:S(2)}) async-start(f32[8,40,128]{2,1,0:T(8,128)} %bitcast.11), calls=%async_computation.1 | async-start | bytes 327680 | tf_op jit(solution)/shard_map/all_to_all | solution.py:60
  56.1 3.9 %collective-permute-start.13 = (f32[40,128]{1,0:T(8,128)S(1)}, f32[40,128]{1,0:T(8,128)S(1)}, u32[]{:S(2)}, u32[]{:S(2)}) collective-permute-start(f32[40,128]{1,0:T(8,128)S(1)} %get-tuple-element.39), channel_id=1, source_target_pairs={{0,1},{1,2},{2,3},{3,0},{4,5},{5,6},{6,7},{7,4},{8,9},{9,10},{10,1... | collective-permute-start | bytes 61448 | tf_op jit(solution)/shard_map/ppermute | solution.py:55
  57.7 5.0 %collective-permute-start.14 = (f32[40,128]{1,0:T(8,128)S(1)}, f32[40,128]{1,0:T(8,128)S(1)}, u32[]{:S(2)}, u32[]{:S(2)}) collective-permute-start(f32[40,128]{1,0:T(8,128)S(1)} %get-tuple-element.40), channel_id=1, source_target_pairs={{0,3},{1,0},{2,1},{3,2},{4,7},{5,4},{6,5},{7,6},{8,11},{9,8},{10,9... | collective-permute-start | bytes 61448 | tf_op jit(solution)/shard_map/ppermute | solution.py:55
  67.3 4.9 %collective-permute-start.17 = (f32[160,128]{1,0:T(8,128)S(1)}, f32[160,128]{1,0:T(8,128)S(1)}, u32[]{:S(2)}, u32[]{:S(2)}) collective-permute-start(f32[160,128]{1,0:T(8,128)S(1)} %get-tuple-element.41.raw0), channel_id=1, source_target_pairs={{0,192},{4,196},{8,200},{12,204},{16,208},{20,212},{24,216},{28,22... | collective-permute-start | bytes 245768 | tf_op jit(solution)/shard_map/ppermute | solution.py:47
  69.3 6.0 %collective-permute-start.16 = (f32[160,128]{1,0:T(8,128)S(1)}, f32[160,128]{1,0:T(8,128)S(1)}, u32[]{:S(2)}, u32[]{:S(2)}) collective-permute-start(f32[160,128]{1,0:T(8,128)S(1)} %get-tuple-element.41.raw0), channel_id=1, source_target_pairs={{0,128},{4,132},{8,136},{12,140},{16,144},{20,148},{24,152},{28,15... | collective-permute-start | bytes 245768 | tf_op jit(solution)/shard_map/ppermute | solution.py:47
  70.1 6.0 %collective-permute-start.15 = (f32[160,128]{1,0:T(8,128)S(1)}, f32[160,128]{1,0:T(8,128)S(1)}, u32[]{:S(2)}, u32[]{:S(2)}) collective-permute-start(f32[160,128]{1,0:T(8,128)S(1)} %get-tuple-element.41.raw0), channel_id=1, source_target_pairs={{0,64},{4,68},{8,72},{12,76},{16,80},{20,84},{24,88},{28,92},{32,9... | collective-permute-start | bytes 245768 | tf_op jit(solution)/shard_map/ppermute | solution.py:47
  77.0 1.5 %collective-permute-start.18 = (f32[320,128]{1,0:T(8,128)S(1)}, f32[320,128]{1,0:T(8,128)S(1)}, u32[]{:S(2)}, u32[]{:S(2)}) collective-permute-start(f32[320,128]{1,0:T(8,128)S(1)} %get-tuple-element.43), channel_id=1, source_target_pairs={{0,4},{4,0},{8,12},{12,8},{16,20},{20,16},{24,28},{28,24},{32,36},... | collective-permute-start | bytes 491528 | tf_op jit(solution)/shard_map/ppermute | solution.py:51
  79.2 13.7 %all-to-all-start.2 = ((f32[8,40,128]{2,1,0:T(8,128)}), f32[8,40,128]{2,1,0:T(8,128)S(1)}, u32[]{:S(2)}, u32[]{:S(2)}) async-start(f32[8,40,128]{2,1,0:T(8,128)} %bitcast.12), calls=%async_computation.2 | async-start | bytes 327680 | tf_op jit(solution)/shard_map/all_to_all | solution.py:60
  82.6 3.9 %collective-permute-start.19 = (f32[40,128]{1,0:T(8,128)S(1)}, f32[40,128]{1,0:T(8,128)S(1)}, u32[]{:S(2)}, u32[]{:S(2)}) collective-permute-start(f32[40,128]{1,0:T(8,128)S(1)} %get-tuple-element.45), channel_id=1, source_target_pairs={{0,1},{1,2},{2,3},{3,0},{4,5},{5,6},{6,7},{7,4},{8,9},{9,10},{10,1... | collective-permute-start | bytes 61448 | tf_op jit(solution)/shard_map/ppermute | solution.py:55
  84.1 5.0 %collective-permute-start.20 = (f32[40,128]{1,0:T(8,128)S(1)}, f32[40,128]{1,0:T(8,128)S(1)}, u32[]{:S(2)}, u32[]{:S(2)}) collective-permute-start(f32[40,128]{1,0:T(8,128)S(1)} %get-tuple-element.46), channel_id=1, source_target_pairs={{0,3},{1,0},{2,1},{3,2},{4,7},{5,4},{6,5},{7,6},{8,11},{9,8},{10,9... | collective-permute-start | bytes 61448 | tf_op jit(solution)/shard_map/ppermute | solution.py:55
  94.5 4.5 %collective-permute-start.23 = (f32[160,128]{1,0:T(8,128)S(1)}, f32[160,128]{1,0:T(8,128)S(1)}, u32[]{:S(2)}, u32[]{:S(2)}) collective-permute-start(f32[160,128]{1,0:T(8,128)S(1)} %get-tuple-element.47.raw0), channel_id=1, source_target_pairs={{0,192},{4,196},{8,200},{12,204},{16,208},{20,212},{24,216},{28,22... | collective-permute-start | bytes 245768 | tf_op jit(solution)/shard_map/ppermute | solution.py:47
  95.1 6.4 %collective-permute-start.22 = (f32[160,128]{1,0:T(8,128)S(1)}, f32[160,128]{1,0:T(8,128)S(1)}, u32[]{:S(2)}, u32[]{:S(2)}) collective-permute-start(f32[160,128]{1,0:T(8,128)S(1)} %get-tuple-element.47.raw0), channel_id=1, source_target_pairs={{0,128},{4,132},{8,136},{12,140},{16,144},{20,148},{24,152},{28,15... | collective-permute-start | bytes 245768 | tf_op jit(solution)/shard_map/ppermute | solution.py:47
  96.0 6.2 %collective-permute-start.21 = (f32[160,128]{1,0:T(8,128)S(1)}, f32[160,128]{1,0:T(8,128)S(1)}, u32[]{:S(2)}, u32[]{:S(2)}) collective-permute-start(f32[160,128]{1,0:T(8,128)S(1)} %get-tuple-element.47.raw0), channel_id=1, source_target_pairs={{0,64},{4,68},{8,72},{12,76},{16,80},{20,84},{24,88},{28,92},{32,9... | collective-permute-start | bytes 245768 | tf_op jit(solution)/shard_map/ppermute | solution.py:47
  103.1 1.5 %collective-permute-start.24 = (f32[320,128]{1,0:T(8,128)S(1)}, f32[320,128]{1,0:T(8,128)S(1)}, u32[]{:S(2)}, u32[]{:S(2)}) collective-permute-start(f32[320,128]{1,0:T(8,128)S(1)} %get-tuple-element.49), channel_id=1, source_target_pairs={{0,4},{4,0},{8,12},{12,8},{16,20},{20,16},{24,28},{28,24},{32,36},... | collective-permute-start | bytes 491528 | tf_op jit(solution)/shard_map/ppermute | solution.py:51
  105.3 13.7 %all-to-all-start.3 = ((f32[8,40,128]{2,1,0:T(8,128)}), f32[8,40,128]{2,1,0:T(8,128)S(1)}, u32[]{:S(2)}, u32[]{:S(2)}) async-start(f32[8,40,128]{2,1,0:T(8,128)} %bitcast.13), calls=%async_computation.3 | async-start | bytes 327680 | tf_op jit(solution)/shard_map/all_to_all | solution.py:60
  108.7 3.9 %collective-permute-start.25 = (f32[40,128]{1,0:T(8,128)S(1)}, f32[40,128]{1,0:T(8,128)S(1)}, u32[]{:S(2)}, u32[]{:S(2)}) collective-permute-start(f32[40,128]{1,0:T(8,128)S(1)} %get-tuple-element.51), channel_id=1, source_target_pairs={{0,1},{1,2},{2,3},{3,0},{4,5},{5,6},{6,7},{7,4},{8,9},{9,10},{10,1... | collective-permute-start | bytes 61448 | tf_op jit(solution)/shard_map/ppermute | solution.py:55
  110.2 5.0 %collective-permute-start.26 = (f32[40,128]{1,0:T(8,128)S(1)}, f32[40,128]{1,0:T(8,128)S(1)}, u32[]{:S(2)}, u32[]{:S(2)}) collective-permute-start(f32[40,128]{1,0:T(8,128)S(1)} %get-tuple-element.52), channel_id=1, source_target_pairs={{0,3},{1,0},{2,1},{3,2},{4,7},{5,4},{6,5},{7,6},{8,11},{9,8},{10,9... | collective-permute-start | bytes 61448 | tf_op jit(solution)/shard_map/ppermute | solution.py:55

commit v2 on v1

v2 whole, which is shorter than its diff:
```python
import math

import jax
import jax.numpy as jnp
from jax import lax
from jax.experimental import pallas as pl
from jax.experimental.pallas import tpu as pltpu
from jax.sharding import PartitionSpec as P

NEWT = 4
STEPS = 2
TR = 10
SECTIONS = 3
BLK = 128
NBAND = 4
NB = 7
LEV = 64
RB = 4
NX, NZ, NCORE = 4, 8, 2
N_LAT = 4
TERMS = RB * NBAND
SLAB = RB * TR
F32 = jnp.float32

ROOT = math.sqrt(6.0)
COEF = [
    [(88.0 - 7.0 * ROOT) / 360.0, (296.0 - 169.0 * ROOT) / 1800.0, (-2.0 + 3.0 * ROOT) / 225.0],
    [(296.0 + 169.0 * ROOT) / 1800.0, (88.0 + 7.0 * ROOT) / 360.0, (-2.0 - 3.0 * ROOT) / 225.0],
    [(16.0 - ROOT) / 36.0, (16.0 + ROOT) / 36.0, 1.0 / 9.0],
]

VMEM = pl.BlockSpec(memory_space=pltpu.VMEM)
SMEM = pl.BlockSpec(memory_space=pltpu.SMEM)
FAR = pl.BlockSpec(memory_space=pltpu.HBM)


def cols_id(x, z, core):
    return (x * NZ + z) * NCORE + core


def shift_x(value, steps):
    pairs = [
        (cols_id(x, z, c), cols_id((x + steps) % NX, z, c))
        for x in range(NX)
        for z in range(NZ)
        for c in range(NCORE)
    ]
    return lax.ppermute(value, "cols", pairs)


def swap_core(value):
    return lax.ppermute(value, "cols", [(i, i ^ 1) for i in range(NX * NZ * NCORE)])


def ring_lat(value, steps):
    return lax.ppermute(value, "lat", [(i, (i + steps) % N_LAT) for i in range(N_LAT)])


def exchange_z(value):
    groups = [[cols_id(x, z, c) for z in range(NZ)] for x in range(NX) for c in range(NCORE)]
    return lax.all_to_all(value, "cols", 0, 0, axis_index_groups=groups, tiled=True)


def emit_terms(blocks, tiles_ref, raw_ref, own_ref, north_ref, south_ref, ready=None):
    for r in range(RB):
        if ready is not None:
            ready[r].wait()
        padded = jnp.concatenate([blocks[r], jnp.zeros((16 - TR, BLK), F32)], axis=0)
        left = padded.astype(jnp.bfloat16)
        for t in range(NB):
            term = jnp.dot(left, tiles_ref[r, t], preferred_element_type=F32)[:TR]
            if t == 0:
                own_ref[r * TR : (r + 1) * TR, :] = term
            elif t <= NBAND:
                k = r * NBAND + t - 1
                raw_ref[k * TR : (k + 1) * TR, :] = term
            elif t == NBAND + 1:
                north_ref[r * TR : (r + 1) * TR, :] = term
            else:
                south_ref[r * TR : (r + 1) * TR, :] = term


def first_kernel(
    field_far, impl_dest_far, impl_local_far, expl_dest_far, expl_local_far, tiles_far,
    raw_ref, own_ref, north_ref, south_ref,
    field_ref, impl_dest, impl_local, expl_dest, expl_local, tiles_ref, arrivals, tile_arrivals,
):
    copies = [
        pltpu.make_async_copy(far, near, arrivals.at[i])
        for i, (far, near) in enumerate(
            (
                (field_far, field_ref),
                (impl_dest_far, impl_dest),
                (impl_local_far, impl_local),
                (expl_dest_far, expl_dest),
                (expl_local_far, expl_local),
            )
        )
    ]
    tile_copies = [
        pltpu.make_async_copy(tiles_far.at[r], tiles_ref.at[r], tile_arrivals.at[r])
        for r in range(RB)
    ]
    for copy in copies + tile_copies:
        copy.start()
    raw_ref[TERMS * TR :, :] = jnp.zeros((2 * RB, BLK), F32)
    for copy in copies:
        copy.wait()
    impl_codes = impl_dest[...] * RB + impl_local[...]
    expl_codes = expl_dest[...] * RB + expl_local[...]
    raw_ref[TERMS * TR : TERMS * TR + RB, :NBAND] = impl_codes.astype(F32)
    raw_ref[TERMS * TR + RB :, :NBAND] = expl_codes.astype(F32)
    blocks = [field_ref[:, r * BLK : (r + 1) * BLK] for r in range(RB)]
    emit_terms(blocks, tiles_ref, raw_ref, own_ref, north_ref, south_ref, tile_copies)


def slots_kernel(raw0, raw1, raw2, raw3, impl_ref, expl_ref):
    cols = lax.axis_index("cols")
    my_core = cols & (NCORE - 1)
    my_x = cols // (NZ * NCORE)
    for source, raw in enumerate((raw0, raw1, raw2, raw3)):
        codes = raw[TERMS * TR :, :].astype(jnp.int32)
        owner, local = codes // RB, codes & (RB - 1)
        place = ((owner // NCORE) & (NZ - 1)) * RB + local
        place = place + jnp.where((owner & (NCORE - 1)) == my_core, 0, NZ * RB)
        slot = jnp.where(owner // (NZ * NCORE) == my_x, place, 2 * NZ * RB)
        impl_ref[source * RB : (source + 1) * RB, :] = slot[:RB, :NBAND]
        expl_ref[source * RB : (source + 1) * RB, :] = slot[RB:, :NBAND]


def masks_kernel(depth_ref, newton_ref, mask_ref, sweeps_ref):
    lat = lax.axis_index("lat")
    lane = lax.broadcasted_iota(jnp.int32, (1, BLK), 1)
    first = lane < LEV
    level = jnp.where(first, lane, lane - LEV)
    for r in range(RB):
        depth = jnp.where(first, depth_ref[2 * r], depth_ref[2 * r + 1])
        mask_ref[r : r + 1, :] = jnp.where(level < depth, 1.0, 0.0)
        sweeps_ref[r : r + 1, :] = jnp.where(first, newton_ref[2 * r], newton_ref[2 * r + 1])
    mask_ref[RB : RB + 1, :] = jnp.where(lane * 0 + lat > 0, 1.0, 0.0)
    mask_ref[RB + 1 : RB + 2, :] = jnp.where(lane * 0 + lat < N_LAT - 1, 1.0, 0.0)


def merge_kernel(slot_ref, raw0, raw1, raw2, raw3, mine_ref, other_ref, acc0, acc1):
    acc0[...] = jnp.zeros_like(acc0)
    acc1[...] = jnp.zeros_like(acc1)
    for pair in (((0, raw0, acc0), (1, raw1, acc1)), ((2, raw2, acc0), (3, raw3, acc1))):
        for k in range(TERMS):
            for source, raw, acc in pair:
                slot = slot_ref[source * RB + k // NBAND, k % NBAND]
                acc[slot] = acc[slot] + raw[k * TR : (k + 1) * TR, :]
    for slot in range(NZ * RB):
        mine_ref[slot * TR : (slot + 1) * TR, :] = acc0[slot] + acc1[slot]
        far = NZ * RB + slot
        other_ref[slot * TR : (slot + 1) * TR, :] = acc0[far] + acc1[far]


def arrived_blocks(mask_ref, slabs_ref, own_ref, below_ref, above_ref):
    total = own_ref[...] + below_ref[...] * mask_ref[RB : RB + 1, :]
    total = total + above_ref[...] * mask_ref[RB + 1 : RB + 2, :]
    for z in range(NZ):
        total = total + slabs_ref[z]
    return [total[r * TR : (r + 1) * TR, :] * mask_ref[r : r + 1, :] for r in range(RB)]


def column_block(forcing, r, jac_ref, inv_ref, sweeps):
    lanes = slice(r * BLK, (r + 1) * BLK)

    def image_update(rows):
        total = None
        for q, row in rows:
            part = inv_ref[q, :, lanes].astype(F32) * row
            total = part if total is None else total + part
        return total

    rows = [(2 * TR + i, forcing[i : i + 1, :]) for i in range(TR)]
    update = jnp.where(0 < sweeps, image_update(rows), 0.0)
    z = [update[s * TR : (s + 1) * TR, :] for s in range(SECTIONS)]
    for sweep in range(1, NEWT):
        mixed = [None] * SECTIONS
        for i in range(TR):
            jac = jac_ref[i, :, lanes].astype(F32)
            for s in range(SECTIONS):
                part = jac * z[s][i : i + 1, :]
                mixed[s] = part if mixed[s] is None else mixed[s] + part
        rows = []
        for s in range(SECTIONS):
            mix = COEF[0][s] * mixed[0] + COEF[1][s] * mixed[1] + COEF[2][s] * mixed[2]
            residual = mix - z[s]
            if s == SECTIONS - 1:
                residual = residual + forcing
            rows += [(s * TR + i, residual[i : i + 1, :]) for i in range(TR)]
        update = jnp.where(sweep < sweeps, image_update(rows), 0.0)
        z = [z[s] + update[s * TR : (s + 1) * TR, :] for s in range(SECTIONS)]
    return z[0] + z[1] + z[2]


def react_kernel(
    mask_ref, slabs_ref, own_in, below_ref, above_ref, sweeps_ref, jac_ref, inv_ref,
    tiles_ref, raw_ref, own_ref, north_ref, south_ref,
):
    blocks = arrived_blocks(mask_ref, slabs_ref, own_in, below_ref, above_ref)
    blocks = [
        column_block(blocks[r], r, jac_ref, inv_ref, sweeps_ref[r : r + 1, :]) for r in range(RB)
    ]
    emit_terms(blocks, tiles_ref, raw_ref, own_ref, north_ref, south_ref)


def step_kernel(
    mask_ref, slabs_ref, own_in, below_ref, above_ref,
    tiles_ref, raw_ref, own_ref, north_ref, south_ref,
):
    blocks = arrived_blocks(mask_ref, slabs_ref, own_in, below_ref, above_ref)
    emit_terms(blocks, tiles_ref, raw_ref, own_ref, north_ref, south_ref)


def last_kernel(mask_ref, slabs_ref, own_in, below_ref, above_ref, out_ref):
    blocks = arrived_blocks(mask_ref, slabs_ref, own_in, below_ref, above_ref)
    for r in range(RB):
        out_ref[:, r * BLK : (r + 1) * BLK] = blocks[r]


def struct(*shape):
    return jax.ShapeDtypeStruct(shape, F32)


TERM_SHAPES = (
    struct(TERMS * TR, BLK),
    struct(SLAB, BLK),
    struct(SLAB, BLK),
    struct(SLAB, BLK),
)


def call(kernel, out_shape, operands, smem, name, far=0, scratch=(), vmem_mib=12):
    many = isinstance(out_shape, tuple)
    size = sum(a.size * a.dtype.itemsize for a in operands)
    return pl.pallas_call(
        kernel,
        out_shape=out_shape,
        in_specs=[SMEM] * smem + [VMEM] * (len(operands) - smem - far) + [FAR] * far,
        out_specs=[VMEM] * len(out_shape) if many else VMEM,
        scratch_shapes=scratch,
        compiler_params=pltpu.CompilerParams(vmem_limit_bytes=vmem_mib * 1024 * 1024),
        cost_estimate=pl.CostEstimate(flops=0, bytes_accessed=size, transcendentals=0),
        name=name,
    )(*operands)


def body(
    adjoint,
    impl_tiles,
    expl_tiles,
    impl_dest,
    impl_local,
    expl_dest,
    expl_local,
    column_depth,
    newton,
    jacobian,
    newton_inverse,
):
    def gather_x(raw):
        return [shift_x(raw, k) for k in range(1, NX)]

    def deliver(terms, raws, slot):
        raw, own, north, south = terms
        dense = struct(NZ * SLAB, BLK)
        acc = pltpu.VMEM((2 * NZ * RB + 1, TR, BLK), F32)
        mine, other = call(
            merge_kernel, (dense, dense), [slot, raw, *raws], 1, "merge", scratch=[acc, acc]
        )
        slabs = exchange_z((mine + swap_core(other)).reshape(NZ, SLAB, BLK))
        return [masks, slabs, own, ring_lat(north, 1), ring_lat(south, N_LAT - 1)]

    int_table = jax.ShapeDtypeStruct((RB, BLK), jnp.int32)
    masks, sweeps = call(
        masks_kernel, (struct(RB + 2, BLK), int_table), [column_depth, newton], 2, "masks"
    )
    first_shapes = (struct(TERMS * TR + 2 * RB, BLK),) + TERM_SHAPES[1:]
    terms = call(
        first_kernel,
        first_shapes,
        [adjoint, impl_dest, impl_local, expl_dest, expl_local, impl_tiles],
        0,
        "first",
        far=6,
        vmem_mib=63,
        scratch=[
            pltpu.VMEM((TR, RB * BLK), F32),
            *[pltpu.VMEM((RB, NBAND), jnp.int32)] * 4,
            pltpu.VMEM((RB, NB, BLK, BLK), jnp.bfloat16),
            pltpu.SemaphoreType.DMA((5,)),
            pltpu.SemaphoreType.DMA((RB,)),
        ],
    )
    raws = gather_x(terms[0])
    slot_table = jax.ShapeDtypeStruct((NX * RB, NBAND), jnp.int32)
    slots = call(slots_kernel, (slot_table, slot_table), [terms[0], *raws], 0, "slots")
    for step_index in range(STEPS):
        if step_index:
            raws = gather_x(terms[0])
        arrived = deliver(terms, raws, slots[0])
        terms = call(
            react_kernel,
            TERM_SHAPES,
            arrived + [sweeps, jacobian, newton_inverse, expl_tiles],
            0,
            "react",
        )
        arrived = deliver(terms, gather_x(terms[0]), slots[1])
        if step_index + 1 < STEPS:
            terms = call(step_kernel, TERM_SHAPES, arrived + [impl_tiles], 0, "step")
    return call(last_kernel, struct(TR, RB * BLK), arrived, 0, "last")


def solution(mesh):
    both = ("cols", "lat")
    return jax.shard_map(
        body,
        mesh=mesh,
        in_specs=(
            P(None, both),
            P(both, None, None, None),
            P(both, None, None, None),
            P(both, None),
            P(both, None),
            P(both, None),
            P(both, None),
            P(both),
            P(both),
            P(None, None, both),
            P(None, None, both),
        ),
        out_specs=P(None, both),
        check_vma=False,
    )
```

time: 122 us -> 115 us (0.943)
  waiting for transfers between devices: 58.8 us -> 52 us
  starting transfers between devices: 44 us -> 46.6 us
  local copies, waits for them, and re-layouts: 4.03 us -> 2.44 us
    ppermute x15 -> x12, waiting for transfers between devices: 21.3 us -> 14.6 us  [shift_x(): return lax.ppermute(value, 'cols', pairs)]
    ppermute x15 -> x12, starting transfers between devices: 16.5 us -> 19 us  [shift_x(): return lax.ppermute(value, 'cols', pairs)]
    ppermute x4, waiting for transfers between devices: 4.15 us -> 5.53 us  [swap_core(): lax.ppermute(value, 'cols', [(i, i ^ 1) for i in range(NX * NZ * NCORE)])]
    pallas_call x9 -> x11, Pallas kernels: 9.4 us -> 10.2 us  [call(): pl.pallas_call(kernel, out_shape=out_shape, in_specs=[SMEM] * smem + [VME...]
    add x6 -> x4, other arithmetic: 3.5 us -> 2.74 us  [deliver(): slabs = exchange_z((mine + swap_core(other)).reshape(NZ, SLAB, BLK))]
    unnamed x20 -> x26, local copies, waits for them, and re-layouts: 3.13 us -> 2.44 us
  transfers between devices with their start and end apart: 31 -> 28, of which waited for: 25 -> 28; matrix products, arithmetic and copies ran while one was open for 1% -> 0% of each run, Pallas kernels for 0% -> 0%
where the time goes in v2:
time: 115 us; the launch traced here: 114 us
  waiting for transfers between devices  52 us (45%)
  starting transfers between devices  46.6 us (41%)
  Pallas kernels  10.2 us (9%)
  other arithmetic  2.74 us (2%)
  local copies, waits for them, and re-layouts  2.44 us (2%)
    all_to_all x4, waiting for transfers between devices, exchange_z(): lax.all_to_all(value, 'cols', 0, 0, axis_index_groups=groups, tiled=True)  19.7 us
    ppermute x12, starting transfers between devices, shift_x(): return lax.ppermute(value, 'cols', pairs)  19 us
    all_to_all x4, starting transfers between devices, exchange_z(): lax.all_to_all(value, 'cols', 0, 0, axis_index_groups=groups, tiled=True)  18.9 us
    ppermute x12, waiting for transfers between devices, shift_x(): return lax.ppermute(value, 'cols', pairs)  14.6 us
    ppermute x8, waiting for transfers between devices, ring_lat(): lax.ppermute(value, 'lat', [(i, (i + steps) % N_LAT) for i in range(N_LAT)])  12.1 us
    pallas_call x11, Pallas kernels, call(): pl.pallas_call(kernel, out_shape=out_shape, in_specs=[SMEM] * smem + [VME...  10.2 us
    ppermute x8, starting transfers between devices, ring_lat(): lax.ppermute(value, 'lat', [(i, (i + steps) % N_LAT) for i in range(N_LAT)])  8.41 us
    ppermute x4, waiting for transfers between devices, swap_core(): lax.ppermute(value, 'cols', [(i, i ^ 1) for i in range(NX * NZ * NCORE)])  5.53 us
  transfers between devices with their start and end apart: 28, of which 28 were waited for; matrix products, arithmetic and copies ran while one was open for 0% of the time, Pallas kernels for 0%

profile of v2, /device:TPU:24, one launch (start us, length us, event | category | flops | bytes accessed | tf_op | source)
XLA Modules:
  0.0 114.2 jit_solution(17870686523296865972)
XLA Ops:
  0.0 2.6 %first.1 = (f32[168,128]{1,0:T(8,128)}, f32[40,128]{1,0:T(8,128)}, f32[40,128]{1,0:T(8,128)}, f32[40,128]{1,0:T(8,128)}) custom-call(f32[10,512]{1,0:T(8,128)} %field_far.1, s32[4,4]{1,0:T(4,128)} %impl_dest_far.1, s32[4,4]{1,0:T(4,128)} %impl_local_far.1, s32[4,4]{1,0:T(4,128)} %expl_dest_far.1, s32[4,4]{1,0:T(4,128)} %expl_local_far.1, ...), custom_call_target="tpu_custom_call" | custom-call | bytes 938240 | tf_op jit(solution)/shard_map/first/pallas_call | solution.py:238
  2.6 1.6 %collective-permute-start = (f32[168,128]{1,0:T(8,128)}, f32[168,128]{1,0:T(8,128)S(1)}, u32[]{:S(2)}, u32[]{:S(2)}) collective-permute-start(f32[168,128]{1,0:T(8,128)} %get-tuple-element.34.raw0), channel_id=1, source_target_pairs={{0,64},{4,68},{8,72},{12,76},{16,80},{20,84},{24,88},{28,92},{32,9... | collective-permute-start | bytes 258056 | tf_op jit(solution)/shard_map/ppermute | solution.py:48
  4.2 2.7 %collective-permute-start.1 = (f32[168,128]{1,0:T(8,128)}, f32[168,128]{1,0:T(8,128)S(1)}, u32[]{:S(2)}, u32[]{:S(2)}) collective-permute-start(f32[168,128]{1,0:T(8,128)} %get-tuple-element.34.raw0), channel_id=1, source_target_pairs={{0,128},{4,132},{8,136},{12,140},{16,144},{20,148},{24,152},{28,15... | collective-permute-start | bytes 258056 | tf_op jit(solution)/shard_map/ppermute | solution.py:48
  6.9 1.4 %collective-permute-start.2 = (f32[168,128]{1,0:T(8,128)}, f32[168,128]{1,0:T(8,128)S(1)}, u32[]{:S(2)}, u32[]{:S(2)}) collective-permute-start(f32[168,128]{1,0:T(8,128)} %get-tuple-element.34.raw0), channel_id=1, source_target_pairs={{0,192},{4,196},{8,200},{12,204},{16,208},{20,212},{24,216},{28,22... | collective-permute-start | bytes 258056 | tf_op jit(solution)/shard_map/ppermute | solution.py:48
  8.4 0.6 collective-permute-done.raw1
  9.0 2.2 %collective-permute-done.1.raw2 = f32[168,128]{1,0:T(8,128)S(1)} collective-permute-done((f32[168,128]{1,0:T(8,128)}, f32[168,128]{1,0:T(8,128)S(1)}, u32[]{:S(2)}, u32[]{:S(2)}) %collective-permute-start.1) | collective-permute-done | bytes 86048 | tf_op jit(solution)/shard_map/ppermute | solution.py:48
  11.2 0.4 collective-permute-done.2.raw3
  11.6 0.9 copy-done.4
  12.6 0.9 copy-done.5
  13.4 1.0 merge.4
  14.5 1.4 %collective-permute-done.3 = f32[320,128]{1,0:T(8,128)S(1)} collective-permute-done((f32[320,128]{1,0:T(8,128)S(1)}, f32[320,128]{1,0:T(8,128)S(1)}, u32[]{:S(2)}, u32[]{:S(2)}) %collective-permute-start.3) | collective-permute-done | bytes 163872 | tf_op jit(solution)/shard_map/ppermute | solution.py:52
  15.9 0.7 add.12
  16.6 8.6 %all-to-all-start = ((f32[8,40,128]{2,1,0:T(8,128)}), f32[8,40,128]{2,1,0:T(8,128)S(1)}, u32[]{:S(2)}, u32[]{:S(2)}) async-start(f32[8,40,128]{2,1,0:T(8,128)} %bitcast), calls=%async_computation | async-start | bytes 327680 | tf_op jit(solution)/shard_map/all_to_all | solution.py:61
  25.6 1.8 %collective-permute-start.5 = (f32[40,128]{1,0:T(8,128)S(1)}, f32[40,128]{1,0:T(8,128)S(1)}, u32[]{:S(2)}, u32[]{:S(2)}) collective-permute-start(f32[40,128]{1,0:T(8,128)S(1)} %copy-done.11), channel_id=1, source_target_pairs={{0,3},{1,0},{2,1},{3,2},{4,7},{5,4},{6,5},{7,6},{8,11},{9,8},{10,9... | collective-permute-start | bytes 61448 | tf_op jit(solution)/shard_map/ppermute | solution.py:56
  27.4 0.6 masks.1
  27.9 1.2 %collective-permute-done.4.below_ref = f32[40,128]{1,0:T(8,128)S(1)} collective-permute-done((f32[40,128]{1,0:T(8,128)S(1)}, f32[40,128]{1,0:T(8,128)S(1)}, u32[]{:S(2)}, u32[]{:S(2)}) %collective-permute-start.4) | collective-permute-done | bytes 20512 | tf_op jit(solution)/shard_map/ppermute | solution.py:56
  29.1 1.5 %collective-permute-done.5.above_ref = f32[40,128]{1,0:T(8,128)S(1)} collective-permute-done((f32[40,128]{1,0:T(8,128)S(1)}, f32[40,128]{1,0:T(8,128)S(1)}, u32[]{:S(2)}, u32[]{:S(2)}) %collective-permute-start.5) | collective-permute-done | bytes 20512 | tf_op jit(solution)/shard_map/ppermute | solution.py:56
  30.6 4.7 %all-to-all-done.slabs_ref = f32[8,40,128]{2,1,0:T(8,128)S(1)} async-done(((f32[8,40,128]{2,1,0:T(8,128)}), f32[8,40,128]{2,1,0:T(8,128)S(1)}, u32[]{:S(2)}, u32[]{:S(2)}) %all-to-all-start) | async-done | bytes 163872 | tf_op jit(solution)/shard_map/all_to_all | solution.py:61
  35.3 1.1 react.2
  36.4 0.6 copy-done.7
  37.0 1.0 collective-permute-start.6
  38.0 3.1 %collective-permute-start.7 = (f32[160,128]{1,0:T(8,128)S(1)}, f32[160,128]{1,0:T(8,128)S(1)}, u32[]{:S(2)}, u32[]{:S(2)}) collective-permute-start(f32[160,128]{1,0:T(8,128)S(1)} %get-tuple-element.43.raw0), channel_id=1, source_target_pairs={{0,128},{4,132},{8,136},{12,140},{16,144},{20,148},{24,152},{28,15... | collective-permute-start | bytes 245768 | tf_op jit(solution)/shard_map/ppermute | solution.py:48
  41.1 0.7 collective-permute-start.8
  41.8 0.9 collective-permute-done.6.raw1
  42.7 1.7 %collective-permute-done.7.raw2 = f32[160,128]{1,0:T(8,128)S(1)} collective-permute-done((f32[160,128]{1,0:T(8,128)S(1)}, f32[160,128]{1,0:T(8,128)S(1)}, u32[]{:S(2)}, u32[]{:S(2)}) %collective-permute-start.7) | collective-permute-done | bytes 81952 | tf_op jit(solution)/shard_map/ppermute | solution.py:48
  44.4 1.1 %collective-permute-done.8.raw3 = f32[160,128]{1,0:T(8,128)S(1)} collective-permute-done((f32[160,128]{1,0:T(8,128)S(1)}, f32[160,128]{1,0:T(8,128)S(1)}, u32[]{:S(2)}, u32[]{:S(2)}) %collective-permute-start.8) | collective-permute-done | bytes 81952 | tf_op jit(solution)/shard_map/ppermute | solution.py:48
  45.6 1.0 merge.5
  46.6 1.4 %collective-permute-done.9 = f32[320,128]{1,0:T(8,128)S(1)} collective-permute-done((f32[320,128]{1,0:T(8,128)S(1)}, f32[320,128]{1,0:T(8,128)S(1)}, u32[]{:S(2)}, u32[]{:S(2)}) %collective-permute-start.9) | collective-permute-done | bytes 163872 | tf_op jit(solution)/shard_map/ppermute | solution.py:52
  48.0 0.7 add.13
  48.7 3.5 %all-to-all-start.1 = ((f32[8,40,128]{2,1,0:T(8,128)}), f32[8,40,128]{2,1,0:T(8,128)S(1)}, u32[]{:S(2)}, u32[]{:S(2)}) async-start(f32[8,40,128]{2,1,0:T(8,128)} %bitcast.1), calls=%async_computation.1 | async-start | bytes 327680 | tf_op jit(solution)/shard_map/all_to_all | solution.py:61
  52.5 1.8 %collective-permute-start.11 = (f32[40,128]{1,0:T(8,128)S(1)}, f32[40,128]{1,0:T(8,128)S(1)}, u32[]{:S(2)}, u32[]{:S(2)}) collective-permute-start(f32[40,128]{1,0:T(8,128)S(1)} %get-tuple-element.48), channel_id=1, source_target_pairs={{0,3},{1,0},{2,1},{3,2},{4,7},{5,4},{6,5},{7,6},{8,11},{9,8},{10,9... | collective-permute-start | bytes 61448 | tf_op jit(solution)/shard_map/ppermute | solution.py:56
  54.4 1.8 %collective-permute-done.10.below_ref = f32[40,128]{1,0:T(8,128)S(1)} collective-permute-done((f32[40,128]{1,0:T(8,128)S(1)}, f32[40,128]{1,0:T(8,128)S(1)}, u32[]{:S(2)}, u32[]{:S(2)}) %collective-permute-start.10) | collective-permute-done | bytes 20512 | tf_op jit(solution)/shard_map/ppermute | solution.py:56
  56.1 1.4 %collective-permute-done.11.above_ref = f32[40,128]{1,0:T(8,128)S(1)} collective-permute-done((f32[40,128]{1,0:T(8,128)S(1)}, f32[40,128]{1,0:T(8,128)S(1)}, u32[]{:S(2)}, u32[]{:S(2)}) %collective-permute-start.11) | collective-permute-done | bytes 20512 | tf_op jit(solution)/shard_map/ppermute | solution.py:56
  57.5 5.0 %all-to-all-done.1.slabs_ref = f32[8,40,128]{2,1,0:T(8,128)S(1)} async-done(((f32[8,40,128]{2,1,0:T(8,128)}), f32[8,40,128]{2,1,0:T(8,128)S(1)}, u32[]{:S(2)}, u32[]{:S(2)}) %all-to-all-start.1) | async-done | bytes 163872 | tf_op jit(solution)/shard_map/all_to_all | solution.py:61
  62.8 0.5 collective-permute-start.12
  63.3 3.0 %collective-permute-start.13 = (f32[160,128]{1,0:T(8,128)S(1)}, f32[160,128]{1,0:T(8,128)S(1)}, u32[]{:S(2)}, u32[]{:S(2)}) collective-permute-start(f32[160,128]{1,0:T(8,128)S(1)} %get-tuple-element.49.raw0), channel_id=1, source_target_pairs={{0,128},{4,132},{8,136},{12,140},{16,144},{20,148},{24,152},{28,15... | collective-permute-start | bytes 245768 | tf_op jit(solution)/shard_map/ppermute | solution.py:48
  66.3 0.8 collective-permute-start.14
  67.0 1.5 %collective-permute-done.12.raw1 = f32[160,128]{1,0:T(8,128)S(1)} collective-permute-done((f32[160,128]{1,0:T(8,128)S(1)}, f32[160,128]{1,0:T(8,128)S(1)}, u32[]{:S(2)}, u32[]{:S(2)}) %collective-permute-start.12) | collective-permute-done | bytes 81952 | tf_op jit(solution)/shard_map/ppermute | solution.py:48
  68.5 1.0 collective-permute-done.13.raw2
  69.6 1.1 %collective-permute-done.14.raw3 = f32[160,128]{1,0:T(8,128)S(1)} collective-permute-done((f32[160,128]{1,0:T(8,128)S(1)}, f32[160,128]{1,0:T(8,128)S(1)}, u32[]{:S(2)}, u32[]{:S(2)}) %collective-permute-start.14) | collective-permute-done | bytes 81952 | tf_op jit(solution)/shard_map/ppermute | solution.py:48
  70.7 1.0 merge.6
  71.8 1.4 %collective-permute-done.15 = f32[320,128]{1,0:T(8,128)S(1)} collective-permute-done((f32[320,128]{1,0:T(8,128)S(1)}, f32[320,128]{1,0:T(8,128)S(1)}, u32[]{:S(2)}, u32[]{:S(2)}) %collective-permute-start.15) | collective-permute-done | bytes 163872 | tf_op jit(solution)/shard_map/ppermute | solution.py:52
  73.2 0.7 add.14
  73.9 3.4 %all-to-all-start.2 = ((f32[8,40,128]{2,1,0:T(8,128)}), f32[8,40,128]{2,1,0:T(8,128)S(1)}, u32[]{:S(2)}, u32[]{:S(2)}) async-start(f32[8,40,128]{2,1,0:T(8,128)} %bitcast.2), calls=%async_computation.2 | async-start | bytes 327680 | tf_op jit(solution)/shard_map/all_to_all | solution.py:61
  77.5 1.8 %collective-permute-start.17 = (f32[40,128]{1,0:T(8,128)S(1)}, f32[40,128]{1,0:T(8,128)S(1)}, u32[]{:S(2)}, u32[]{:S(2)}) collective-permute-start(f32[40,128]{1,0:T(8,128)S(1)} %get-tuple-element.54), channel_id=1, source_target_pairs={{0,3},{1,0},{2,1},{3,2},{4,7},{5,4},{6,5},{7,6},{8,11},{9,8},{10,9... | collective-permute-start | bytes 61448 | tf_op jit(solution)/shard_map/ppermute | solution.py:56
  79.4 1.8 %collective-permute-done.16.below_ref = f32[40,128]{1,0:T(8,128)S(1)} collective-permute-done((f32[40,128]{1,0:T(8,128)S(1)}, f32[40,128]{1,0:T(8,128)S(1)}, u32[]{:S(2)}, u32[]{:S(2)}) %collective-permute-start.16) | collective-permute-done | bytes 20512 | tf_op jit(solution)/shard_map/ppermute | solution.py:56
  81.1 1.4 %collective-permute-done.17.above_ref = f32[40,128]{1,0:T(8,128)S(1)} collective-permute-done((f32[40,128]{1,0:T(8,128)S(1)}, f32[40,128]{1,0:T(8,128)S(1)}, u32[]{:S(2)}, u32[]{:S(2)}) %collective-permute-start.17) | collective-permute-done | bytes 20512 | tf_op jit(solution)/shard_map/ppermute | solution.py:56
  82.5 5.0 %all-to-all-done.2.slabs_ref = f32[8,40,128]{2,1,0:T(8,128)S(1)} async-done(((f32[8,40,128]{2,1,0:T(8,128)}), f32[8,40,128]{2,1,0:T(8,128)S(1)}, u32[]{:S(2)}, u32[]{:S(2)}) %all-to-all-start.2) | async-done | bytes 163872 | tf_op jit(solution)/shard_map/all_to_all | solution.py:61
  87.5 1.1 react.3
  88.6 0.8 collective-permute-start.18
  89.4 3.0 %collective-permute-start.19 = (f32[160,128]{1,0:T(8,128)S(1)}, f32[160,128]{1,0:T(8,128)S(1)}, u32[]{:S(2)}, u32[]{:S(2)}) collective-permute-start(f32[160,128]{1,0:T(8,128)S(1)} %get-tuple-element.55.raw0), channel_id=1, source_target_pairs={{0,128},{4,132},{8,136},{12,140},{16,144},{20,148},{24,152},{28,15... | collective-permute-start | bytes 245768 | tf_op jit(solution)/shard_map/ppermute | solution.py:48
  92.3 0.4 collective-permute-start.20
  92.8 1.7 %collective-permute-done.18.raw1 = f32[160,128]{1,0:T(8,128)S(1)} collective-permute-done((f32[160,128]{1,0:T(8,128)S(1)}, f32[160,128]{1,0:T(8,128)S(1)}, u32[]{:S(2)}, u32[]{:S(2)}) %collective-permute-start.18) | collective-permute-done | bytes 81952 | tf_op jit(solution)/shard_map/ppermute | solution.py:48
  94.5 1.2 %collective-permute-done.19.raw2 = f32[160,128]{1,0:T(8,128)S(1)} collective-permute-done((f32[160,128]{1,0:T(8,128)S(1)}, f32[160,128]{1,0:T(8,128)S(1)}, u32[]{:S(2)}, u32[]{:S(2)}) %collective-permute-start.19) | collective-permute-done | bytes 81952 | tf_op jit(solution)/shard_map/ppermute | solution.py:48
  95.6 1.1 %collective-permute-done.20.raw3 = f32[160,128]{1,0:T(8,128)S(1)} collective-permute-done((f32[160,128]{1,0:T(8,128)S(1)}, f32[160,128]{1,0:T(8,128)S(1)}, u32[]{:S(2)}, u32[]{:S(2)}) %collective-permute-start.20) | collective-permute-done | bytes 81952 | tf_op jit(solution)/shard_map/ppermute | solution.py:48
  96.8 1.0 merge.7
  97.8 1.4 %collective-permute-done.21 = f32[320,128]{1,0:T(8,128)S(1)} collective-permute-done((f32[320,128]{1,0:T(8,128)S(1)}, f32[320,128]{1,0:T(8,128)S(1)}, u32[]{:S(2)}, u32[]{:S(2)}) %collective-permute-start.21) | collective-permute-done | bytes 163872 | tf_op jit(solution)/shard_map/ppermute | solution.py:52
  99.2 0.7 add.15
  99.9 3.4 %all-to-all-start.3 = ((f32[8,40,128]{2,1,0:T(8,128)}), f32[8,40,128]{2,1,0:T(8,128)S(1)}, u32[]{:S(2)}, u32[]{:S(2)}) async-start(f32[8,40,128]{2,1,0:T(8,128)} %bitcast.3), calls=%async_computation.3 | async-start | bytes 327680 | tf_op jit(solution)/shard_map/all_to_all | solution.py:61
  103.6 1.8 %collective-permute-start.23 = (f32[40,128]{1,0:T(8,128)S(1)}, f32[40,128]{1,0:T(8,128)S(1)}, u32[]{:S(2)}, u32[]{:S(2)}) collective-permute-start(f32[40,128]{1,0:T(8,128)S(1)} %get-tuple-element.60), channel_id=1, source_target_pairs={{0,3},{1,0},{2,1},{3,2},{4,7},{5,4},{6,5},{7,6},{8,11},{9,8},{10,9... | collective-permute-start | bytes 61448 | tf_op jit(solution)/shard_map/ppermute | solution.py:56
  105.4 1.8 %collective-permute-done.22.below_ref = f32[40,128]{1,0:T(8,128)S(1)} collective-permute-done((f32[40,128]{1,0:T(8,128)S(1)}, f32[40,128]{1,0:T(8,128)S(1)}, u32[]{:S(2)}, u32[]{:S(2)}) %collective-permute-start.22) | collective-permute-done | bytes 20512 | tf_op jit(solution)/shard_map/ppermute | solution.py:56
  107.2 1.4 %collective-permute-done.23.above_ref = f32[40,128]{1,0:T(8,128)S(1)} collective-permute-done((f32[40,128]{1,0:T(8,128)S(1)}, f32[40,128]{1,0:T(8,128)S(1)}, u32[]{:S(2)}, u32[]{:S(2)}) %collective-permute-start.23) | collective-permute-done | bytes 20512 | tf_op jit(solution)/shard_map/ppermute | solution.py:56
  108.6 5.0 %all-to-all-done.3.slabs_ref = f32[8,40,128]{2,1,0:T(8,128)S(1)} async-done(((f32[8,40,128]{2,1,0:T(8,128)}), f32[8,40,128]{2,1,0:T(8,128)S(1)}, u32[]{:S(2)}, u32[]{:S(2)}) %all-to-all-start.3) | async-done | bytes 163872 | tf_op jit(solution)/shard_map/all_to_all | solution.py:61
  113.6 0.6 last.1
  (33 shorter events, 2.0 us)
Async XLA Ops:
  0.0 35.3 %copy-start.2 = (bf16[4,7,128,128]{3,2,1,0:T(8,128)(2,1)S(1)}, bf16[4,7,128,128]{3,2,1,0:T(8,128)(2,1)}, u32[]{:S(2)}) copy-start(bf16[4,7,128,128]{3,2,1,0:T(8,128)(2,1)} %tiles_ref.5) | copy-start | bytes 2752516
  2.6 32.7 %copy-start = (bf16[30,30,512]{2,1,0:T(8,128)(2,1)S(1)}, bf16[30,30,512]{2,1,0:T(8,128)(2,1)}, u32[]{:S(2)}) copy-start(bf16[30,30,512]{2,1,0:T(8,128)(2,1)} %inv_ref.3) | copy-start | bytes 2764804
  2.6 6.4 %collective-permute-start = (f32[168,128]{1,0:T(8,128)}, f32[168,128]{1,0:T(8,128)S(1)}, u32[]{:S(2)}, u32[]{:S(2)}) collective-permute-start(f32[168,128]{1,0:T(8,128)} %get-tuple-element.34.raw0), channel_id=1, source_target_pairs={{0,64},{4,68},{8,72},{12,76},{16,80},{20,84},{24,88},{28,92},{32,9... | collective-permute-start | bytes 258056 | tf_op jit(solution)/shard_map/ppermute | solution.py:48
  4.2 7.0 %collective-permute-start.1 = (f32[168,128]{1,0:T(8,128)}, f32[168,128]{1,0:T(8,128)S(1)}, u32[]{:S(2)}, u32[]{:S(2)}) collective-permute-start(f32[168,128]{1,0:T(8,128)} %get-tuple-element.34.raw0), channel_id=1, source_target_pairs={{0,128},{4,132},{8,136},{12,140},{16,144},{20,148},{24,152},{28,15... | collective-permute-start | bytes 258056 | tf_op jit(solution)/shard_map/ppermute | solution.py:48
  6.9 4.7 %collective-permute-start.2 = (f32[168,128]{1,0:T(8,128)}, f32[168,128]{1,0:T(8,128)S(1)}, u32[]{:S(2)}, u32[]{:S(2)}) collective-permute-start(f32[168,128]{1,0:T(8,128)} %get-tuple-element.34.raw0), channel_id=1, source_target_pairs={{0,192},{4,196},{8,200},{12,204},{16,208},{20,212},{24,216},{28,22... | collective-permute-start | bytes 258056 | tf_op jit(solution)/shard_map/ppermute | solution.py:48
  11.6 0.9 copy-start.4
  12.5 0.9 copy-start.5
  14.4 1.5 %collective-permute-start.3 = (f32[320,128]{1,0:T(8,128)S(1)}, f32[320,128]{1,0:T(8,128)S(1)}, u32[]{:S(2)}, u32[]{:S(2)}) collective-permute-start(f32[320,128]{1,0:T(8,128)S(1)} %get-tuple-element.38), channel_id=1, source_target_pairs={{0,4},{4,0},{8,12},{12,8},{16,20},{20,16},{24,28},{28,24},{32,36},... | collective-permute-start | bytes 491528 | tf_op jit(solution)/shard_map/ppermute | solution.py:52
  16.6 8.6 %copy-start.12 = (f32[40,128]{1,0:T(8,128)S(1)}, f32[40,128]{1,0:T(8,128)}, u32[]{:S(2)}) copy-start(f32[40,128]{1,0:T(8,128)} %get-tuple-element.40) | copy-start | bytes 61444
  16.6 9.0 %copy-start.11 = (f32[40,128]{1,0:T(8,128)S(1)}, f32[40,128]{1,0:T(8,128)}, u32[]{:S(2)}) copy-start(f32[40,128]{1,0:T(8,128)} %get-tuple-element.41) | copy-start | bytes 61444
  16.6 18.7 %copy-start.3 = (bf16[10,10,512]{2,1,0:T(8,128)(2,1)S(1)}, bf16[10,10,512]{2,1,0:T(8,128)(2,1)}, u32[]{:S(2)}) copy-start(bf16[10,10,512]{2,1,0:T(8,128)(2,1)} %jac_ref.3) | copy-start | bytes 307204
  16.6 18.7 %copy-start.6 = (f32[40,128]{1,0:T(8,128)S(1)}, f32[40,128]{1,0:T(8,128)}, u32[]{:S(2)}) copy-start(f32[40,128]{1,0:T(8,128)} %get-tuple-element.39.own_in) | copy-start | bytes 61444
  16.6 18.7 %all-to-all-start = ((f32[8,40,128]{2,1,0:T(8,128)}), f32[8,40,128]{2,1,0:T(8,128)S(1)}, u32[]{:S(2)}, u32[]{:S(2)}) async-start(f32[8,40,128]{2,1,0:T(8,128)} %bitcast), calls=%async_computation | async-start | bytes 327680 | tf_op jit(solution)/shard_map/all_to_all | solution.py:61
  25.2 2.1 %copy-start.9 = (s32[8]{0:T(128)S(1)}, s32[8]{0:T(128)}, u32[]{:S(2)}) copy-start(s32[8]{0:T(128)} %depth_ref.1) | copy-start | bytes 100
  25.2 2.1 %copy-start.10 = (s32[8]{0:T(128)S(1)}, s32[8]{0:T(128)}, u32[]{:S(2)}) copy-start(s32[8]{0:T(128)} %newton_ref.1) | copy-start | bytes 100
  25.2 3.9 %collective-permute-start.4 = (f32[40,128]{1,0:T(8,128)S(1)}, f32[40,128]{1,0:T(8,128)S(1)}, u32[]{:S(2)}, u32[]{:S(2)}) collective-permute-start(f32[40,128]{1,0:T(8,128)S(1)} %copy-done.12), channel_id=1, source_target_pairs={{0,1},{1,2},{2,3},{3,0},{4,5},{5,6},{6,7},{7,4},{8,9},{9,10},{10,1... | collective-permute-start | bytes 61448 | tf_op jit(solution)/shard_map/ppermute | solution.py:56
  25.6 5.0 %collective-permute-start.5 = (f32[40,128]{1,0:T(8,128)S(1)}, f32[40,128]{1,0:T(8,128)S(1)}, u32[]{:S(2)}, u32[]{:S(2)}) collective-permute-start(f32[40,128]{1,0:T(8,128)S(1)} %copy-done.11), channel_id=1, source_target_pairs={{0,3},{1,0},{2,1},{3,2},{4,7},{5,4},{6,5},{7,6},{8,11},{9,8},{10,9... | collective-permute-start | bytes 61448 | tf_op jit(solution)/shard_map/ppermute | solution.py:56
  36.4 0.6 copy-start.7
  37.0 25.5 %copy-start.1 = (bf16[4,7,128,128]{3,2,1,0:T(8,128)(2,1)S(1)}, bf16[4,7,128,128]{3,2,1,0:T(8,128)(2,1)}, u32[]{:S(2)}) copy-start(bf16[4,7,128,128]{3,2,1,0:T(8,128)(2,1)} %tiles_ref.4) | copy-start | bytes 2752516
  37.0 5.7 %collective-permute-start.6 = (f32[160,128]{1,0:T(8,128)S(1)}, f32[160,128]{1,0:T(8,128)S(1)}, u32[]{:S(2)}, u32[]{:S(2)}) collective-permute-start(f32[160,128]{1,0:T(8,128)S(1)} %get-tuple-element.43.raw0), channel_id=1, source_target_pairs={{0,64},{4,68},{8,72},{12,76},{16,80},{20,84},{24,88},{28,92},{32,9... | collective-permute-start | bytes 245768 | tf_op jit(solution)/shard_map/ppermute | solution.py:48
  38.0 6.4 %collective-permute-start.7 = (f32[160,128]{1,0:T(8,128)S(1)}, f32[160,128]{1,0:T(8,128)S(1)}, u32[]{:S(2)}, u32[]{:S(2)}) collective-permute-start(f32[160,128]{1,0:T(8,128)S(1)} %get-tuple-element.43.raw0), channel_id=1, source_target_pairs={{0,128},{4,132},{8,136},{12,140},{16,144},{20,148},{24,152},{28,15... | collective-permute-start | bytes 245768 | tf_op jit(solution)/shard_map/ppermute | solution.py:48
  41.1 4.4 %collective-permute-start.8 = (f32[160,128]{1,0:T(8,128)S(1)}, f32[160,128]{1,0:T(8,128)S(1)}, u32[]{:S(2)}, u32[]{:S(2)}) collective-permute-start(f32[160,128]{1,0:T(8,128)S(1)} %get-tuple-element.43.raw0), channel_id=1, source_target_pairs={{0,192},{4,196},{8,200},{12,204},{16,208},{20,212},{24,216},{28,22... | collective-permute-start | bytes 245768 | tf_op jit(solution)/shard_map/ppermute | solution.py:48
  46.5 1.5 %collective-permute-start.9 = (f32[320,128]{1,0:T(8,128)S(1)}, f32[320,128]{1,0:T(8,128)S(1)}, u32[]{:S(2)}, u32[]{:S(2)}) collective-permute-start(f32[320,128]{1,0:T(8,128)S(1)} %get-tuple-element.45), channel_id=1, source_target_pairs={{0,4},{4,0},{8,12},{12,8},{16,20},{20,16},{24,28},{28,24},{32,36},... | collective-permute-start | bytes 491528 | tf_op jit(solution)/shard_map/ppermute | solution.py:52
  48.7 3.5 %copy-start.8 = (f32[40,128]{1,0:T(8,128)S(1)}, f32[40,128]{1,0:T(8,128)}, u32[]{:S(2)}) copy-start(f32[40,128]{1,0:T(8,128)} %copy-done.7) | copy-start | bytes 61444
  48.7 13.8 %all-to-all-start.1 = ((f32[8,40,128]{2,1,0:T(8,128)}), f32[8,40,128]{2,1,0:T(8,128)S(1)}, u32[]{:S(2)}, u32[]{:S(2)}) async-start(f32[8,40,128]{2,1,0:T(8,128)} %bitcast.1), calls=%async_computation.1 | async-start | bytes 327680 | tf_op jit(solution)/shard_map/all_to_all | solution.py:61
  52.2 3.9 %collective-permute-start.10 = (f32[40,128]{1,0:T(8,128)S(1)}, f32[40,128]{1,0:T(8,128)S(1)}, u32[]{:S(2)}, u32[]{:S(2)}) collective-permute-start(f32[40,128]{1,0:T(8,128)S(1)} %copy-done.8), channel_id=1, source_target_pairs={{0,1},{1,2},{2,3},{3,0},{4,5},{5,6},{6,7},{7,4},{8,9},{9,10},{10,1... | collective-permute-start | bytes 61448 | tf_op jit(solution)/shard_map/ppermute | solution.py:56
  52.5 5.0 %collective-permute-start.11 = (f32[40,128]{1,0:T(8,128)S(1)}, f32[40,128]{1,0:T(8,128)S(1)}, u32[]{:S(2)}, u32[]{:S(2)}) collective-permute-start(f32[40,128]{1,0:T(8,128)S(1)} %get-tuple-element.48), channel_id=1, source_target_pairs={{0,3},{1,0},{2,1},{3,2},{4,7},{5,4},{6,5},{7,6},{8,11},{9,8},{10,9... | collective-permute-start | bytes 61448 | tf_op jit(solution)/shard_map/ppermute | solution.py:56
  62.8 5.7 %collective-permute-start.12 = (f32[160,128]{1,0:T(8,128)S(1)}, f32[160,128]{1,0:T(8,128)S(1)}, u32[]{:S(2)}, u32[]{:S(2)}) collective-permute-start(f32[160,128]{1,0:T(8,128)S(1)} %get-tuple-element.49.raw0), channel_id=1, source_target_pairs={{0,64},{4,68},{8,72},{12,76},{16,80},{20,84},{24,88},{28,92},{32,9... | collective-permute-start | bytes 245768 | tf_op jit(solution)/shard_map/ppermute | solution.py:48
  63.3 6.2 %collective-permute-start.13 = (f32[160,128]{1,0:T(8,128)S(1)}, f32[160,128]{1,0:T(8,128)S(1)}, u32[]{:S(2)}, u32[]{:S(2)}) collective-permute-start(f32[160,128]{1,0:T(8,128)S(1)} %get-tuple-element.49.raw0), channel_id=1, source_target_pairs={{0,128},{4,132},{8,136},{12,140},{16,144},{20,148},{24,152},{28,15... | collective-permute-start | bytes 245768 | tf_op jit(solution)/shard_map/ppermute | solution.py:48
  66.3 4.4 %collective-permute-start.14 = (f32[160,128]{1,0:T(8,128)S(1)}, f32[160,128]{1,0:T(8,128)S(1)}, u32[]{:S(2)}, u32[]{:S(2)}) collective-permute-start(f32[160,128]{1,0:T(8,128)S(1)} %get-tuple-element.49.raw0), channel_id=1, source_target_pairs={{0,192},{4,196},{8,200},{12,204},{16,208},{20,212},{24,216},{28,22... | collective-permute-start | bytes 245768 | tf_op jit(solution)/shard_map/ppermute | solution.py:48
  71.7 1.5 %collective-permute-start.15 = (f32[320,128]{1,0:T(8,128)S(1)}, f32[320,128]{1,0:T(8,128)S(1)}, u32[]{:S(2)}, u32[]{:S(2)}) collective-permute-start(f32[320,128]{1,0:T(8,128)S(1)} %get-tuple-element.51), channel_id=1, source_target_pairs={{0,4},{4,0},{8,12},{12,8},{16,20},{20,16},{24,28},{28,24},{32,36},... | collective-permute-start | bytes 491528 | tf_op jit(solution)/shard_map/ppermute | solution.py:52
  73.9 13.7 %all-to-all-start.2 = ((f32[8,40,128]{2,1,0:T(8,128)}), f32[8,40,128]{2,1,0:T(8,128)S(1)}, u32[]{:S(2)}, u32[]{:S(2)}) async-start(f32[8,40,128]{2,1,0:T(8,128)} %bitcast.2), calls=%async_computation.2 | async-start | bytes 327680 | tf_op jit(solution)/shard_map/all_to_all | solution.py:61
  77.3 3.9 %collective-permute-start.16 = (f32[40,128]{1,0:T(8,128)S(1)}, f32[40,128]{1,0:T(8,128)S(1)}, u32[]{:S(2)}, u32[]{:S(2)}) collective-permute-start(f32[40,128]{1,0:T(8,128)S(1)} %get-tuple-element.53), channel_id=1, source_target_pairs={{0,1},{1,2},{2,3},{3,0},{4,5},{5,6},{6,7},{7,4},{8,9},{9,10},{10,1... | collective-permute-start | bytes 61448 | tf_op jit(solution)/shard_map/ppermute | solution.py:56
  77.5 5.0 %collective-permute-start.17 = (f32[40,128]{1,0:T(8,128)S(1)}, f32[40,128]{1,0:T(8,128)S(1)}, u32[]{:S(2)}, u32[]{:S(2)}) collective-permute-start(f32[40,128]{1,0:T(8,128)S(1)} %get-tuple-element.54), channel_id=1, source_target_pairs={{0,3},{1,0},{2,1},{3,2},{4,7},{5,4},{6,5},{7,6},{8,11},{9,8},{10,9... | collective-permute-start | bytes 61448 | tf_op jit(solution)/shard_map/ppermute | solution.py:56
  88.6 5.9 %collective-permute-start.18 = (f32[160,128]{1,0:T(8,128)S(1)}, f32[160,128]{1,0:T(8,128)S(1)}, u32[]{:S(2)}, u32[]{:S(2)}) collective-permute-start(f32[160,128]{1,0:T(8,128)S(1)} %get-tuple-element.55.raw0), channel_id=1, source_target_pairs={{0,64},{4,68},{8,72},{12,76},{16,80},{20,84},{24,88},{28,92},{32,9... | collective-permute-start | bytes 245768 | tf_op jit(solution)/shard_map/ppermute | solution.py:48
  89.4 6.2 %collective-permute-start.19 = (f32[160,128]{1,0:T(8,128)S(1)}, f32[160,128]{1,0:T(8,128)S(1)}, u32[]{:S(2)}, u32[]{:S(2)}) collective-permute-start(f32[160,128]{1,0:T(8,128)S(1)} %get-tuple-element.55.raw0), channel_id=1, source_target_pairs={{0,128},{4,132},{8,136},{12,140},{16,144},{20,148},{24,152},{28,15... | collective-permute-start | bytes 245768 | tf_op jit(solution)/shard_map/ppermute | solution.py:48
  92.3 4.4 %collective-permute-start.20 = (f32[160,128]{1,0:T(8,128)S(1)}, f32[160,128]{1,0:T(8,128)S(1)}, u32[]{:S(2)}, u32[]{:S(2)}) collective-permute-start(f32[160,128]{1,0:T(8,128)S(1)} %get-tuple-element.55.raw0), channel_id=1, source_target_pairs={{0,192},{4,196},{8,200},{12,204},{16,208},{20,212},{24,216},{28,22... | collective-permute-start | bytes 245768 | tf_op jit(solution)/shard_map/ppermute | solution.py:48
  97.7 1.5 %collective-permute-start.21 = (f32[320,128]{1,0:T(8,128)S(1)}, f32[320,128]{1,0:T(8,128)S(1)}, u32[]{:S(2)}, u32[]{:S(2)}) collective-permute-start(f32[320,128]{1,0:T(8,128)S(1)} %get-tuple-element.57), channel_id=1, source_target_pairs={{0,4},{4,0},{8,12},{12,8},{16,20},{20,16},{24,28},{28,24},{32,36},... | collective-permute-start | bytes 491528 | tf_op jit(solution)/shard_map/ppermute | solution.py:52
  99.9 13.7 %all-to-all-start.3 = ((f32[8,40,128]{2,1,0:T(8,128)}), f32[8,40,128]{2,1,0:T(8,128)S(1)}, u32[]{:S(2)}, u32[]{:S(2)}) async-start(f32[8,40,128]{2,1,0:T(8,128)} %bitcast.3), calls=%async_computation.3 | async-start | bytes 327680 | tf_op jit(solution)/shard_map/all_to_all | solution.py:61
  103.3 3.9 %collective-permute-start.22 = (f32[40,128]{1,0:T(8,128)S(1)}, f32[40,128]{1,0:T(8,128)S(1)}, u32[]{:S(2)}, u32[]{:S(2)}) collective-permute-start(f32[40,128]{1,0:T(8,128)S(1)} %get-tuple-element.59), channel_id=1, source_target_pairs={{0,1},{1,2},{2,3},{3,0},{4,5},{5,6},{6,7},{7,4},{8,9},{9,10},{10,1... | collective-permute-start | bytes 61448 | tf_op jit(solution)/shard_map/ppermute | solution.py:56
  103.6 5.0 %collective-permute-start.23 = (f32[40,128]{1,0:T(8,128)S(1)}, f32[40,128]{1,0:T(8,128)S(1)}, u32[]{:S(2)}, u32[]{:S(2)}) collective-permute-start(f32[40,128]{1,0:T(8,128)S(1)} %get-tuple-element.60), channel_id=1, source_target_pairs={{0,3},{1,0},{2,1},{3,2},{4,7},{5,4},{6,5},{7,6},{8,11},{9,8},{10,9... | collective-permute-start | bytes 61448 | tf_op jit(solution)/shard_map/ppermute | solution.py:56

commit v3 on v2

--- a/solution.py
+++ b/solution.py
@@ -144,10 +144,11 @@
 def merge_kernel(slot_ref, raw0, raw1, raw2, raw3, mine_ref, other_ref, acc0, acc1):
     acc0[...] = jnp.zeros_like(acc0)
     acc1[...] = jnp.zeros_like(acc1)
+    slots = slot_ref[...]
     for pair in (((0, raw0, acc0), (1, raw1, acc1)), ((2, raw2, acc0), (3, raw3, acc1))):
         for k in range(TERMS):
             for source, raw, acc in pair:
-                slot = slot_ref[source * RB + k // NBAND, k % NBAND]
+                slot = slots[source * RB + k // NBAND, k % NBAND]
                 acc[slot] = acc[slot] + raw[k * TR : (k + 1) * TR, :]
     for slot in range(NZ * RB):
         mine_ref[slot * TR : (slot + 1) * TR, :] = acc0[slot] + acc1[slot]
@@ -232,7 +233,7 @@
 )
 
 
-def call(kernel, out_shape, operands, smem, name, far=0, scratch=(), vmem_mib=12):
+def call(kernel, out_shape, operands, smem, name, far=0, scratch=()):
     many = isinstance(out_shape, tuple)
     size = sum(a.size * a.dtype.itemsize for a in operands)
     return pl.pallas_call(
@@ -241,7 +242,7 @@
         in_specs=[SMEM] * smem + [VMEM] * (len(operands) - smem - far) + [FAR] * far,
         out_specs=[VMEM] * len(out_shape) if many else VMEM,
         scratch_shapes=scratch,
-        compiler_params=pltpu.CompilerParams(vmem_limit_bytes=vmem_mib * 1024 * 1024),
+        compiler_params=pltpu.CompilerParams(vmem_limit_bytes=12 * 1024 * 1024),
         cost_estimate=pl.CostEstimate(flops=0, bytes_accessed=size, transcendentals=0),
         name=name,
     )(*operands)
@@ -265,27 +266,27 @@
 
     def deliver(terms, raws, slot):
         raw, own, north, south = terms
+        below, above = ring_lat(north, 1), ring_lat(south, N_LAT - 1)
+        *raws, below, above = lax.optimization_barrier((*raws, below, above))
         dense = struct(NZ * SLAB, BLK)
         acc = pltpu.VMEM((2 * NZ * RB + 1, TR, BLK), F32)
         mine, other = call(
-            merge_kernel, (dense, dense), [slot, raw, *raws], 1, "merge", scratch=[acc, acc]
+            merge_kernel, (dense, dense), [slot, raw, *raws], 0, "merge", scratch=[acc, acc]
         )
         slabs = exchange_z((mine + swap_core(other)).reshape(NZ, SLAB, BLK))
-        return [masks, slabs, own, ring_lat(north, 1), ring_lat(south, N_LAT - 1)]
-
-    int_table = jax.ShapeDtypeStruct((RB, BLK), jnp.int32)
-    masks, sweeps = call(
-        masks_kernel, (struct(RB + 2, BLK), int_table), [column_depth, newton], 2, "masks"
-    )
+        return [masks, slabs, own, below, above]
+
     first_shapes = (struct(TERMS * TR + 2 * RB, BLK),) + TERM_SHAPES[1:]
     terms = call(
         first_kernel,
         first_shapes,
-        [adjoint, impl_dest, impl_local, expl_dest, expl_local, impl_tiles],
+        [
+            pltpu.with_memory_space_constraint(value, pltpu.HBM)
+            for value in (adjoint, impl_dest, impl_local, expl_dest, expl_local, impl_tiles)
+        ],
         0,
         "first",
         far=6,
-        vmem_mib=63,
         scratch=[
             pltpu.VMEM((TR, RB * BLK), F32),
             *[pltpu.VMEM((RB, NBAND), jnp.int32)] * 4,
@@ -294,7 +295,12 @@
             pltpu.SemaphoreType.DMA((RB,)),
         ],
     )
+    int_table = jax.ShapeDtypeStruct((RB, BLK), jnp.int32)
+    masks, sweeps = call(
+        masks_kernel, (struct(RB + 2, BLK), int_table), [column_depth, newton], 2, "masks"
+    )
     raws = gather_x(terms[0])
+    *raws, masks, sweeps = lax.optimization_barrier((*raws, masks, sweeps))
     slot_table = jax.ShapeDtypeStruct((NX * RB, NBAND), jnp.int32)
     slots = call(slots_kernel, (slot_table, slot_table), [terms[0], *raws], 0, "slots")
     for step_index in range(STEPS):

time: 115 us -> 109 us (0.948)
  blocking collectives: 0 us -> 56.7 us
  waiting for transfers between devices: 52 us -> 19.5 us
  starting transfers between devices: 46.6 us -> 24.7 us
  Pallas kernels: 10.2 us -> 7.15 us
  other arithmetic: 2.74 us -> 0.08 us
  local copies, waits for them, and re-layouts: 2.44 us -> 0.03 us
    all_to_all x0 -> x4, blocking collectives: none -> 56.7 us  [exchange_z(): lax.all_to_all(value, 'cols', 0, 0, axis_index_groups=groups, tiled=True)]
    all_to_all x4 -> x0, waiting for transfers between devices: 19.7 us -> none  [exchange_z(): lax.all_to_all(value, 'cols', 0, 0, axis_index_groups=groups, tiled=True)]
    all_to_all x4 -> x0, starting transfers between devices: 18.9 us -> none  [exchange_z(): lax.all_to_all(value, 'cols', 0, 0, axis_index_groups=groups, tiled=True)]
    ppermute x12, waiting for transfers between devices: 14.6 us -> 4.2 us  [shift_x(): return lax.ppermute(value, 'cols', pairs)]
    pallas_call x11, Pallas kernels: 10.2 us -> 7.15 us  [call(): pl.pallas_call(kernel, out_shape=out_shape, in_specs=[SMEM] * smem + [VME...]
    ppermute x12, starting transfers between devices: 19 us -> 16.3 us  [shift_x(): return lax.ppermute(value, 'cols', pairs)]
    add x4, other arithmetic: 2.74 us -> 0.08 us  [deliver(): slabs = exchange_z((mine + swap_core(other)).reshape(NZ, SLAB, BLK))]
    unnamed x26 -> x12, local copies, waits for them, and re-layouts: 2.44 us -> 0.03 us
  transfers between devices with their start and end apart: 28 -> 24, of which waited for: 28 -> 15; matrix products, arithmetic and copies ran while one was open for 0% -> 0% of each run, Pallas kernels for 0% -> 1%
where the time goes in v3:
time: 109 us; the launch traced here: 108 us
  blocking collectives  56.7 us (52%)
  starting transfers between devices  24.7 us (23%)
  waiting for transfers between devices  19.5 us (18%)
  Pallas kernels  7.15 us (7%)
    all_to_all x4, blocking collectives, exchange_z(): lax.all_to_all(value, 'cols', 0, 0, axis_index_groups=groups, tiled=True)  56.7 us
    ppermute x12, starting transfers between devices, shift_x(): return lax.ppermute(value, 'cols', pairs)  16.3 us
    ppermute x8, waiting for transfers between devices, ring_lat(): lax.ppermute(value, 'lat', [(i, (i + steps) % N_LAT) for i in range(N_LAT)])  9.75 us
    ppermute x8, starting transfers between devices, ring_lat(): lax.ppermute(value, 'lat', [(i, (i + steps) % N_LAT) for i in range(N_LAT)])  8.1 us
    pallas_call x11, Pallas kernels, call(): pl.pallas_call(kernel, out_shape=out_shape, in_specs=[SMEM] * smem + [VME...  7.15 us
    ppermute x4, waiting for transfers between devices, swap_core(): lax.ppermute(value, 'cols', [(i, i ^ 1) for i in range(NX * NZ * NCORE)])  5.53 us
    ppermute x12, waiting for transfers between devices, shift_x(): return lax.ppermute(value, 'cols', pairs)  4.2 us
  transfers between devices with their start and end apart: 24, of which 15 were waited for; matrix products, arithmetic and copies ran while one was open for 0% of the time, Pallas kernels for 1%

profile of v3, /device:TPU:24, one launch (start us, length us, event | category | flops | bytes accessed | tf_op | source)
XLA Modules:
  0.0 108.3 jit_solution(13752133493740108523)
XLA Ops:
  0.0 2.0 %first.1 = (f32[168,128]{1,0:T(8,128)S(1)}, f32[40,128]{1,0:T(8,128)S(1)}, f32[40,128]{1,0:T(8,128)S(1)}, f32[40,128]{1,0:T(8,128)S(1)}) custom-call(f32[10,512]{1,0:T(8,128)} %field_far.1, s32[4,4]{1,0:T(4,128)} %impl_dest_far.1, s32[4,4]{1,0:T(4,128)} %impl_local_far.1, s32[4,4]{1,0:T(4,128)} %expl_dest_far.1, s32[4,4]{1,0:T(4,128)} %expl_local_far.1, ...), custom_call_target="tpu_custom_call" | custom-call | bytes 938240 | tf_op jit(solution)/shard_map/first/pallas_call | solution.py:239
  2.0 0.0 copy-start
  2.0 2.8 %collective-permute-start.2 = (f32[168,128]{1,0:T(8,128)S(1)}, f32[168,128]{1,0:T(8,128)S(1)}, u32[]{:S(2)}, u32[]{:S(2)}) collective-permute-start(f32[168,128]{1,0:T(8,128)S(1)} %get-tuple-element.58.raw0), channel_id=1, source_target_pairs={{0,192},{4,196},{8,200},{12,204},{16,208},{20,212},{24,216},{28,22... | collective-permute-start | bytes 258056 | tf_op jit(solution)/shard_map/ppermute | solution.py:48
  4.8 0.8 collective-permute-start.1
  5.6 0.9 collective-permute-start
  6.5 0.2 collective-permute-start.3
  6.8 1.8 %collective-permute-start.4 = (f32[40,128]{1,0:T(8,128)S(1)}, f32[40,128]{1,0:T(8,128)S(1)}, u32[]{:S(2)}, u32[]{:S(2)}) collective-permute-start(f32[40,128]{1,0:T(8,128)S(1)} %get-tuple-element.68), channel_id=1, source_target_pairs={{0,3},{1,0},{2,1},{3,2},{4,7},{5,4},{6,5},{7,6},{8,11},{9,8},{10,9... | collective-permute-start | bytes 61448 | tf_op jit(solution)/shard_map/ppermute | solution.py:56
  8.6 0.6 masks.1
  9.1 0.0 collective-permute-done.2.raw3
  9.1 2.2 %collective-permute-done.1.raw2 = f32[168,128]{1,0:T(8,128)S(1)} collective-permute-done((f32[168,128]{1,0:T(8,128)S(1)}, f32[168,128]{1,0:T(8,128)S(1)}, u32[]{:S(2)}, u32[]{:S(2)}) %collective-permute-start.1) | collective-permute-done | bytes 86048 | tf_op jit(solution)/shard_map/ppermute | solution.py:48
  11.3 0.9 collective-permute-done.raw1
  12.2 0.0 collective-permute-done.3.below_ref
  12.2 0.0 collective-permute-done.4.above_ref
  12.2 0.3 merge.4
  12.6 0.1 collective-permute-start.5
  12.7 1.4 %collective-permute-done.5 = f32[320,128]{1,0:T(8,128)S(1)} collective-permute-done((f32[320,128]{1,0:T(8,128)S(1)}, f32[320,128]{1,0:T(8,128)S(1)}, u32[]{:S(2)}, u32[]{:S(2)}) %collective-permute-start.5) | collective-permute-done | bytes 163872 | tf_op jit(solution)/shard_map/ppermute | solution.py:52
  14.1 0.0 copy-start.3
  14.1 18.5 %all_to_all.20.slabs_ref = f32[8,40,128]{2,1,0:T(8,128)S(1)} all-to-all(f32[8,40,128]{2,1,0:T(8,128)S(1)} %bitcast.4), channel_id=1, replica_groups={{0,8,16,24,32,40,48,56},{4,12,20,28,36,44,52,60},{64,72,80,88,96,104,11..., dimensions={0} | all-to-all | bytes 327680 | tf_op jit(solution)/shard_map/all_to_all | solution.py:61
  32.6 1.1 react.2
  33.7 1.9 %collective-permute-start.8 = (f32[160,128]{1,0:T(8,128)S(1)}, f32[160,128]{1,0:T(8,128)S(1)}, u32[]{:S(2)}, u32[]{:S(2)}) collective-permute-start(f32[160,128]{1,0:T(8,128)S(1)} %get-tuple-element.78.raw0), channel_id=1, source_target_pairs={{0,192},{4,196},{8,200},{12,204},{16,208},{20,212},{24,216},{28,22... | collective-permute-start | bytes 245768 | tf_op jit(solution)/shard_map/ppermute | solution.py:48
  35.6 1.5 %collective-permute-start.7 = (f32[160,128]{1,0:T(8,128)S(1)}, f32[160,128]{1,0:T(8,128)S(1)}, u32[]{:S(2)}, u32[]{:S(2)}) collective-permute-start(f32[160,128]{1,0:T(8,128)S(1)} %get-tuple-element.78.raw0), channel_id=1, source_target_pairs={{0,128},{4,132},{8,136},{12,140},{16,144},{20,148},{24,152},{28,15... | collective-permute-start | bytes 245768 | tf_op jit(solution)/shard_map/ppermute | solution.py:48
  37.1 0.0 collective-permute-start.6
  37.1 0.4 collective-permute-start.9
  37.5 1.6 %collective-permute-start.10 = (f32[40,128]{1,0:T(8,128)S(1)}, f32[40,128]{1,0:T(8,128)S(1)}, u32[]{:S(2)}, u32[]{:S(2)}) collective-permute-start(f32[40,128]{1,0:T(8,128)S(1)} %get-tuple-element.80), channel_id=1, source_target_pairs={{0,3},{1,0},{2,1},{3,2},{4,7},{5,4},{6,5},{7,6},{8,11},{9,8},{10,9... | collective-permute-start | bytes 61448 | tf_op jit(solution)/shard_map/ppermute | solution.py:56
  39.1 1.8 %collective-permute-done.9.below_ref = f32[40,128]{1,0:T(8,128)S(1)} collective-permute-done((f32[40,128]{1,0:T(8,128)S(1)}, f32[40,128]{1,0:T(8,128)S(1)}, u32[]{:S(2)}, u32[]{:S(2)}) %collective-permute-start.9) | collective-permute-done | bytes 20512 | tf_op jit(solution)/shard_map/ppermute | solution.py:56
  40.9 1.6 %collective-permute-done.10.above_ref = f32[40,128]{1,0:T(8,128)S(1)} collective-permute-done((f32[40,128]{1,0:T(8,128)S(1)}, f32[40,128]{1,0:T(8,128)S(1)}, u32[]{:S(2)}, u32[]{:S(2)}) %collective-permute-start.10) | collective-permute-done | bytes 20512 | tf_op jit(solution)/shard_map/ppermute | solution.py:56
  42.5 0.0 collective-permute-done.8.raw3
  42.5 0.0 collective-permute-done.7.raw2
  42.5 0.3 collective-permute-done.6.raw1
  42.8 0.4 merge.5
  43.1 0.1 collective-permute-start.11
  43.2 1.4 %collective-permute-done.11 = f32[320,128]{1,0:T(8,128)S(1)} collective-permute-done((f32[320,128]{1,0:T(8,128)S(1)}, f32[320,128]{1,0:T(8,128)S(1)}, u32[]{:S(2)}, u32[]{:S(2)}) %collective-permute-start.11) | collective-permute-done | bytes 163872 | tf_op jit(solution)/shard_map/ppermute | solution.py:52
  44.6 12.7 %all_to_all.21.slabs_ref = f32[8,40,128]{2,1,0:T(8,128)S(1)} all-to-all(f32[8,40,128]{2,1,0:T(8,128)S(1)} %bitcast.5), channel_id=1, replica_groups={{0,8,16,24,32,40,48,56},{4,12,20,28,36,44,52,60},{64,72,80,88,96,104,11..., dimensions={0} | all-to-all | bytes 327680 | tf_op jit(solution)/shard_map/all_to_all | solution.py:61
  57.4 0.3 step.1
  57.7 3.0 %collective-permute-start.14 = (f32[160,128]{1,0:T(8,128)S(1)}, f32[160,128]{1,0:T(8,128)S(1)}, u32[]{:S(2)}, u32[]{:S(2)}) collective-permute-start(f32[160,128]{1,0:T(8,128)S(1)} %get-tuple-element.89.raw0), channel_id=1, source_target_pairs={{0,192},{4,196},{8,200},{12,204},{16,208},{20,212},{24,216},{28,22... | collective-permute-start | bytes 245768 | tf_op jit(solution)/shard_map/ppermute | solution.py:48
  60.7 0.8 collective-permute-start.13
  61.5 0.3 collective-permute-start.12
  61.9 0.4 collective-permute-start.15
  62.2 1.7 %collective-permute-start.16 = (f32[40,128]{1,0:T(8,128)S(1)}, f32[40,128]{1,0:T(8,128)S(1)}, u32[]{:S(2)}, u32[]{:S(2)}) collective-permute-start(f32[40,128]{1,0:T(8,128)S(1)} %get-tuple-element.91), channel_id=1, source_target_pairs={{0,3},{1,0},{2,1},{3,2},{4,7},{5,4},{6,5},{7,6},{8,11},{9,8},{10,9... | collective-permute-start | bytes 61448 | tf_op jit(solution)/shard_map/ppermute | solution.py:56
  63.9 1.8 %collective-permute-done.15.below_ref = f32[40,128]{1,0:T(8,128)S(1)} collective-permute-done((f32[40,128]{1,0:T(8,128)S(1)}, f32[40,128]{1,0:T(8,128)S(1)}, u32[]{:S(2)}, u32[]{:S(2)}) %collective-permute-start.15) | collective-permute-done | bytes 20512 | tf_op jit(solution)/shard_map/ppermute | solution.py:56
  65.6 1.6 %collective-permute-done.16.above_ref = f32[40,128]{1,0:T(8,128)S(1)} collective-permute-done((f32[40,128]{1,0:T(8,128)S(1)}, f32[40,128]{1,0:T(8,128)S(1)}, u32[]{:S(2)}, u32[]{:S(2)}) %collective-permute-start.16) | collective-permute-done | bytes 20512 | tf_op jit(solution)/shard_map/ppermute | solution.py:56
  67.2 0.0 collective-permute-done.14.raw3
  67.2 0.0 collective-permute-done.13.raw2
  67.2 0.3 collective-permute-done.12.raw1
  67.5 0.3 merge.6
  67.9 0.1 collective-permute-start.17
  68.0 1.4 %collective-permute-done.17 = f32[320,128]{1,0:T(8,128)S(1)} collective-permute-done((f32[320,128]{1,0:T(8,128)S(1)}, f32[320,128]{1,0:T(8,128)S(1)}, u32[]{:S(2)}, u32[]{:S(2)}) %collective-permute-start.17) | collective-permute-done | bytes 163872 | tf_op jit(solution)/shard_map/ppermute | solution.py:52
  69.4 12.7 %all_to_all.22.slabs_ref = f32[8,40,128]{2,1,0:T(8,128)S(1)} all-to-all(f32[8,40,128]{2,1,0:T(8,128)S(1)} %bitcast.6), channel_id=1, replica_groups={{0,8,16,24,32,40,48,56},{4,12,20,28,36,44,52,60},{64,72,80,88,96,104,11..., dimensions={0} | all-to-all | bytes 327680 | tf_op jit(solution)/shard_map/all_to_all | solution.py:61
  82.1 1.1 react.3
  83.2 2.7 %collective-permute-start.20 = (f32[160,128]{1,0:T(8,128)S(1)}, f32[160,128]{1,0:T(8,128)S(1)}, u32[]{:S(2)}, u32[]{:S(2)}) collective-permute-start(f32[160,128]{1,0:T(8,128)S(1)} %get-tuple-element.100.raw0), channel_id=1, source_target_pairs={{0,192},{4,196},{8,200},{12,204},{16,208},{20,212},{24,216},{28,22... | collective-permute-start | bytes 245768 | tf_op jit(solution)/shard_map/ppermute | solution.py:48
  85.9 1.5 %collective-permute-start.19 = (f32[160,128]{1,0:T(8,128)S(1)}, f32[160,128]{1,0:T(8,128)S(1)}, u32[]{:S(2)}, u32[]{:S(2)}) collective-permute-start(f32[160,128]{1,0:T(8,128)S(1)} %get-tuple-element.100.raw0), channel_id=1, source_target_pairs={{0,128},{4,132},{8,136},{12,140},{16,144},{20,148},{24,152},{28,15... | collective-permute-start | bytes 245768 | tf_op jit(solution)/shard_map/ppermute | solution.py:48
  87.4 0.0 collective-permute-start.18
  87.4 0.1 collective-permute-start.21
  87.5 1.9 %collective-permute-start.22 = (f32[40,128]{1,0:T(8,128)S(1)}, f32[40,128]{1,0:T(8,128)S(1)}, u32[]{:S(2)}, u32[]{:S(2)}) collective-permute-start(f32[40,128]{1,0:T(8,128)S(1)} %get-tuple-element.102), channel_id=1, source_target_pairs={{0,3},{1,0},{2,1},{3,2},{4,7},{5,4},{6,5},{7,6},{8,11},{9,8},{10,9... | collective-permute-start | bytes 61448 | tf_op jit(solution)/shard_map/ppermute | solution.py:56
  89.4 1.8 %collective-permute-done.21.below_ref = f32[40,128]{1,0:T(8,128)S(1)} collective-permute-done((f32[40,128]{1,0:T(8,128)S(1)}, f32[40,128]{1,0:T(8,128)S(1)}, u32[]{:S(2)}, u32[]{:S(2)}) %collective-permute-start.21) | collective-permute-done | bytes 20512 | tf_op jit(solution)/shard_map/ppermute | solution.py:56
  91.2 1.3 %collective-permute-done.22.above_ref = f32[40,128]{1,0:T(8,128)S(1)} collective-permute-done((f32[40,128]{1,0:T(8,128)S(1)}, f32[40,128]{1,0:T(8,128)S(1)}, u32[]{:S(2)}, u32[]{:S(2)}) %collective-permute-start.22) | collective-permute-done | bytes 20512 | tf_op jit(solution)/shard_map/ppermute | solution.py:56
  92.5 0.0 collective-permute-done.20.raw3
  92.5 0.0 collective-permute-done.19.raw2
  92.5 0.6 collective-permute-done.18.raw1
  93.0 0.4 merge.7
  93.4 0.1 collective-permute-start.23
  93.5 1.4 %collective-permute-done.23 = f32[320,128]{1,0:T(8,128)S(1)} collective-permute-done((f32[320,128]{1,0:T(8,128)S(1)}, f32[320,128]{1,0:T(8,128)S(1)}, u32[]{:S(2)}, u32[]{:S(2)}) %collective-permute-start.23) | collective-permute-done | bytes 163872 | tf_op jit(solution)/shard_map/ppermute | solution.py:52
  94.9 12.7 %all_to_all.23.slabs_ref = f32[8,40,128]{2,1,0:T(8,128)S(1)} all-to-all(f32[8,40,128]{2,1,0:T(8,128)S(1)} %bitcast.7), channel_id=1, replica_groups={{0,8,16,24,32,40,48,56},{4,12,20,28,36,44,52,60},{64,72,80,88,96,104,11..., dimensions={0} | all-to-all | bytes 327680 | tf_op jit(solution)/shard_map/all_to_all | solution.py:61
  107.7 0.6 last.1
  (15 shorter events, 0.1 us)
Async XLA Ops:
  0.0 8.6 %copy-start.4 = (s32[8]{0:T(128)S(1)}, s32[8]{0:T(128)}, u32[]{:S(2)}) copy-start(s32[8]{0:T(128)} %depth_ref.1) | copy-start | bytes 100
  0.0 8.6 %copy-start.5 = (s32[8]{0:T(128)S(1)}, s32[8]{0:T(128)}, u32[]{:S(2)}) copy-start(s32[8]{0:T(128)} %newton_ref.1) | copy-start | bytes 100
  0.0 32.6 %copy-start.2 = (bf16[4,7,128,128]{3,2,1,0:T(8,128)(2,1)S(1)}, bf16[4,7,128,128]{3,2,1,0:T(8,128)(2,1)}, u32[]{:S(2)}) copy-start(bf16[4,7,128,128]{3,2,1,0:T(8,128)(2,1)} %tiles_ref.5) | copy-start | bytes 2752516
  2.0 30.6 %copy-start = (bf16[30,30,512]{2,1,0:T(8,128)(2,1)S(1)}, bf16[30,30,512]{2,1,0:T(8,128)(2,1)}, u32[]{:S(2)}) copy-start(bf16[30,30,512]{2,1,0:T(8,128)(2,1)} %inv_ref.3) | copy-start | bytes 2764804
  2.0 7.1 %collective-permute-start.2 = (f32[168,128]{1,0:T(8,128)S(1)}, f32[168,128]{1,0:T(8,128)S(1)}, u32[]{:S(2)}, u32[]{:S(2)}) collective-permute-start(f32[168,128]{1,0:T(8,128)S(1)} %get-tuple-element.58.raw0), channel_id=1, source_target_pairs={{0,192},{4,196},{8,200},{12,204},{16,208},{20,212},{24,216},{28,22... | collective-permute-start | bytes 258056 | tf_op jit(solution)/shard_map/ppermute | solution.py:48
  4.8 6.5 %collective-permute-start.1 = (f32[168,128]{1,0:T(8,128)S(1)}, f32[168,128]{1,0:T(8,128)S(1)}, u32[]{:S(2)}, u32[]{:S(2)}) collective-permute-start(f32[168,128]{1,0:T(8,128)S(1)} %get-tuple-element.58.raw0), channel_id=1, source_target_pairs={{0,128},{4,132},{8,136},{12,140},{16,144},{20,148},{24,152},{28,15... | collective-permute-start | bytes 258056 | tf_op jit(solution)/shard_map/ppermute | solution.py:48
  5.6 6.5 %collective-permute-start = (f32[168,128]{1,0:T(8,128)S(1)}, f32[168,128]{1,0:T(8,128)S(1)}, u32[]{:S(2)}, u32[]{:S(2)}) collective-permute-start(f32[168,128]{1,0:T(8,128)S(1)} %get-tuple-element.58.raw0), channel_id=1, source_target_pairs={{0,64},{4,68},{8,72},{12,76},{16,80},{20,84},{24,88},{28,92},{32,9... | collective-permute-start | bytes 258056 | tf_op jit(solution)/shard_map/ppermute | solution.py:48
  6.5 5.7 %collective-permute-start.3 = (f32[40,128]{1,0:T(8,128)S(1)}, f32[40,128]{1,0:T(8,128)S(1)}, u32[]{:S(2)}, u32[]{:S(2)}) collective-permute-start(f32[40,128]{1,0:T(8,128)S(1)} %get-tuple-element.67), channel_id=1, source_target_pairs={{0,1},{1,2},{2,3},{3,0},{4,5},{5,6},{6,7},{7,4},{8,9},{9,10},{10,1... | collective-permute-start | bytes 61448 | tf_op jit(solution)/shard_map/ppermute | solution.py:56
  6.8 5.5 %collective-permute-start.4 = (f32[40,128]{1,0:T(8,128)S(1)}, f32[40,128]{1,0:T(8,128)S(1)}, u32[]{:S(2)}, u32[]{:S(2)}) collective-permute-start(f32[40,128]{1,0:T(8,128)S(1)} %get-tuple-element.68), channel_id=1, source_target_pairs={{0,3},{1,0},{2,1},{3,2},{4,7},{5,4},{6,5},{7,6},{8,11},{9,8},{10,9... | collective-permute-start | bytes 61448 | tf_op jit(solution)/shard_map/ppermute | solution.py:56
  12.6 1.5 %collective-permute-start.5 = (f32[320,128]{1,0:T(8,128)S(1)}, f32[320,128]{1,0:T(8,128)S(1)}, u32[]{:S(2)}, u32[]{:S(2)}) collective-permute-start(f32[320,128]{1,0:T(8,128)S(1)} %get-tuple-element.73), channel_id=1, source_target_pairs={{0,4},{4,0},{8,12},{12,8},{16,20},{20,16},{24,28},{28,24},{32,36},... | collective-permute-start | bytes 491528 | tf_op jit(solution)/shard_map/ppermute | solution.py:52
  14.1 18.5 %copy-start.3 = (bf16[10,10,512]{2,1,0:T(8,128)(2,1)S(1)}, bf16[10,10,512]{2,1,0:T(8,128)(2,1)}, u32[]{:S(2)}) copy-start(bf16[10,10,512]{2,1,0:T(8,128)(2,1)} %jac_ref.3) | copy-start | bytes 307204
  33.7 23.7 %copy-start.1 = (bf16[4,7,128,128]{3,2,1,0:T(8,128)(2,1)S(1)}, bf16[4,7,128,128]{3,2,1,0:T(8,128)(2,1)}, u32[]{:S(2)}) copy-start(bf16[4,7,128,128]{3,2,1,0:T(8,128)(2,1)} %tiles_ref.4) | copy-start | bytes 2752516
  33.7 8.8 %collective-permute-start.8 = (f32[160,128]{1,0:T(8,128)S(1)}, f32[160,128]{1,0:T(8,128)S(1)}, u32[]{:S(2)}, u32[]{:S(2)}) collective-permute-start(f32[160,128]{1,0:T(8,128)S(1)} %get-tuple-element.78.raw0), channel_id=1, source_target_pairs={{0,192},{4,196},{8,200},{12,204},{16,208},{20,212},{24,216},{28,22... | collective-permute-start | bytes 245768 | tf_op jit(solution)/shard_map/ppermute | solution.py:48
  35.6 6.9 %collective-permute-start.7 = (f32[160,128]{1,0:T(8,128)S(1)}, f32[160,128]{1,0:T(8,128)S(1)}, u32[]{:S(2)}, u32[]{:S(2)}) collective-permute-start(f32[160,128]{1,0:T(8,128)S(1)} %get-tuple-element.78.raw0), channel_id=1, source_target_pairs={{0,128},{4,132},{8,136},{12,140},{16,144},{20,148},{24,152},{28,15... | collective-permute-start | bytes 245768 | tf_op jit(solution)/shard_map/ppermute | solution.py:48
  37.1 5.7 %collective-permute-start.6 = (f32[160,128]{1,0:T(8,128)S(1)}, f32[160,128]{1,0:T(8,128)S(1)}, u32[]{:S(2)}, u32[]{:S(2)}) collective-permute-start(f32[160,128]{1,0:T(8,128)S(1)} %get-tuple-element.78.raw0), channel_id=1, source_target_pairs={{0,64},{4,68},{8,72},{12,76},{16,80},{20,84},{24,88},{28,92},{32,9... | collective-permute-start | bytes 245768 | tf_op jit(solution)/shard_map/ppermute | solution.py:48
  37.1 3.8 %collective-permute-start.9 = (f32[40,128]{1,0:T(8,128)S(1)}, f32[40,128]{1,0:T(8,128)S(1)}, u32[]{:S(2)}, u32[]{:S(2)}) collective-permute-start(f32[40,128]{1,0:T(8,128)S(1)} %get-tuple-element.79), channel_id=1, source_target_pairs={{0,1},{1,2},{2,3},{3,0},{4,5},{5,6},{6,7},{7,4},{8,9},{9,10},{10,1... | collective-permute-start | bytes 61448 | tf_op jit(solution)/shard_map/ppermute | solution.py:56
  37.5 5.0 %collective-permute-start.10 = (f32[40,128]{1,0:T(8,128)S(1)}, f32[40,128]{1,0:T(8,128)S(1)}, u32[]{:S(2)}, u32[]{:S(2)}) collective-permute-start(f32[40,128]{1,0:T(8,128)S(1)} %get-tuple-element.80), channel_id=1, source_target_pairs={{0,3},{1,0},{2,1},{3,2},{4,7},{5,4},{6,5},{7,6},{8,11},{9,8},{10,9... | collective-permute-start | bytes 61448 | tf_op jit(solution)/shard_map/ppermute | solution.py:56
  43.1 1.5 %collective-permute-start.11 = (f32[320,128]{1,0:T(8,128)S(1)}, f32[320,128]{1,0:T(8,128)S(1)}, u32[]{:S(2)}, u32[]{:S(2)}) collective-permute-start(f32[320,128]{1,0:T(8,128)S(1)} %get-tuple-element.85), channel_id=1, source_target_pairs={{0,4},{4,0},{8,12},{12,8},{16,20},{20,16},{24,28},{28,24},{32,36},... | collective-permute-start | bytes 491528 | tf_op jit(solution)/shard_map/ppermute | solution.py:52
  57.7 9.5 %collective-permute-start.14 = (f32[160,128]{1,0:T(8,128)S(1)}, f32[160,128]{1,0:T(8,128)S(1)}, u32[]{:S(2)}, u32[]{:S(2)}) collective-permute-start(f32[160,128]{1,0:T(8,128)S(1)} %get-tuple-element.89.raw0), channel_id=1, source_target_pairs={{0,192},{4,196},{8,200},{12,204},{16,208},{20,212},{24,216},{28,22... | collective-permute-start | bytes 245768 | tf_op jit(solution)/shard_map/ppermute | solution.py:48
  60.7 6.5 %collective-permute-start.13 = (f32[160,128]{1,0:T(8,128)S(1)}, f32[160,128]{1,0:T(8,128)S(1)}, u32[]{:S(2)}, u32[]{:S(2)}) collective-permute-start(f32[160,128]{1,0:T(8,128)S(1)} %get-tuple-element.89.raw0), channel_id=1, source_target_pairs={{0,128},{4,132},{8,136},{12,140},{16,144},{20,148},{24,152},{28,15... | collective-permute-start | bytes 245768 | tf_op jit(solution)/shard_map/ppermute | solution.py:48
  61.5 6.0 %collective-permute-start.12 = (f32[160,128]{1,0:T(8,128)S(1)}, f32[160,128]{1,0:T(8,128)S(1)}, u32[]{:S(2)}, u32[]{:S(2)}) collective-permute-start(f32[160,128]{1,0:T(8,128)S(1)} %get-tuple-element.89.raw0), channel_id=1, source_target_pairs={{0,64},{4,68},{8,72},{12,76},{16,80},{20,84},{24,88},{28,92},{32,9... | collective-permute-start | bytes 245768 | tf_op jit(solution)/shard_map/ppermute | solution.py:48
  61.9 3.8 %collective-permute-start.15 = (f32[40,128]{1,0:T(8,128)S(1)}, f32[40,128]{1,0:T(8,128)S(1)}, u32[]{:S(2)}, u32[]{:S(2)}) collective-permute-start(f32[40,128]{1,0:T(8,128)S(1)} %get-tuple-element.90), channel_id=1, source_target_pairs={{0,1},{1,2},{2,3},{3,0},{4,5},{5,6},{6,7},{7,4},{8,9},{9,10},{10,1... | collective-permute-start | bytes 61448 | tf_op jit(solution)/shard_map/ppermute | solution.py:56
  62.2 5.0 %collective-permute-start.16 = (f32[40,128]{1,0:T(8,128)S(1)}, f32[40,128]{1,0:T(8,128)S(1)}, u32[]{:S(2)}, u32[]{:S(2)}) collective-permute-start(f32[40,128]{1,0:T(8,128)S(1)} %get-tuple-element.91), channel_id=1, source_target_pairs={{0,3},{1,0},{2,1},{3,2},{4,7},{5,4},{6,5},{7,6},{8,11},{9,8},{10,9... | collective-permute-start | bytes 61448 | tf_op jit(solution)/shard_map/ppermute | solution.py:56
  67.9 1.5 %collective-permute-start.17 = (f32[320,128]{1,0:T(8,128)S(1)}, f32[320,128]{1,0:T(8,128)S(1)}, u32[]{:S(2)}, u32[]{:S(2)}) collective-permute-start(f32[320,128]{1,0:T(8,128)S(1)} %get-tuple-element.96), channel_id=1, source_target_pairs={{0,4},{4,0},{8,12},{12,8},{16,20},{20,16},{24,28},{28,24},{32,36},... | collective-permute-start | bytes 491528 | tf_op jit(solution)/shard_map/ppermute | solution.py:52
  83.2 9.3 %collective-permute-start.20 = (f32[160,128]{1,0:T(8,128)S(1)}, f32[160,128]{1,0:T(8,128)S(1)}, u32[]{:S(2)}, u32[]{:S(2)}) collective-permute-start(f32[160,128]{1,0:T(8,128)S(1)} %get-tuple-element.100.raw0), channel_id=1, source_target_pairs={{0,192},{4,196},{8,200},{12,204},{16,208},{20,212},{24,216},{28,22... | collective-permute-start | bytes 245768 | tf_op jit(solution)/shard_map/ppermute | solution.py:48
  85.9 6.6 %collective-permute-start.19 = (f32[160,128]{1,0:T(8,128)S(1)}, f32[160,128]{1,0:T(8,128)S(1)}, u32[]{:S(2)}, u32[]{:S(2)}) collective-permute-start(f32[160,128]{1,0:T(8,128)S(1)} %get-tuple-element.100.raw0), channel_id=1, source_target_pairs={{0,128},{4,132},{8,136},{12,140},{16,144},{20,148},{24,152},{28,15... | collective-permute-start | bytes 245768 | tf_op jit(solution)/shard_map/ppermute | solution.py:48
  87.4 5.7 %collective-permute-start.18 = (f32[160,128]{1,0:T(8,128)S(1)}, f32[160,128]{1,0:T(8,128)S(1)}, u32[]{:S(2)}, u32[]{:S(2)}) collective-permute-start(f32[160,128]{1,0:T(8,128)S(1)} %get-tuple-element.100.raw0), channel_id=1, source_target_pairs={{0,64},{4,68},{8,72},{12,76},{16,80},{20,84},{24,88},{28,92},{32,9... | collective-permute-start | bytes 245768 | tf_op jit(solution)/shard_map/ppermute | solution.py:48
  87.4 3.8 %collective-permute-start.21 = (f32[40,128]{1,0:T(8,128)S(1)}, f32[40,128]{1,0:T(8,128)S(1)}, u32[]{:S(2)}, u32[]{:S(2)}) collective-permute-start(f32[40,128]{1,0:T(8,128)S(1)} %get-tuple-element.101), channel_id=1, source_target_pairs={{0,1},{1,2},{2,3},{3,0},{4,5},{5,6},{6,7},{7,4},{8,9},{9,10},{10,1... | collective-permute-start | bytes 61448 | tf_op jit(solution)/shard_map/ppermute | solution.py:56
  87.5 5.0 %collective-permute-start.22 = (f32[40,128]{1,0:T(8,128)S(1)}, f32[40,128]{1,0:T(8,128)S(1)}, u32[]{:S(2)}, u32[]{:S(2)}) collective-permute-start(f32[40,128]{1,0:T(8,128)S(1)} %get-tuple-element.102), channel_id=1, source_target_pairs={{0,3},{1,0},{2,1},{3,2},{4,7},{5,4},{6,5},{7,6},{8,11},{9,8},{10,9... | collective-permute-start | bytes 61448 | tf_op jit(solution)/shard_map/ppermute | solution.py:56
  93.4 1.5 %collective-permute-start.23 = (f32[320,128]{1,0:T(8,128)S(1)}, f32[320,128]{1,0:T(8,128)S(1)}, u32[]{:S(2)}, u32[]{:S(2)}) collective-permute-start(f32[320,128]{1,0:T(8,128)S(1)} %get-tuple-element.107), channel_id=1, source_target_pairs={{0,4},{4,0},{8,12},{12,8},{16,20},{20,16},{24,28},{28,24},{32,36},... | collective-permute-start | bytes 491528 | tf_op jit(solution)/shard_map/ppermute | solution.py:52

commit v4 on v3

--- a/solution.py
+++ b/solution.py
@@ -267,12 +267,12 @@
     def deliver(terms, raws, slot):
         raw, own, north, south = terms
         below, above = ring_lat(north, 1), ring_lat(south, N_LAT - 1)
-        *raws, below, above = lax.optimization_barrier((*raws, below, above))
         dense = struct(NZ * SLAB, BLK)
         acc = pltpu.VMEM((2 * NZ * RB + 1, TR, BLK), F32)
         mine, other = call(
             merge_kernel, (dense, dense), [slot, raw, *raws], 0, "merge", scratch=[acc, acc]
         )
+        other, below, above = lax.optimization_barrier((other, below, above))
         slabs = exchange_z((mine + swap_core(other)).reshape(NZ, SLAB, BLK))
         return [masks, slabs, own, below, above]
 

time: 109 us -> 107 us (0.982)
  starting transfers between devices: 24.7 us -> 23.5 us
    ppermute x8, waiting for transfers between devices: 9.75 us -> 0.02 us  [ring_lat(): lax.ppermute(value, 'lat', [(i, (i + steps) % N_LAT) for i in range(N_LAT)])]
    ppermute x12, waiting for transfers between devices: 4.2 us -> 13.8 us  [shift_x(): return lax.ppermute(value, 'cols', pairs)]
    ppermute x12, starting transfers between devices: 16.3 us -> 15 us  [shift_x(): return lax.ppermute(value, 'cols', pairs)]
  transfers between devices with their start and end apart: 24 -> 24, of which waited for: 15 -> 12; matrix products, arithmetic and copies ran while one was open for 0% -> 0% of each run, Pallas kernels for 1% -> 2%
where the time goes in v4:
time: 107 us
  blocking collectives  56.7 us (53%)
  starting transfers between devices  23.5 us (22%)
  waiting for transfers between devices  19.3 us (18%)
  Pallas kernels  7.14 us (7%)
    all_to_all x4, blocking collectives, exchange_z(): lax.all_to_all(value, 'cols', 0, 0, axis_index_groups=groups, tiled=True)  56.7 us
    ppermute x12, starting transfers between devices, shift_x(): return lax.ppermute(value, 'cols', pairs)  15 us
    ppermute x12, waiting for transfers between devices, shift_x(): return lax.ppermute(value, 'cols', pairs)  13.8 us
    ppermute x8, starting transfers between devices, ring_lat(): lax.ppermute(value, 'lat', [(i, (i + steps) % N_LAT) for i in range(N_LAT)])  8.1 us
    pallas_call x11, Pallas kernels, call(): pl.pallas_call(kernel, out_shape=out_shape, in_specs=[SMEM] * smem + [VME...  7.14 us
    ppermute x4, waiting for transfers between devices, swap_core(): lax.ppermute(value, 'cols', [(i, i ^ 1) for i in range(NX * NZ * NCORE)])  5.53 us
  transfers between devices with their start and end apart: 24, of which 12 were waited for; matrix products, arithmetic and copies ran while one was open for 0% of the time, Pallas kernels for 2%

profile of v4, /device:TPU:24, one launch (start us, length us, event | category | flops | bytes accessed | tf_op | source)
XLA Modules:
  0.0 107.0 jit_solution(6927112158171854280)
XLA Ops:
  0.0 2.0 %first.1 = (f32[168,128]{1,0:T(8,128)S(1)}, f32[40,128]{1,0:T(8,128)S(1)}, f32[40,128]{1,0:T(8,128)S(1)}, f32[40,128]{1,0:T(8,128)S(1)}) custom-call(f32[10,512]{1,0:T(8,128)} %field_far.1, s32[4,4]{1,0:T(4,128)} %impl_dest_far.1, s32[4,4]{1,0:T(4,128)} %impl_local_far.1, s32[4,4]{1,0:T(4,128)} %expl_dest_far.1, s32[4,4]{1,0:T(4,128)} %expl_local_far.1, ...), custom_call_target="tpu_custom_call" | custom-call | bytes 938240 | tf_op jit(solution)/shard_map/first/pallas_call | solution.py:239
  2.0 0.0 copy-start
  2.0 2.8 %collective-permute-start.2 = (f32[168,128]{1,0:T(8,128)S(1)}, f32[168,128]{1,0:T(8,128)S(1)}, u32[]{:S(2)}, u32[]{:S(2)}) collective-permute-start(f32[168,128]{1,0:T(8,128)S(1)} %get-tuple-element.50.raw0), channel_id=1, source_target_pairs={{0,192},{4,196},{8,200},{12,204},{16,208},{20,212},{24,216},{28,22... | collective-permute-start | bytes 258056 | tf_op jit(solution)/shard_map/ppermute | solution.py:48
  4.8 0.8 collective-permute-start.1
  5.6 0.9 collective-permute-start
  6.5 0.2 collective-permute-start.3
  6.8 1.8 %collective-permute-start.4 = (f32[40,128]{1,0:T(8,128)S(1)}, f32[40,128]{1,0:T(8,128)S(1)}, u32[]{:S(2)}, u32[]{:S(2)}) collective-permute-start(f32[40,128]{1,0:T(8,128)S(1)} %get-tuple-element.62), channel_id=1, source_target_pairs={{0,3},{1,0},{2,1},{3,2},{4,7},{5,4},{6,5},{7,6},{8,11},{9,8},{10,9... | collective-permute-start | bytes 61448 | tf_op jit(solution)/shard_map/ppermute | solution.py:56
  8.6 0.6 masks.1
  9.1 0.0 collective-permute-done.2.raw3
  9.1 2.2 %collective-permute-done.1.raw2 = f32[168,128]{1,0:T(8,128)S(1)} collective-permute-done((f32[168,128]{1,0:T(8,128)S(1)}, f32[168,128]{1,0:T(8,128)S(1)}, u32[]{:S(2)}, u32[]{:S(2)}) %collective-permute-start.1) | collective-permute-done | bytes 86048 | tf_op jit(solution)/shard_map/ppermute | solution.py:48
  11.3 0.9 collective-permute-done.raw1
  12.2 0.4 merge.4
  12.6 0.0 collective-permute-done.3.below_ref
  12.6 0.0 collective-permute-done.4.above_ref
  12.6 0.1 collective-permute-start.5
  12.7 1.4 %collective-permute-done.5 = f32[320,128]{1,0:T(8,128)S(1)} collective-permute-done((f32[320,128]{1,0:T(8,128)S(1)}, f32[320,128]{1,0:T(8,128)S(1)}, u32[]{:S(2)}, u32[]{:S(2)}) %collective-permute-start.5) | collective-permute-done | bytes 163872 | tf_op jit(solution)/shard_map/ppermute | solution.py:52
  14.1 0.0 copy-start.3
  14.1 18.5 %all_to_all.20.slabs_ref = f32[8,40,128]{2,1,0:T(8,128)S(1)} all-to-all(f32[8,40,128]{2,1,0:T(8,128)S(1)} %bitcast.4), channel_id=1, replica_groups={{0,8,16,24,32,40,48,56},{4,12,20,28,36,44,52,60},{64,72,80,88,96,104,11..., dimensions={0} | all-to-all | bytes 327680 | tf_op jit(solution)/shard_map/all_to_all | solution.py:61
  32.6 1.1 %react.2 = (f32[160,128]{1,0:T(8,128)S(1)}, f32[40,128]{1,0:T(8,128)S(1)}, f32[40,128]{1,0:T(8,128)S(1)}, f32[40,128]{1,0:T(8,128)S(1)}) custom-call(f32[6,128]{1,0:T(8,128)S(1)} %get-tuple-element.53.mask_ref, f32[8,40,128]{2,1,0:T(8,128)S(1)} %all_to_all.20.slabs_ref, f32[40,128]{1,0:T(8,128)S(1)} %get-tuple-element.64.own_in, ...), custom_call_target="tpu_custom_call" | custom-call | bytes 2171904 | tf_op jit(solution)/shard_map/react/pallas_call | solution.py:239
  33.7 1.5 %collective-permute-start.8 = (f32[160,128]{1,0:T(8,128)S(1)}, f32[160,128]{1,0:T(8,128)S(1)}, u32[]{:S(2)}, u32[]{:S(2)}) collective-permute-start(f32[160,128]{1,0:T(8,128)S(1)} %get-tuple-element.68.raw0), channel_id=1, source_target_pairs={{0,192},{4,196},{8,200},{12,204},{16,208},{20,212},{24,216},{28,22... | collective-permute-start | bytes 245768 | tf_op jit(solution)/shard_map/ppermute | solution.py:48
  35.2 1.5 %collective-permute-start.7 = (f32[160,128]{1,0:T(8,128)S(1)}, f32[160,128]{1,0:T(8,128)S(1)}, u32[]{:S(2)}, u32[]{:S(2)}) collective-permute-start(f32[160,128]{1,0:T(8,128)S(1)} %get-tuple-element.68.raw0), channel_id=1, source_target_pairs={{0,128},{4,132},{8,136},{12,140},{16,144},{20,148},{24,152},{28,15... | collective-permute-start | bytes 245768 | tf_op jit(solution)/shard_map/ppermute | solution.py:48
  36.7 0.0 collective-permute-start.6
  36.7 0.4 collective-permute-start.9
  37.0 1.7 %collective-permute-start.10 = (f32[40,128]{1,0:T(8,128)S(1)}, f32[40,128]{1,0:T(8,128)S(1)}, u32[]{:S(2)}, u32[]{:S(2)}) collective-permute-start(f32[40,128]{1,0:T(8,128)S(1)} %get-tuple-element.72), channel_id=1, source_target_pairs={{0,3},{1,0},{2,1},{3,2},{4,7},{5,4},{6,5},{7,6},{8,11},{9,8},{10,9... | collective-permute-start | bytes 61448 | tf_op jit(solution)/shard_map/ppermute | solution.py:56
  38.7 0.0 collective-permute-done.8.raw3
  38.7 2.4 %collective-permute-done.7.raw2 = f32[160,128]{1,0:T(8,128)S(1)} collective-permute-done((f32[160,128]{1,0:T(8,128)S(1)}, f32[160,128]{1,0:T(8,128)S(1)}, u32[]{:S(2)}, u32[]{:S(2)}) %collective-permute-start.7) | collective-permute-done | bytes 81952 | tf_op jit(solution)/shard_map/ppermute | solution.py:48
  41.1 1.2 %collective-permute-done.6.raw1 = f32[160,128]{1,0:T(8,128)S(1)} collective-permute-done((f32[160,128]{1,0:T(8,128)S(1)}, f32[160,128]{1,0:T(8,128)S(1)}, u32[]{:S(2)}, u32[]{:S(2)}) %collective-permute-start.6) | collective-permute-done | bytes 81952 | tf_op jit(solution)/shard_map/ppermute | solution.py:48
  42.3 0.3 merge.5
  42.7 0.0 collective-permute-done.9.below_ref
  42.7 0.0 collective-permute-done.10.above_ref
  42.7 0.1 collective-permute-start.11
  42.8 1.4 %collective-permute-done.11 = f32[320,128]{1,0:T(8,128)S(1)} collective-permute-done((f32[320,128]{1,0:T(8,128)S(1)}, f32[320,128]{1,0:T(8,128)S(1)}, u32[]{:S(2)}, u32[]{:S(2)}) %collective-permute-start.11) | collective-permute-done | bytes 163872 | tf_op jit(solution)/shard_map/ppermute | solution.py:52
  44.2 12.7 %all_to_all.21.slabs_ref = f32[8,40,128]{2,1,0:T(8,128)S(1)} all-to-all(f32[8,40,128]{2,1,0:T(8,128)S(1)} %bitcast.5), channel_id=1, replica_groups={{0,8,16,24,32,40,48,56},{4,12,20,28,36,44,52,60},{64,72,80,88,96,104,11..., dimensions={0} | all-to-all | bytes 327680 | tf_op jit(solution)/shard_map/all_to_all | solution.py:61
  57.0 0.3 step.1
  57.3 2.5 %collective-permute-start.14 = (f32[160,128]{1,0:T(8,128)S(1)}, f32[160,128]{1,0:T(8,128)S(1)}, u32[]{:S(2)}, u32[]{:S(2)}) collective-permute-start(f32[160,128]{1,0:T(8,128)S(1)} %get-tuple-element.77.raw0), channel_id=1, source_target_pairs={{0,192},{4,196},{8,200},{12,204},{16,208},{20,212},{24,216},{28,22... | collective-permute-start | bytes 245768 | tf_op jit(solution)/shard_map/ppermute | solution.py:48
  59.8 0.8 collective-permute-start.13
  60.6 0.5 collective-permute-start.12
  61.1 0.3 collective-permute-start.15
  61.5 1.7 %collective-permute-start.16 = (f32[40,128]{1,0:T(8,128)S(1)}, f32[40,128]{1,0:T(8,128)S(1)}, u32[]{:S(2)}, u32[]{:S(2)}) collective-permute-start(f32[40,128]{1,0:T(8,128)S(1)} %get-tuple-element.81), channel_id=1, source_target_pairs={{0,3},{1,0},{2,1},{3,2},{4,7},{5,4},{6,5},{7,6},{8,11},{9,8},{10,9... | collective-permute-start | bytes 61448 | tf_op jit(solution)/shard_map/ppermute | solution.py:56
  63.2 0.0 collective-permute-done.14.raw3
  63.2 2.7 %collective-permute-done.13.raw2 = f32[160,128]{1,0:T(8,128)S(1)} collective-permute-done((f32[160,128]{1,0:T(8,128)S(1)}, f32[160,128]{1,0:T(8,128)S(1)}, u32[]{:S(2)}, u32[]{:S(2)}) %collective-permute-start.13) | collective-permute-done | bytes 81952 | tf_op jit(solution)/shard_map/ppermute | solution.py:48
  65.8 0.8 collective-permute-done.12.raw1
  66.6 0.4 merge.6
  67.0 0.0 collective-permute-done.15.below_ref
  67.0 0.0 collective-permute-done.16.above_ref
  67.0 0.1 collective-permute-start.17
  67.1 1.4 %collective-permute-done.17 = f32[320,128]{1,0:T(8,128)S(1)} collective-permute-done((f32[320,128]{1,0:T(8,128)S(1)}, f32[320,128]{1,0:T(8,128)S(1)}, u32[]{:S(2)}, u32[]{:S(2)}) %collective-permute-start.17) | collective-permute-done | bytes 163872 | tf_op jit(solution)/shard_map/ppermute | solution.py:52
  68.5 12.7 %all_to_all.22.slabs_ref = f32[8,40,128]{2,1,0:T(8,128)S(1)} all-to-all(f32[8,40,128]{2,1,0:T(8,128)S(1)} %bitcast.6), channel_id=1, replica_groups={{0,8,16,24,32,40,48,56},{4,12,20,28,36,44,52,60},{64,72,80,88,96,104,11..., dimensions={0} | all-to-all | bytes 327680 | tf_op jit(solution)/shard_map/all_to_all | solution.py:61
  81.3 1.1 %react.3 = (f32[160,128]{1,0:T(8,128)S(1)}, f32[40,128]{1,0:T(8,128)S(1)}, f32[40,128]{1,0:T(8,128)S(1)}, f32[40,128]{1,0:T(8,128)S(1)}) custom-call(f32[6,128]{1,0:T(8,128)S(1)} %get-tuple-element.53.mask_ref, f32[8,40,128]{2,1,0:T(8,128)S(1)} %all_to_all.22.slabs_ref, f32[40,128]{1,0:T(8,128)S(1)} %get-tuple-element.83.own_in, ...), custom_call_target="tpu_custom_call" | custom-call | bytes 2171904 | tf_op jit(solution)/shard_map/react/pallas_call | solution.py:239
  82.4 2.2 %collective-permute-start.20 = (f32[160,128]{1,0:T(8,128)S(1)}, f32[160,128]{1,0:T(8,128)S(1)}, u32[]{:S(2)}, u32[]{:S(2)}) collective-permute-start(f32[160,128]{1,0:T(8,128)S(1)} %get-tuple-element.86.raw0), channel_id=1, source_target_pairs={{0,192},{4,196},{8,200},{12,204},{16,208},{20,212},{24,216},{28,22... | collective-permute-start | bytes 245768 | tf_op jit(solution)/shard_map/ppermute | solution.py:48
  84.5 1.5 %collective-permute-start.19 = (f32[160,128]{1,0:T(8,128)S(1)}, f32[160,128]{1,0:T(8,128)S(1)}, u32[]{:S(2)}, u32[]{:S(2)}) collective-permute-start(f32[160,128]{1,0:T(8,128)S(1)} %get-tuple-element.86.raw0), channel_id=1, source_target_pairs={{0,128},{4,132},{8,136},{12,140},{16,144},{20,148},{24,152},{28,15... | collective-permute-start | bytes 245768 | tf_op jit(solution)/shard_map/ppermute | solution.py:48
  86.0 0.0 collective-permute-start.18
  86.0 0.1 collective-permute-start.21
  86.1 2.0 %collective-permute-start.22 = (f32[40,128]{1,0:T(8,128)S(1)}, f32[40,128]{1,0:T(8,128)S(1)}, u32[]{:S(2)}, u32[]{:S(2)}) collective-permute-start(f32[40,128]{1,0:T(8,128)S(1)} %get-tuple-element.90), channel_id=1, source_target_pairs={{0,3},{1,0},{2,1},{3,2},{4,7},{5,4},{6,5},{7,6},{8,11},{9,8},{10,9... | collective-permute-start | bytes 61448 | tf_op jit(solution)/shard_map/ppermute | solution.py:56
  88.1 0.0 collective-permute-done.20.raw3
  88.1 2.4 %collective-permute-done.19.raw2 = f32[160,128]{1,0:T(8,128)S(1)} collective-permute-done((f32[160,128]{1,0:T(8,128)S(1)}, f32[160,128]{1,0:T(8,128)S(1)}, u32[]{:S(2)}, u32[]{:S(2)}) %collective-permute-start.19) | collective-permute-done | bytes 81952 | tf_op jit(solution)/shard_map/ppermute | solution.py:48
  90.5 1.2 %collective-permute-done.18.raw1 = f32[160,128]{1,0:T(8,128)S(1)} collective-permute-done((f32[160,128]{1,0:T(8,128)S(1)}, f32[160,128]{1,0:T(8,128)S(1)}, u32[]{:S(2)}, u32[]{:S(2)}) %collective-permute-start.18) | collective-permute-done | bytes 81952 | tf_op jit(solution)/shard_map/ppermute | solution.py:48
  91.7 0.4 merge.7
  92.0 0.0 collective-permute-done.21.below_ref
  92.0 0.0 collective-permute-done.22.above_ref
  92.1 0.1 collective-permute-start.23
  92.2 1.4 %collective-permute-done.23 = f32[320,128]{1,0:T(8,128)S(1)} collective-permute-done((f32[320,128]{1,0:T(8,128)S(1)}, f32[320,128]{1,0:T(8,128)S(1)}, u32[]{:S(2)}, u32[]{:S(2)}) %collective-permute-start.23) | collective-permute-done | bytes 163872 | tf_op jit(solution)/shard_map/ppermute | solution.py:52
  93.6 12.7 %all_to_all.23.slabs_ref = f32[8,40,128]{2,1,0:T(8,128)S(1)} all-to-all(f32[8,40,128]{2,1,0:T(8,128)S(1)} %bitcast.7), channel_id=1, replica_groups={{0,8,16,24,32,40,48,56},{4,12,20,28,36,44,52,60},{64,72,80,88,96,104,11..., dimensions={0} | all-to-all | bytes 327680 | tf_op jit(solution)/shard_map/all_to_all | solution.py:61
  106.3 0.6 last.1
  (15 shorter events, 0.1 us)
Async XLA Ops:
  0.0 8.6 %copy-start.4 = (s32[8]{0:T(128)S(1)}, s32[8]{0:T(128)}, u32[]{:S(2)}) copy-start(s32[8]{0:T(128)} %depth_ref.1) | copy-start | bytes 100
  0.0 8.6 %copy-start.5 = (s32[8]{0:T(128)S(1)}, s32[8]{0:T(128)}, u32[]{:S(2)}) copy-start(s32[8]{0:T(128)} %newton_ref.1) | copy-start | bytes 100
  0.0 32.6 %copy-start.2 = (bf16[4,7,128,128]{3,2,1,0:T(8,128)(2,1)S(1)}, bf16[4,7,128,128]{3,2,1,0:T(8,128)(2,1)}, u32[]{:S(2)}) copy-start(bf16[4,7,128,128]{3,2,1,0:T(8,128)(2,1)} %tiles_ref.5) | copy-start | bytes 2752516
  2.0 30.6 %copy-start = (bf16[30,30,512]{2,1,0:T(8,128)(2,1)S(1)}, bf16[30,30,512]{2,1,0:T(8,128)(2,1)}, u32[]{:S(2)}) copy-start(bf16[30,30,512]{2,1,0:T(8,128)(2,1)} %inv_ref.3) | copy-start | bytes 2764804
  2.0 7.1 %collective-permute-start.2 = (f32[168,128]{1,0:T(8,128)S(1)}, f32[168,128]{1,0:T(8,128)S(1)}, u32[]{:S(2)}, u32[]{:S(2)}) collective-permute-start(f32[168,128]{1,0:T(8,128)S(1)} %get-tuple-element.50.raw0), channel_id=1, source_target_pairs={{0,192},{4,196},{8,200},{12,204},{16,208},{20,212},{24,216},{28,22... | collective-permute-start | bytes 258056 | tf_op jit(solution)/shard_map/ppermute | solution.py:48
  4.8 6.5 %collective-permute-start.1 = (f32[168,128]{1,0:T(8,128)S(1)}, f32[168,128]{1,0:T(8,128)S(1)}, u32[]{:S(2)}, u32[]{:S(2)}) collective-permute-start(f32[168,128]{1,0:T(8,128)S(1)} %get-tuple-element.50.raw0), channel_id=1, source_target_pairs={{0,128},{4,132},{8,136},{12,140},{16,144},{20,148},{24,152},{28,15... | collective-permute-start | bytes 258056 | tf_op jit(solution)/shard_map/ppermute | solution.py:48
  5.6 6.5 %collective-permute-start = (f32[168,128]{1,0:T(8,128)S(1)}, f32[168,128]{1,0:T(8,128)S(1)}, u32[]{:S(2)}, u32[]{:S(2)}) collective-permute-start(f32[168,128]{1,0:T(8,128)S(1)} %get-tuple-element.50.raw0), channel_id=1, source_target_pairs={{0,64},{4,68},{8,72},{12,76},{16,80},{20,84},{24,88},{28,92},{32,9... | collective-permute-start | bytes 258056 | tf_op jit(solution)/shard_map/ppermute | solution.py:48
  6.5 6.1 %collective-permute-start.3 = (f32[40,128]{1,0:T(8,128)S(1)}, f32[40,128]{1,0:T(8,128)S(1)}, u32[]{:S(2)}, u32[]{:S(2)}) collective-permute-start(f32[40,128]{1,0:T(8,128)S(1)} %get-tuple-element.61), channel_id=1, source_target_pairs={{0,1},{1,2},{2,3},{3,0},{4,5},{5,6},{6,7},{7,4},{8,9},{9,10},{10,1... | collective-permute-start | bytes 61448 | tf_op jit(solution)/shard_map/ppermute | solution.py:56
  6.8 5.9 %collective-permute-start.4 = (f32[40,128]{1,0:T(8,128)S(1)}, f32[40,128]{1,0:T(8,128)S(1)}, u32[]{:S(2)}, u32[]{:S(2)}) collective-permute-start(f32[40,128]{1,0:T(8,128)S(1)} %get-tuple-element.62), channel_id=1, source_target_pairs={{0,3},{1,0},{2,1},{3,2},{4,7},{5,4},{6,5},{7,6},{8,11},{9,8},{10,9... | collective-permute-start | bytes 61448 | tf_op jit(solution)/shard_map/ppermute | solution.py:56
  12.6 1.5 %collective-permute-start.5 = (f32[320,128]{1,0:T(8,128)S(1)}, f32[320,128]{1,0:T(8,128)S(1)}, u32[]{:S(2)}, u32[]{:S(2)}) collective-permute-start(f32[320,128]{1,0:T(8,128)S(1)} %get-tuple-element.63), channel_id=1, source_target_pairs={{0,4},{4,0},{8,12},{12,8},{16,20},{20,16},{24,28},{28,24},{32,36},... | collective-permute-start | bytes 491528 | tf_op jit(solution)/shard_map/ppermute | solution.py:52
  14.1 18.5 %copy-start.3 = (bf16[10,10,512]{2,1,0:T(8,128)(2,1)S(1)}, bf16[10,10,512]{2,1,0:T(8,128)(2,1)}, u32[]{:S(2)}) copy-start(bf16[10,10,512]{2,1,0:T(8,128)(2,1)} %jac_ref.3) | copy-start | bytes 307204
  33.7 23.3 %copy-start.1 = (bf16[4,7,128,128]{3,2,1,0:T(8,128)(2,1)S(1)}, bf16[4,7,128,128]{3,2,1,0:T(8,128)(2,1)}, u32[]{:S(2)}) copy-start(bf16[4,7,128,128]{3,2,1,0:T(8,128)(2,1)} %tiles_ref.4) | copy-start | bytes 2752516
  33.7 5.0 %collective-permute-start.8 = (f32[160,128]{1,0:T(8,128)S(1)}, f32[160,128]{1,0:T(8,128)S(1)}, u32[]{:S(2)}, u32[]{:S(2)}) collective-permute-start(f32[160,128]{1,0:T(8,128)S(1)} %get-tuple-element.68.raw0), channel_id=1, source_target_pairs={{0,192},{4,196},{8,200},{12,204},{16,208},{20,212},{24,216},{28,22... | collective-permute-start | bytes 245768 | tf_op jit(solution)/shard_map/ppermute | solution.py:48
  35.2 5.9 %collective-permute-start.7 = (f32[160,128]{1,0:T(8,128)S(1)}, f32[160,128]{1,0:T(8,128)S(1)}, u32[]{:S(2)}, u32[]{:S(2)}) collective-permute-start(f32[160,128]{1,0:T(8,128)S(1)} %get-tuple-element.68.raw0), channel_id=1, source_target_pairs={{0,128},{4,132},{8,136},{12,140},{16,144},{20,148},{24,152},{28,15... | collective-permute-start | bytes 245768 | tf_op jit(solution)/shard_map/ppermute | solution.py:48
  36.7 5.7 %collective-permute-start.6 = (f32[160,128]{1,0:T(8,128)S(1)}, f32[160,128]{1,0:T(8,128)S(1)}, u32[]{:S(2)}, u32[]{:S(2)}) collective-permute-start(f32[160,128]{1,0:T(8,128)S(1)} %get-tuple-element.68.raw0), channel_id=1, source_target_pairs={{0,64},{4,68},{8,72},{12,76},{16,80},{20,84},{24,88},{28,92},{32,9... | collective-permute-start | bytes 245768 | tf_op jit(solution)/shard_map/ppermute | solution.py:48
  36.7 6.0 %collective-permute-start.9 = (f32[40,128]{1,0:T(8,128)S(1)}, f32[40,128]{1,0:T(8,128)S(1)}, u32[]{:S(2)}, u32[]{:S(2)}) collective-permute-start(f32[40,128]{1,0:T(8,128)S(1)} %get-tuple-element.71), channel_id=1, source_target_pairs={{0,1},{1,2},{2,3},{3,0},{4,5},{5,6},{6,7},{7,4},{8,9},{9,10},{10,1... | collective-permute-start | bytes 61448 | tf_op jit(solution)/shard_map/ppermute | solution.py:56
  37.0 5.6 %collective-permute-start.10 = (f32[40,128]{1,0:T(8,128)S(1)}, f32[40,128]{1,0:T(8,128)S(1)}, u32[]{:S(2)}, u32[]{:S(2)}) collective-permute-start(f32[40,128]{1,0:T(8,128)S(1)} %get-tuple-element.72), channel_id=1, source_target_pairs={{0,3},{1,0},{2,1},{3,2},{4,7},{5,4},{6,5},{7,6},{8,11},{9,8},{10,9... | collective-permute-start | bytes 61448 | tf_op jit(solution)/shard_map/ppermute | solution.py:56
  42.7 1.5 %collective-permute-start.11 = (f32[320,128]{1,0:T(8,128)S(1)}, f32[320,128]{1,0:T(8,128)S(1)}, u32[]{:S(2)}, u32[]{:S(2)}) collective-permute-start(f32[320,128]{1,0:T(8,128)S(1)} %get-tuple-element.73), channel_id=1, source_target_pairs={{0,4},{4,0},{8,12},{12,8},{16,20},{20,16},{24,28},{28,24},{32,36},... | collective-permute-start | bytes 491528 | tf_op jit(solution)/shard_map/ppermute | solution.py:52
  57.3 5.9 %collective-permute-start.14 = (f32[160,128]{1,0:T(8,128)S(1)}, f32[160,128]{1,0:T(8,128)S(1)}, u32[]{:S(2)}, u32[]{:S(2)}) collective-permute-start(f32[160,128]{1,0:T(8,128)S(1)} %get-tuple-element.77.raw0), channel_id=1, source_target_pairs={{0,192},{4,196},{8,200},{12,204},{16,208},{20,212},{24,216},{28,22... | collective-permute-start | bytes 245768 | tf_op jit(solution)/shard_map/ppermute | solution.py:48
  59.8 6.0 %collective-permute-start.13 = (f32[160,128]{1,0:T(8,128)S(1)}, f32[160,128]{1,0:T(8,128)S(1)}, u32[]{:S(2)}, u32[]{:S(2)}) collective-permute-start(f32[160,128]{1,0:T(8,128)S(1)} %get-tuple-element.77.raw0), channel_id=1, source_target_pairs={{0,128},{4,132},{8,136},{12,140},{16,144},{20,148},{24,152},{28,15... | collective-permute-start | bytes 245768 | tf_op jit(solution)/shard_map/ppermute | solution.py:48
  60.6 6.0 %collective-permute-start.12 = (f32[160,128]{1,0:T(8,128)S(1)}, f32[160,128]{1,0:T(8,128)S(1)}, u32[]{:S(2)}, u32[]{:S(2)}) collective-permute-start(f32[160,128]{1,0:T(8,128)S(1)} %get-tuple-element.77.raw0), channel_id=1, source_target_pairs={{0,64},{4,68},{8,72},{12,76},{16,80},{20,84},{24,88},{28,92},{32,9... | collective-permute-start | bytes 245768 | tf_op jit(solution)/shard_map/ppermute | solution.py:48
  61.1 5.9 %collective-permute-start.15 = (f32[40,128]{1,0:T(8,128)S(1)}, f32[40,128]{1,0:T(8,128)S(1)}, u32[]{:S(2)}, u32[]{:S(2)}) collective-permute-start(f32[40,128]{1,0:T(8,128)S(1)} %get-tuple-element.80), channel_id=1, source_target_pairs={{0,1},{1,2},{2,3},{3,0},{4,5},{5,6},{6,7},{7,4},{8,9},{9,10},{10,1... | collective-permute-start | bytes 61448 | tf_op jit(solution)/shard_map/ppermute | solution.py:56
  61.5 5.6 %collective-permute-start.16 = (f32[40,128]{1,0:T(8,128)S(1)}, f32[40,128]{1,0:T(8,128)S(1)}, u32[]{:S(2)}, u32[]{:S(2)}) collective-permute-start(f32[40,128]{1,0:T(8,128)S(1)} %get-tuple-element.81), channel_id=1, source_target_pairs={{0,3},{1,0},{2,1},{3,2},{4,7},{5,4},{6,5},{7,6},{8,11},{9,8},{10,9... | collective-permute-start | bytes 61448 | tf_op jit(solution)/shard_map/ppermute | solution.py:56
  67.0 1.5 %collective-permute-start.17 = (f32[320,128]{1,0:T(8,128)S(1)}, f32[320,128]{1,0:T(8,128)S(1)}, u32[]{:S(2)}, u32[]{:S(2)}) collective-permute-start(f32[320,128]{1,0:T(8,128)S(1)} %get-tuple-element.82), channel_id=1, source_target_pairs={{0,4},{4,0},{8,12},{12,8},{16,20},{20,16},{24,28},{28,24},{32,36},... | collective-permute-start | bytes 491528 | tf_op jit(solution)/shard_map/ppermute | solution.py:52
  82.4 5.7 %collective-permute-start.20 = (f32[160,128]{1,0:T(8,128)S(1)}, f32[160,128]{1,0:T(8,128)S(1)}, u32[]{:S(2)}, u32[]{:S(2)}) collective-permute-start(f32[160,128]{1,0:T(8,128)S(1)} %get-tuple-element.86.raw0), channel_id=1, source_target_pairs={{0,192},{4,196},{8,200},{12,204},{16,208},{20,212},{24,216},{28,22... | collective-permute-start | bytes 245768 | tf_op jit(solution)/shard_map/ppermute | solution.py:48
  84.5 5.9 %collective-permute-start.19 = (f32[160,128]{1,0:T(8,128)S(1)}, f32[160,128]{1,0:T(8,128)S(1)}, u32[]{:S(2)}, u32[]{:S(2)}) collective-permute-start(f32[160,128]{1,0:T(8,128)S(1)} %get-tuple-element.86.raw0), channel_id=1, source_target_pairs={{0,128},{4,132},{8,136},{12,140},{16,144},{20,148},{24,152},{28,15... | collective-permute-start | bytes 245768 | tf_op jit(solution)/shard_map/ppermute | solution.py:48
  86.0 5.7 %collective-permute-start.18 = (f32[160,128]{1,0:T(8,128)S(1)}, f32[160,128]{1,0:T(8,128)S(1)}, u32[]{:S(2)}, u32[]{:S(2)}) collective-permute-start(f32[160,128]{1,0:T(8,128)S(1)} %get-tuple-element.86.raw0), channel_id=1, source_target_pairs={{0,64},{4,68},{8,72},{12,76},{16,80},{20,84},{24,88},{28,92},{32,9... | collective-permute-start | bytes 245768 | tf_op jit(solution)/shard_map/ppermute | solution.py:48
  86.0 6.0 %collective-permute-start.21 = (f32[40,128]{1,0:T(8,128)S(1)}, f32[40,128]{1,0:T(8,128)S(1)}, u32[]{:S(2)}, u32[]{:S(2)}) collective-permute-start(f32[40,128]{1,0:T(8,128)S(1)} %get-tuple-element.89), channel_id=1, source_target_pairs={{0,1},{1,2},{2,3},{3,0},{4,5},{5,6},{6,7},{7,4},{8,9},{9,10},{10,1... | collective-permute-start | bytes 61448 | tf_op jit(solution)/shard_map/ppermute | solution.py:56
  86.1 5.9 %collective-permute-start.22 = (f32[40,128]{1,0:T(8,128)S(1)}, f32[40,128]{1,0:T(8,128)S(1)}, u32[]{:S(2)}, u32[]{:S(2)}) collective-permute-start(f32[40,128]{1,0:T(8,128)S(1)} %get-tuple-element.90), channel_id=1, source_target_pairs={{0,3},{1,0},{2,1},{3,2},{4,7},{5,4},{6,5},{7,6},{8,11},{9,8},{10,9... | collective-permute-start | bytes 61448 | tf_op jit(solution)/shard_map/ppermute | solution.py:56
  92.1 1.5 %collective-permute-start.23 = (f32[320,128]{1,0:T(8,128)S(1)}, f32[320,128]{1,0:T(8,128)S(1)}, u32[]{:S(2)}, u32[]{:S(2)}) collective-permute-start(f32[320,128]{1,0:T(8,128)S(1)} %get-tuple-element.91), channel_id=1, source_target_pairs={{0,4},{4,0},{8,12},{12,8},{16,20},{20,16},{24,28},{28,24},{32,36},... | collective-permute-start | bytes 491528 | tf_op jit(solution)/shard_map/ppermute | solution.py:52

commit v5 on v4

--- a/solution.py
+++ b/solution.py
@@ -17,6 +17,7 @@
 LEV = 64
 RB = 4
 NX, NZ, NCORE = 4, 8, 2
+X_SHIFTS = (1, 3, 2)
 N_LAT = 4
 TERMS = RB * NBAND
 SLAB = RB * TR
@@ -80,10 +81,25 @@
                 south_ref[r * TR : (r + 1) * TR, :] = term
 
 
+def start_tiles(tiles_far, tiles_ref, arrivals):
+    copies = [
+        pltpu.make_async_copy(tiles_far.at[r], tiles_ref.at[r], arrivals.at[r]) for r in range(RB)
+    ]
+    for copy in copies:
+        copy.start()
+    return copies
+
+
+TILE_SCRATCH = [
+    pltpu.VMEM((RB, NB, BLK, BLK), jnp.bfloat16),
+    pltpu.SemaphoreType.DMA((RB,)),
+]
+
+
 def first_kernel(
     field_far, impl_dest_far, impl_local_far, expl_dest_far, expl_local_far, tiles_far,
     raw_ref, own_ref, north_ref, south_ref,
-    field_ref, impl_dest, impl_local, expl_dest, expl_local, tiles_ref, arrivals, tile_arrivals,
+    field_ref, impl_dest, impl_local, expl_dest, expl_local, tiles_ref, tile_arrivals, arrivals,
 ):
     copies = [
         pltpu.make_async_copy(far, near, arrivals.at[i])
@@ -97,12 +113,9 @@
             )
         )
     ]
-    tile_copies = [
-        pltpu.make_async_copy(tiles_far.at[r], tiles_ref.at[r], tile_arrivals.at[r])
-        for r in range(RB)
-    ]
-    for copy in copies + tile_copies:
+    for copy in copies:
         copy.start()
+    tile_copies = start_tiles(tiles_far, tiles_ref, tile_arrivals)
     raw_ref[TERMS * TR :, :] = jnp.zeros((2 * RB, BLK), F32)
     for copy in copies:
         copy.wait()
@@ -198,13 +211,14 @@
 
 def react_kernel(
     mask_ref, slabs_ref, own_in, below_ref, above_ref, sweeps_ref, jac_ref, inv_ref,
-    tiles_ref, raw_ref, own_ref, north_ref, south_ref,
+    tiles_far, raw_ref, own_ref, north_ref, south_ref, tiles_ref, tile_arrivals,
 ):
+    tile_copies = start_tiles(tiles_far, tiles_ref, tile_arrivals)
     blocks = arrived_blocks(mask_ref, slabs_ref, own_in, below_ref, above_ref)
     blocks = [
         column_block(blocks[r], r, jac_ref, inv_ref, sweeps_ref[r : r + 1, :]) for r in range(RB)
     ]
-    emit_terms(blocks, tiles_ref, raw_ref, own_ref, north_ref, south_ref)
+    emit_terms(blocks, tiles_ref, raw_ref, own_ref, north_ref, south_ref, tile_copies)
 
 
 def step_kernel(
@@ -262,7 +276,7 @@
     newton_inverse,
 ):
     def gather_x(raw):
-        return [shift_x(raw, k) for k in range(1, NX)]
+        return [shift_x(raw, k) for k in X_SHIFTS]
 
     def deliver(terms, raws, slot):
         raw, own, north, south = terms
@@ -290,9 +304,8 @@
         scratch=[
             pltpu.VMEM((TR, RB * BLK), F32),
             *[pltpu.VMEM((RB, NBAND), jnp.int32)] * 4,
-            pltpu.VMEM((RB, NB, BLK, BLK), jnp.bfloat16),
+            *TILE_SCRATCH,
             pltpu.SemaphoreType.DMA((5,)),
-            pltpu.SemaphoreType.DMA((RB,)),
         ],
     )
     int_table = jax.ShapeDtypeStruct((RB, BLK), jnp.int32)
@@ -303,6 +316,7 @@
     *raws, masks, sweeps = lax.optimization_barrier((*raws, masks, sweeps))
     slot_table = jax.ShapeDtypeStruct((NX * RB, NBAND), jnp.int32)
     slots = call(slots_kernel, (slot_table, slot_table), [terms[0], *raws], 0, "slots")
+    expl_far = pltpu.with_memory_space_constraint(expl_tiles, pltpu.HBM)
     for step_index in range(STEPS):
         if step_index:
             raws = gather_x(terms[0])
@@ -310,9 +324,11 @@
         terms = call(
             react_kernel,
             TERM_SHAPES,
-            arrived + [sweeps, jacobian, newton_inverse, expl_tiles],
+            arrived + [sweeps, jacobian, newton_inverse, expl_far],
             0,
             "react",
+            far=1,
+            scratch=TILE_SCRATCH,
         )
         arrived = deliver(terms, gather_x(terms[0]), slots[1])
         if step_index + 1 < STEPS:

time: 107 us -> 109 us (1.019)
  Pallas kernels: 7.14 us -> 8.32 us
    pallas_call x11, Pallas kernels: 7.14 us -> 8.32 us  [call(): pl.pallas_call(kernel, out_shape=out_shape, in_specs=[SMEM] * smem + [VME...]
  transfers between devices with their start and end apart: 24 -> 24, of which waited for: 12 -> 15; matrix products, arithmetic and copies ran while one was open for 0% -> 0% of each run, Pallas kernels for 2% -> 2%
where the time goes in v5:
time: 109 us; the launch traced here: 108 us
  blocking collectives  56.7 us (52%)
  starting transfers between devices  24.3 us (22%)
  waiting for transfers between devices  18.6 us (17%)
  Pallas kernels  8.32 us (8%)
    all_to_all x4, blocking collectives, exchange_z(): lax.all_to_all(value, 'cols', 0, 0, axis_index_groups=groups, tiled=True)  56.7 us
    ppermute x12, starting transfers between devices, shift_x(): return lax.ppermute(value, 'cols', pairs)  15.8 us
    ppermute x12, waiting for transfers between devices, shift_x(): return lax.ppermute(value, 'cols', pairs)  13.1 us
    pallas_call x11, Pallas kernels, call(): pl.pallas_call(kernel, out_shape=out_shape, in_specs=[SMEM] * smem + [VME...  8.32 us
    ppermute x8, starting transfers between devices, ring_lat(): lax.ppermute(value, 'lat', [(i, (i + steps) % N_LAT) for i in range(N_LAT)])  8.1 us
    ppermute x4, waiting for transfers between devices, swap_core(): lax.ppermute(value, 'cols', [(i, i ^ 1) for i in range(NX * NZ * NCORE)])  5.53 us
  transfers between devices with their start and end apart: 24, of which 15 were waited for; matrix products, arithmetic and copies ran while one was open for 0% of the time, Pallas kernels for 2%

profile of v5, /device:TPU:24, one launch (start us, length us, event | category | flops | bytes accessed | tf_op | source)
XLA Modules:
  0.0 108.3 jit_solution(596902553756591857)
XLA Ops:
  0.0 1.9 %first.1 = (f32[168,128]{1,0:T(8,128)S(1)}, f32[40,128]{1,0:T(8,128)S(1)}, f32[40,128]{1,0:T(8,128)S(1)}, f32[40,128]{1,0:T(8,128)S(1)}) custom-call(f32[10,512]{1,0:T(8,128)} %field_far.1, s32[4,4]{1,0:T(4,128)} %impl_dest_far.1, s32[4,4]{1,0:T(4,128)} %impl_local_far.1, s32[4,4]{1,0:T(4,128)} %expl_dest_far.1, s32[4,4]{1,0:T(4,128)} %expl_local_far.1, ...), custom_call_target="tpu_custom_call" | custom-call | bytes 938240 | tf_op jit(solution)/shard_map/first/pallas_call | solution.py:253
  1.9 0.0 copy-start
  1.9 3.1 %collective-permute-start.2 = (f32[168,128]{1,0:T(8,128)S(1)}, f32[168,128]{1,0:T(8,128)S(1)}, u32[]{:S(2)}, u32[]{:S(2)}) collective-permute-start(f32[168,128]{1,0:T(8,128)S(1)} %get-tuple-element.50.raw0), channel_id=1, source_target_pairs={{0,128},{4,132},{8,136},{12,140},{16,144},{20,148},{24,152},{28,15... | collective-permute-start | bytes 258056 | tf_op jit(solution)/shard_map/ppermute | solution.py:49
  5.1 1.1 %collective-permute-start.1 = (f32[168,128]{1,0:T(8,128)S(1)}, f32[168,128]{1,0:T(8,128)S(1)}, u32[]{:S(2)}, u32[]{:S(2)}) collective-permute-start(f32[168,128]{1,0:T(8,128)S(1)} %get-tuple-element.50.raw0), channel_id=1, source_target_pairs={{0,192},{4,196},{8,200},{12,204},{16,208},{20,212},{24,216},{28,22... | collective-permute-start | bytes 258056 | tf_op jit(solution)/shard_map/ppermute | solution.py:49
  6.2 0.9 collective-permute-start
  7.1 0.2 collective-permute-start.3
  7.3 1.8 %collective-permute-start.4 = (f32[40,128]{1,0:T(8,128)S(1)}, f32[40,128]{1,0:T(8,128)S(1)}, u32[]{:S(2)}, u32[]{:S(2)}) collective-permute-start(f32[40,128]{1,0:T(8,128)S(1)} %get-tuple-element.62), channel_id=1, source_target_pairs={{0,3},{1,0},{2,1},{3,2},{4,7},{5,4},{6,5},{7,6},{8,11},{9,8},{10,9... | collective-permute-start | bytes 61448 | tf_op jit(solution)/shard_map/ppermute | solution.py:57
  9.1 0.6 masks.1
  9.7 0.0 collective-permute-done.2.raw3
  9.7 0.3 collective-permute-done.1.raw2
  10.0 1.9 %collective-permute-done.raw1 = f32[168,128]{1,0:T(8,128)S(1)} collective-permute-done((f32[168,128]{1,0:T(8,128)S(1)}, f32[168,128]{1,0:T(8,128)S(1)}, u32[]{:S(2)}, u32[]{:S(2)}) %collective-permute-start) | collective-permute-done | bytes 86048 | tf_op jit(solution)/shard_map/ppermute | solution.py:49
  11.9 0.3 merge.4
  12.3 0.0 collective-permute-done.3.below_ref
  12.3 0.0 collective-permute-done.4.above_ref
  12.3 0.1 collective-permute-start.5
  12.4 1.4 %collective-permute-done.5 = f32[320,128]{1,0:T(8,128)S(1)} collective-permute-done((f32[320,128]{1,0:T(8,128)S(1)}, f32[320,128]{1,0:T(8,128)S(1)}, u32[]{:S(2)}, u32[]{:S(2)}) %collective-permute-start.5) | collective-permute-done | bytes 163872 | tf_op jit(solution)/shard_map/ppermute | solution.py:53
  13.8 0.0 copy-start.2
  13.8 18.5 %all_to_all.20.slabs_ref = f32[8,40,128]{2,1,0:T(8,128)S(1)} all-to-all(f32[8,40,128]{2,1,0:T(8,128)S(1)} %bitcast.4), channel_id=1, replica_groups={{0,8,16,24,32,40,48,56},{4,12,20,28,36,44,52,60},{64,72,80,88,96,104,11..., dimensions={0} | all-to-all | bytes 327680 | tf_op jit(solution)/shard_map/all_to_all | solution.py:62
  32.3 1.7 %react.2 = (f32[160,128]{1,0:T(8,128)S(1)}, f32[40,128]{1,0:T(8,128)S(1)}, f32[40,128]{1,0:T(8,128)S(1)}, f32[40,128]{1,0:T(8,128)S(1)}) custom-call(f32[6,128]{1,0:T(8,128)S(1)} %get-tuple-element.53.mask_ref, f32[8,40,128]{2,1,0:T(8,128)S(1)} %all_to_all.20.slabs_ref, f32[40,128]{1,0:T(8,128)S(1)} %get-tuple-element.64.own_in, ...), custom_call_target="tpu_custom_call" | custom-call | bytes 2171904 | tf_op jit(solution)/shard_map/react/pallas_call | solution.py:253
  34.0 0.0 copy-start.1
  34.0 0.9 collective-permute-start.8
  34.9 2.4 %collective-permute-start.7 = (f32[160,128]{1,0:T(8,128)S(1)}, f32[160,128]{1,0:T(8,128)S(1)}, u32[]{:S(2)}, u32[]{:S(2)}) collective-permute-start(f32[160,128]{1,0:T(8,128)S(1)} %get-tuple-element.68.raw0), channel_id=1, source_target_pairs={{0,192},{4,196},{8,200},{12,204},{16,208},{20,212},{24,216},{28,22... | collective-permute-start | bytes 245768 | tf_op jit(solution)/shard_map/ppermute | solution.py:49
  37.3 0.0 collective-permute-start.6
  37.3 0.4 collective-permute-start.9
  37.7 1.7 %collective-permute-start.10 = (f32[40,128]{1,0:T(8,128)S(1)}, f32[40,128]{1,0:T(8,128)S(1)}, u32[]{:S(2)}, u32[]{:S(2)}) collective-permute-start(f32[40,128]{1,0:T(8,128)S(1)} %get-tuple-element.72), channel_id=1, source_target_pairs={{0,3},{1,0},{2,1},{3,2},{4,7},{5,4},{6,5},{7,6},{8,11},{9,8},{10,9... | collective-permute-start | bytes 61448 | tf_op jit(solution)/shard_map/ppermute | solution.py:57
  39.3 0.8 collective-permute-done.8.raw3
  40.2 0.4 collective-permute-done.7.raw2
  40.5 2.4 %collective-permute-done.6.raw1 = f32[160,128]{1,0:T(8,128)S(1)} collective-permute-done((f32[160,128]{1,0:T(8,128)S(1)}, f32[160,128]{1,0:T(8,128)S(1)}, u32[]{:S(2)}, u32[]{:S(2)}) %collective-permute-start.6) | collective-permute-done | bytes 81952 | tf_op jit(solution)/shard_map/ppermute | solution.py:49
  42.9 0.4 merge.5
  43.3 0.0 collective-permute-done.9.below_ref
  43.3 0.0 collective-permute-done.10.above_ref
  43.3 0.1 collective-permute-start.11
  43.4 1.4 %collective-permute-done.11 = f32[320,128]{1,0:T(8,128)S(1)} collective-permute-done((f32[320,128]{1,0:T(8,128)S(1)}, f32[320,128]{1,0:T(8,128)S(1)}, u32[]{:S(2)}, u32[]{:S(2)}) %collective-permute-start.11) | collective-permute-done | bytes 163872 | tf_op jit(solution)/shard_map/ppermute | solution.py:53
  44.8 12.7 %all_to_all.21.slabs_ref = f32[8,40,128]{2,1,0:T(8,128)S(1)} all-to-all(f32[8,40,128]{2,1,0:T(8,128)S(1)} %bitcast.5), channel_id=1, replica_groups={{0,8,16,24,32,40,48,56},{4,12,20,28,36,44,52,60},{64,72,80,88,96,104,11..., dimensions={0} | all-to-all | bytes 327680 | tf_op jit(solution)/shard_map/all_to_all | solution.py:62
  57.6 0.3 step.1
  57.9 1.6 %collective-permute-start.14 = (f32[160,128]{1,0:T(8,128)S(1)}, f32[160,128]{1,0:T(8,128)S(1)}, u32[]{:S(2)}, u32[]{:S(2)}) collective-permute-start(f32[160,128]{1,0:T(8,128)S(1)} %get-tuple-element.77.raw0), channel_id=1, source_target_pairs={{0,128},{4,132},{8,136},{12,140},{16,144},{20,148},{24,152},{28,15... | collective-permute-start | bytes 245768 | tf_op jit(solution)/shard_map/ppermute | solution.py:49
  59.5 2.4 %collective-permute-start.13 = (f32[160,128]{1,0:T(8,128)S(1)}, f32[160,128]{1,0:T(8,128)S(1)}, u32[]{:S(2)}, u32[]{:S(2)}) collective-permute-start(f32[160,128]{1,0:T(8,128)S(1)} %get-tuple-element.77.raw0), channel_id=1, source_target_pairs={{0,192},{4,196},{8,200},{12,204},{16,208},{20,212},{24,216},{28,22... | collective-permute-start | bytes 245768 | tf_op jit(solution)/shard_map/ppermute | solution.py:49
  61.9 0.0 collective-permute-start.12
  61.9 0.4 collective-permute-start.15
  62.2 1.7 %collective-permute-start.16 = (f32[40,128]{1,0:T(8,128)S(1)}, f32[40,128]{1,0:T(8,128)S(1)}, u32[]{:S(2)}, u32[]{:S(2)}) collective-permute-start(f32[40,128]{1,0:T(8,128)S(1)} %get-tuple-element.81), channel_id=1, source_target_pairs={{0,3},{1,0},{2,1},{3,2},{4,7},{5,4},{6,5},{7,6},{8,11},{9,8},{10,9... | collective-permute-start | bytes 61448 | tf_op jit(solution)/shard_map/ppermute | solution.py:57
  63.9 0.5 collective-permute-done.14.raw3
  64.4 0.2 collective-permute-done.13.raw2
  64.6 2.9 %collective-permute-done.12.raw1 = f32[160,128]{1,0:T(8,128)S(1)} collective-permute-done((f32[160,128]{1,0:T(8,128)S(1)}, f32[160,128]{1,0:T(8,128)S(1)}, u32[]{:S(2)}, u32[]{:S(2)}) %collective-permute-start.12) | collective-permute-done | bytes 81952 | tf_op jit(solution)/shard_map/ppermute | solution.py:49
  67.5 0.3 merge.6
  67.8 0.0 collective-permute-done.15.below_ref
  67.9 0.0 collective-permute-done.16.above_ref
  67.9 0.1 collective-permute-start.17
  68.0 1.4 %collective-permute-done.17 = f32[320,128]{1,0:T(8,128)S(1)} collective-permute-done((f32[320,128]{1,0:T(8,128)S(1)}, f32[320,128]{1,0:T(8,128)S(1)}, u32[]{:S(2)}, u32[]{:S(2)}) %collective-permute-start.17) | collective-permute-done | bytes 163872 | tf_op jit(solution)/shard_map/ppermute | solution.py:53
  69.4 12.7 %all_to_all.22.slabs_ref = f32[8,40,128]{2,1,0:T(8,128)S(1)} all-to-all(f32[8,40,128]{2,1,0:T(8,128)S(1)} %bitcast.6), channel_id=1, replica_groups={{0,8,16,24,32,40,48,56},{4,12,20,28,36,44,52,60},{64,72,80,88,96,104,11..., dimensions={0} | all-to-all | bytes 327680 | tf_op jit(solution)/shard_map/all_to_all | solution.py:62
  82.1 1.7 %react.3 = (f32[160,128]{1,0:T(8,128)S(1)}, f32[40,128]{1,0:T(8,128)S(1)}, f32[40,128]{1,0:T(8,128)S(1)}, f32[40,128]{1,0:T(8,128)S(1)}) custom-call(f32[6,128]{1,0:T(8,128)S(1)} %get-tuple-element.53.mask_ref, f32[8,40,128]{2,1,0:T(8,128)S(1)} %all_to_all.22.slabs_ref, f32[40,128]{1,0:T(8,128)S(1)} %get-tuple-element.83.own_in, ...), custom_call_target="tpu_custom_call" | custom-call | bytes 2171904 | tf_op jit(solution)/shard_map/react/pallas_call | solution.py:253
  83.8 1.0 collective-permute-start.20
  84.8 2.5 %collective-permute-start.19 = (f32[160,128]{1,0:T(8,128)S(1)}, f32[160,128]{1,0:T(8,128)S(1)}, u32[]{:S(2)}, u32[]{:S(2)}) collective-permute-start(f32[160,128]{1,0:T(8,128)S(1)} %get-tuple-element.86.raw0), channel_id=1, source_target_pairs={{0,192},{4,196},{8,200},{12,204},{16,208},{20,212},{24,216},{28,22... | collective-permute-start | bytes 245768 | tf_op jit(solution)/shard_map/ppermute | solution.py:49
  87.3 0.0 collective-permute-start.18
  87.3 0.1 collective-permute-start.21
  87.4 2.0 %collective-permute-start.22 = (f32[40,128]{1,0:T(8,128)S(1)}, f32[40,128]{1,0:T(8,128)S(1)}, u32[]{:S(2)}, u32[]{:S(2)}) collective-permute-start(f32[40,128]{1,0:T(8,128)S(1)} %get-tuple-element.90), channel_id=1, source_target_pairs={{0,3},{1,0},{2,1},{3,2},{4,7},{5,4},{6,5},{7,6},{8,11},{9,8},{10,9... | collective-permute-start | bytes 61448 | tf_op jit(solution)/shard_map/ppermute | solution.py:57
  89.4 1.1 collective-permute-done.20.raw3
  90.4 0.1 collective-permute-done.19.raw2
  90.6 2.4 %collective-permute-done.18.raw1 = f32[160,128]{1,0:T(8,128)S(1)} collective-permute-done((f32[160,128]{1,0:T(8,128)S(1)}, f32[160,128]{1,0:T(8,128)S(1)}, u32[]{:S(2)}, u32[]{:S(2)}) %collective-permute-start.18) | collective-permute-done | bytes 81952 | tf_op jit(solution)/shard_map/ppermute | solution.py:49
  93.0 0.4 merge.7
  93.4 0.0 collective-permute-done.22.above_ref
  93.4 0.1 collective-permute-start.23
  93.5 1.4 %collective-permute-done.23 = f32[320,128]{1,0:T(8,128)S(1)} collective-permute-done((f32[320,128]{1,0:T(8,128)S(1)}, f32[320,128]{1,0:T(8,128)S(1)}, u32[]{:S(2)}, u32[]{:S(2)}) %collective-permute-start.23) | collective-permute-done | bytes 163872 | tf_op jit(solution)/shard_map/ppermute | solution.py:53
  94.9 12.7 %all_to_all.23.slabs_ref = f32[8,40,128]{2,1,0:T(8,128)S(1)} all-to-all(f32[8,40,128]{2,1,0:T(8,128)S(1)} %bitcast.7), channel_id=1, replica_groups={{0,8,16,24,32,40,48,56},{4,12,20,28,36,44,52,60},{64,72,80,88,96,104,11..., dimensions={0} | all-to-all | bytes 327680 | tf_op jit(solution)/shard_map/all_to_all | solution.py:62
  107.6 0.6 last.1
  (13 shorter events, 0.1 us)
Async XLA Ops:
  0.0 9.1 %copy-start.3 = (s32[8]{0:T(128)S(1)}, s32[8]{0:T(128)}, u32[]{:S(2)}) copy-start(s32[8]{0:T(128)} %depth_ref.1) | copy-start | bytes 100
  0.0 9.1 %copy-start.4 = (s32[8]{0:T(128)S(1)}, s32[8]{0:T(128)}, u32[]{:S(2)}) copy-start(s32[8]{0:T(128)} %newton_ref.1) | copy-start | bytes 100
  1.9 30.4 %copy-start = (bf16[30,30,512]{2,1,0:T(8,128)(2,1)S(1)}, bf16[30,30,512]{2,1,0:T(8,128)(2,1)}, u32[]{:S(2)}) copy-start(bf16[30,30,512]{2,1,0:T(8,128)(2,1)} %inv_ref.3) | copy-start | bytes 2764804
  1.9 7.7 %collective-permute-start.2 = (f32[168,128]{1,0:T(8,128)S(1)}, f32[168,128]{1,0:T(8,128)S(1)}, u32[]{:S(2)}, u32[]{:S(2)}) collective-permute-start(f32[168,128]{1,0:T(8,128)S(1)} %get-tuple-element.50.raw0), channel_id=1, source_target_pairs={{0,128},{4,132},{8,136},{12,140},{16,144},{20,148},{24,152},{28,15... | collective-permute-start | bytes 258056 | tf_op jit(solution)/shard_map/ppermute | solution.py:49
  5.1 4.9 %collective-permute-start.1 = (f32[168,128]{1,0:T(8,128)S(1)}, f32[168,128]{1,0:T(8,128)S(1)}, u32[]{:S(2)}, u32[]{:S(2)}) collective-permute-start(f32[168,128]{1,0:T(8,128)S(1)} %get-tuple-element.50.raw0), channel_id=1, source_target_pairs={{0,192},{4,196},{8,200},{12,204},{16,208},{20,212},{24,216},{28,22... | collective-permute-start | bytes 258056 | tf_op jit(solution)/shard_map/ppermute | solution.py:49
  6.2 5.7 %collective-permute-start = (f32[168,128]{1,0:T(8,128)S(1)}, f32[168,128]{1,0:T(8,128)S(1)}, u32[]{:S(2)}, u32[]{:S(2)}) collective-permute-start(f32[168,128]{1,0:T(8,128)S(1)} %get-tuple-element.50.raw0), channel_id=1, source_target_pairs={{0,64},{4,68},{8,72},{12,76},{16,80},{20,84},{24,88},{28,92},{32,9... | collective-permute-start | bytes 258056 | tf_op jit(solution)/shard_map/ppermute | solution.py:49
  7.1 5.2 %collective-permute-start.3 = (f32[40,128]{1,0:T(8,128)S(1)}, f32[40,128]{1,0:T(8,128)S(1)}, u32[]{:S(2)}, u32[]{:S(2)}) collective-permute-start(f32[40,128]{1,0:T(8,128)S(1)} %get-tuple-element.61), channel_id=1, source_target_pairs={{0,1},{1,2},{2,3},{3,0},{4,5},{5,6},{6,7},{7,4},{8,9},{9,10},{10,1... | collective-permute-start | bytes 61448 | tf_op jit(solution)/shard_map/ppermute | solution.py:57
  7.3 5.0 %collective-permute-start.4 = (f32[40,128]{1,0:T(8,128)S(1)}, f32[40,128]{1,0:T(8,128)S(1)}, u32[]{:S(2)}, u32[]{:S(2)}) collective-permute-start(f32[40,128]{1,0:T(8,128)S(1)} %get-tuple-element.62), channel_id=1, source_target_pairs={{0,3},{1,0},{2,1},{3,2},{4,7},{5,4},{6,5},{7,6},{8,11},{9,8},{10,9... | collective-permute-start | bytes 61448 | tf_op jit(solution)/shard_map/ppermute | solution.py:57
  12.3 1.5 %collective-permute-start.5 = (f32[320,128]{1,0:T(8,128)S(1)}, f32[320,128]{1,0:T(8,128)S(1)}, u32[]{:S(2)}, u32[]{:S(2)}) collective-permute-start(f32[320,128]{1,0:T(8,128)S(1)} %get-tuple-element.63), channel_id=1, source_target_pairs={{0,4},{4,0},{8,12},{12,8},{16,20},{20,16},{24,28},{28,24},{32,36},... | collective-permute-start | bytes 491528 | tf_op jit(solution)/shard_map/ppermute | solution.py:53
  13.8 18.5 %copy-start.2 = (bf16[10,10,512]{2,1,0:T(8,128)(2,1)S(1)}, bf16[10,10,512]{2,1,0:T(8,128)(2,1)}, u32[]{:S(2)}) copy-start(bf16[10,10,512]{2,1,0:T(8,128)(2,1)} %jac_ref.3) | copy-start | bytes 307204
  34.0 23.6 %copy-start.1 = (bf16[4,7,128,128]{3,2,1,0:T(8,128)(2,1)S(1)}, bf16[4,7,128,128]{3,2,1,0:T(8,128)(2,1)}, u32[]{:S(2)}) copy-start(bf16[4,7,128,128]{3,2,1,0:T(8,128)(2,1)} %tiles_ref.1) | copy-start | bytes 2752516
  34.0 6.1 %collective-permute-start.8 = (f32[160,128]{1,0:T(8,128)S(1)}, f32[160,128]{1,0:T(8,128)S(1)}, u32[]{:S(2)}, u32[]{:S(2)}) collective-permute-start(f32[160,128]{1,0:T(8,128)S(1)} %get-tuple-element.68.raw0), channel_id=1, source_target_pairs={{0,128},{4,132},{8,136},{12,140},{16,144},{20,148},{24,152},{28,15... | collective-permute-start | bytes 245768 | tf_op jit(solution)/shard_map/ppermute | solution.py:49
  34.9 5.6 %collective-permute-start.7 = (f32[160,128]{1,0:T(8,128)S(1)}, f32[160,128]{1,0:T(8,128)S(1)}, u32[]{:S(2)}, u32[]{:S(2)}) collective-permute-start(f32[160,128]{1,0:T(8,128)S(1)} %get-tuple-element.68.raw0), channel_id=1, source_target_pairs={{0,192},{4,196},{8,200},{12,204},{16,208},{20,212},{24,216},{28,22... | collective-permute-start | bytes 245768 | tf_op jit(solution)/shard_map/ppermute | solution.py:49
  37.3 5.7 %collective-permute-start.6 = (f32[160,128]{1,0:T(8,128)S(1)}, f32[160,128]{1,0:T(8,128)S(1)}, u32[]{:S(2)}, u32[]{:S(2)}) collective-permute-start(f32[160,128]{1,0:T(8,128)S(1)} %get-tuple-element.68.raw0), channel_id=1, source_target_pairs={{0,64},{4,68},{8,72},{12,76},{16,80},{20,84},{24,88},{28,92},{32,9... | collective-permute-start | bytes 245768 | tf_op jit(solution)/shard_map/ppermute | solution.py:49
  37.3 6.0 %collective-permute-start.9 = (f32[40,128]{1,0:T(8,128)S(1)}, f32[40,128]{1,0:T(8,128)S(1)}, u32[]{:S(2)}, u32[]{:S(2)}) collective-permute-start(f32[40,128]{1,0:T(8,128)S(1)} %get-tuple-element.71), channel_id=1, source_target_pairs={{0,1},{1,2},{2,3},{3,0},{4,5},{5,6},{6,7},{7,4},{8,9},{9,10},{10,1... | collective-permute-start | bytes 61448 | tf_op jit(solution)/shard_map/ppermute | solution.py:57
  37.7 5.7 %collective-permute-start.10 = (f32[40,128]{1,0:T(8,128)S(1)}, f32[40,128]{1,0:T(8,128)S(1)}, u32[]{:S(2)}, u32[]{:S(2)}) collective-permute-start(f32[40,128]{1,0:T(8,128)S(1)} %get-tuple-element.72), channel_id=1, source_target_pairs={{0,3},{1,0},{2,1},{3,2},{4,7},{5,4},{6,5},{7,6},{8,11},{9,8},{10,9... | collective-permute-start | bytes 61448 | tf_op jit(solution)/shard_map/ppermute | solution.py:57
  43.3 1.5 %collective-permute-start.11 = (f32[320,128]{1,0:T(8,128)S(1)}, f32[320,128]{1,0:T(8,128)S(1)}, u32[]{:S(2)}, u32[]{:S(2)}) collective-permute-start(f32[320,128]{1,0:T(8,128)S(1)} %get-tuple-element.73), channel_id=1, source_target_pairs={{0,4},{4,0},{8,12},{12,8},{16,20},{20,16},{24,28},{28,24},{32,36},... | collective-permute-start | bytes 491528 | tf_op jit(solution)/shard_map/ppermute | solution.py:53
  57.9 6.5 %collective-permute-start.14 = (f32[160,128]{1,0:T(8,128)S(1)}, f32[160,128]{1,0:T(8,128)S(1)}, u32[]{:S(2)}, u32[]{:S(2)}) collective-permute-start(f32[160,128]{1,0:T(8,128)S(1)} %get-tuple-element.77.raw0), channel_id=1, source_target_pairs={{0,128},{4,132},{8,136},{12,140},{16,144},{20,148},{24,152},{28,15... | collective-permute-start | bytes 245768 | tf_op jit(solution)/shard_map/ppermute | solution.py:49
  59.5 5.1 %collective-permute-start.13 = (f32[160,128]{1,0:T(8,128)S(1)}, f32[160,128]{1,0:T(8,128)S(1)}, u32[]{:S(2)}, u32[]{:S(2)}) collective-permute-start(f32[160,128]{1,0:T(8,128)S(1)} %get-tuple-element.77.raw0), channel_id=1, source_target_pairs={{0,192},{4,196},{8,200},{12,204},{16,208},{20,212},{24,216},{28,22... | collective-permute-start | bytes 245768 | tf_op jit(solution)/shard_map/ppermute | solution.py:49
  61.9 5.7 %collective-permute-start.12 = (f32[160,128]{1,0:T(8,128)S(1)}, f32[160,128]{1,0:T(8,128)S(1)}, u32[]{:S(2)}, u32[]{:S(2)}) collective-permute-start(f32[160,128]{1,0:T(8,128)S(1)} %get-tuple-element.77.raw0), channel_id=1, source_target_pairs={{0,64},{4,68},{8,72},{12,76},{16,80},{20,84},{24,88},{28,92},{32,9... | collective-permute-start | bytes 245768 | tf_op jit(solution)/shard_map/ppermute | solution.py:49
  61.9 6.0 %collective-permute-start.15 = (f32[40,128]{1,0:T(8,128)S(1)}, f32[40,128]{1,0:T(8,128)S(1)}, u32[]{:S(2)}, u32[]{:S(2)}) collective-permute-start(f32[40,128]{1,0:T(8,128)S(1)} %get-tuple-element.80), channel_id=1, source_target_pairs={{0,1},{1,2},{2,3},{3,0},{4,5},{5,6},{6,7},{7,4},{8,9},{9,10},{10,1... | collective-permute-start | bytes 61448 | tf_op jit(solution)/shard_map/ppermute | solution.py:57
  62.2 5.6 %collective-permute-start.16 = (f32[40,128]{1,0:T(8,128)S(1)}, f32[40,128]{1,0:T(8,128)S(1)}, u32[]{:S(2)}, u32[]{:S(2)}) collective-permute-start(f32[40,128]{1,0:T(8,128)S(1)} %get-tuple-element.81), channel_id=1, source_target_pairs={{0,3},{1,0},{2,1},{3,2},{4,7},{5,4},{6,5},{7,6},{8,11},{9,8},{10,9... | collective-permute-start | bytes 61448 | tf_op jit(solution)/shard_map/ppermute | solution.py:57
  67.9 1.5 %collective-permute-start.17 = (f32[320,128]{1,0:T(8,128)S(1)}, f32[320,128]{1,0:T(8,128)S(1)}, u32[]{:S(2)}, u32[]{:S(2)}) collective-permute-start(f32[320,128]{1,0:T(8,128)S(1)} %get-tuple-element.82), channel_id=1, source_target_pairs={{0,4},{4,0},{8,12},{12,8},{16,20},{20,16},{24,28},{28,24},{32,36},... | collective-permute-start | bytes 491528 | tf_op jit(solution)/shard_map/ppermute | solution.py:53
  83.8 6.6 %collective-permute-start.20 = (f32[160,128]{1,0:T(8,128)S(1)}, f32[160,128]{1,0:T(8,128)S(1)}, u32[]{:S(2)}, u32[]{:S(2)}) collective-permute-start(f32[160,128]{1,0:T(8,128)S(1)} %get-tuple-element.86.raw0), channel_id=1, source_target_pairs={{0,128},{4,132},{8,136},{12,140},{16,144},{20,148},{24,152},{28,15... | collective-permute-start | bytes 245768 | tf_op jit(solution)/shard_map/ppermute | solution.py:49
  84.8 5.7 %collective-permute-start.19 = (f32[160,128]{1,0:T(8,128)S(1)}, f32[160,128]{1,0:T(8,128)S(1)}, u32[]{:S(2)}, u32[]{:S(2)}) collective-permute-start(f32[160,128]{1,0:T(8,128)S(1)} %get-tuple-element.86.raw0), channel_id=1, source_target_pairs={{0,192},{4,196},{8,200},{12,204},{16,208},{20,212},{24,216},{28,22... | collective-permute-start | bytes 245768 | tf_op jit(solution)/shard_map/ppermute | solution.py:49
  87.3 5.7 %collective-permute-start.18 = (f32[160,128]{1,0:T(8,128)S(1)}, f32[160,128]{1,0:T(8,128)S(1)}, u32[]{:S(2)}, u32[]{:S(2)}) collective-permute-start(f32[160,128]{1,0:T(8,128)S(1)} %get-tuple-element.86.raw0), channel_id=1, source_target_pairs={{0,64},{4,68},{8,72},{12,76},{16,80},{20,84},{24,88},{28,92},{32,9... | collective-permute-start | bytes 245768 | tf_op jit(solution)/shard_map/ppermute | solution.py:49
  87.3 6.0 %collective-permute-start.21 = (f32[40,128]{1,0:T(8,128)S(1)}, f32[40,128]{1,0:T(8,128)S(1)}, u32[]{:S(2)}, u32[]{:S(2)}) collective-permute-start(f32[40,128]{1,0:T(8,128)S(1)} %get-tuple-element.89), channel_id=1, source_target_pairs={{0,1},{1,2},{2,3},{3,0},{4,5},{5,6},{6,7},{7,4},{8,9},{9,10},{10,1... | collective-permute-start | bytes 61448 | tf_op jit(solution)/shard_map/ppermute | solution.py:57
  87.4 6.0 %collective-permute-start.22 = (f32[40,128]{1,0:T(8,128)S(1)}, f32[40,128]{1,0:T(8,128)S(1)}, u32[]{:S(2)}, u32[]{:S(2)}) collective-permute-start(f32[40,128]{1,0:T(8,128)S(1)} %get-tuple-element.90), channel_id=1, source_target_pairs={{0,3},{1,0},{2,1},{3,2},{4,7},{5,4},{6,5},{7,6},{8,11},{9,8},{10,9... | collective-permute-start | bytes 61448 | tf_op jit(solution)/shard_map/ppermute | solution.py:57
  93.4 1.5 %collective-permute-start.23 = (f32[320,128]{1,0:T(8,128)S(1)}, f32[320,128]{1,0:T(8,128)S(1)}, u32[]{:S(2)}, u32[]{:S(2)}) collective-permute-start(f32[320,128]{1,0:T(8,128)S(1)} %get-tuple-element.91), channel_id=1, source_target_pairs={{0,4},{4,0},{8,12},{12,8},{16,20},{20,16},{24,28},{28,24},{32,36},... | collective-permute-start | bytes 491528 | tf_op jit(solution)/shard_map/ppermute | solution.py:53

commit v6 on v4

--- a/solution.py
+++ b/solution.py
@@ -63,8 +63,8 @@
 
 def emit_terms(blocks, tiles_ref, raw_ref, own_ref, north_ref, south_ref, ready=None):
     for r in range(RB):
-        if ready is not None:
-            ready[r].wait()
+        for copy in ready[r] if ready else ():
+            copy.wait()
         padded = jnp.concatenate([blocks[r], jnp.zeros((16 - TR, BLK), F32)], axis=0)
         left = padded.astype(jnp.bfloat16)
         for t in range(NB):
@@ -81,9 +81,11 @@
 
 
 def first_kernel(
-    field_far, impl_dest_far, impl_local_far, expl_dest_far, expl_local_far, tiles_far,
-    raw_ref, own_ref, north_ref, south_ref,
-    field_ref, impl_dest, impl_local, expl_dest, expl_local, tiles_ref, arrivals, tile_arrivals,
+    field_far, impl_dest_far, impl_local_far, expl_dest_far, expl_local_far, depth_far, newton_far,
+    tiles_far,
+    raw_ref, own_ref, north_ref, south_ref, mask_ref, sweeps_ref,
+    field_ref, impl_dest, impl_local, expl_dest, expl_local, depth_ref, newton_ref,
+    tiles_ref, arrivals, tile_arrivals,
 ):
     copies = [
         pltpu.make_async_copy(far, near, arrivals.at[i])
@@ -94,15 +96,23 @@
                 (impl_local_far, impl_local),
                 (expl_dest_far, expl_dest),
                 (expl_local_far, expl_local),
+                (depth_far, depth_ref),
+                (newton_far, newton_ref),
             )
         )
     ]
     tile_copies = [
-        pltpu.make_async_copy(tiles_far.at[r], tiles_ref.at[r], tile_arrivals.at[r])
+        [
+            pltpu.make_async_copy(tiles_far.at[r, t], tiles_ref.at[r, t], tile_arrivals.at[r, t])
+            for t in range(NB)
+        ]
         for r in range(RB)
     ]
-    for copy in copies + tile_copies:
+    for copy in copies:
         copy.start()
+    for row in tile_copies:
+        for copy in row:
+            copy.start()
     raw_ref[TERMS * TR :, :] = jnp.zeros((2 * RB, BLK), F32)
     for copy in copies:
         copy.wait()
@@ -110,6 +120,7 @@
     expl_codes = expl_dest[...] * RB + expl_local[...]
     raw_ref[TERMS * TR : TERMS * TR + RB, :NBAND] = impl_codes.astype(F32)
     raw_ref[TERMS * TR + RB :, :NBAND] = expl_codes.astype(F32)
+    write_masks(depth_ref, newton_ref, mask_ref, sweeps_ref)
     blocks = [field_ref[:, r * BLK : (r + 1) * BLK] for r in range(RB)]
     emit_terms(blocks, tiles_ref, raw_ref, own_ref, north_ref, south_ref, tile_copies)
 
@@ -128,7 +139,7 @@
         expl_ref[source * RB : (source + 1) * RB, :] = slot[RB:, :NBAND]
 
 
-def masks_kernel(depth_ref, newton_ref, mask_ref, sweeps_ref):
+def write_masks(depth_ref, newton_ref, mask_ref, sweeps_ref):
     lat = lax.axis_index("lat")
     lane = lax.broadcasted_iota(jnp.int32, (1, BLK), 1)
     first = lane < LEV
@@ -276,33 +287,35 @@
         slabs = exchange_z((mine + swap_core(other)).reshape(NZ, SLAB, BLK))
         return [masks, slabs, own, below, above]
 
-    first_shapes = (struct(TERMS * TR + 2 * RB, BLK),) + TERM_SHAPES[1:]
-    terms = call(
+    far_inputs = (adjoint, impl_dest, impl_local, expl_dest, expl_local)
+    far_inputs += (column_depth, newton, impl_tiles)
+    first_shapes = (struct(TERMS * TR + 2 * RB, BLK),) + TERM_SHAPES[1:] + (
+        struct(RB + 2, BLK),
+        jax.ShapeDtypeStruct((RB, BLK), jnp.int32),
+    )
+    raw, own, north, south, masks, sweeps = call(
         first_kernel,
         first_shapes,
         [
             pltpu.with_memory_space_constraint(value, pltpu.HBM)
-            for value in (adjoint, impl_dest, impl_local, expl_dest, expl_local, impl_tiles)
+            for value in far_inputs
         ],
         0,
         "first",
-        far=6,
+        far=8,
         scratch=[
             pltpu.VMEM((TR, RB * BLK), F32),
             *[pltpu.VMEM((RB, NBAND), jnp.int32)] * 4,
+            *[pltpu.SMEM((RB * BLK // LEV,), jnp.int32)] * 2,
             pltpu.VMEM((RB, NB, BLK, BLK), jnp.bfloat16),
-            pltpu.SemaphoreType.DMA((5,)),
-            pltpu.SemaphoreType.DMA((RB,)),
+            pltpu.SemaphoreType.DMA((7,)),
+            pltpu.SemaphoreType.DMA((RB, NB)),
         ],
     )
-    int_table = jax.ShapeDtypeStruct((RB, BLK), jnp.int32)
-    masks, sweeps = call(
-        masks_kernel, (struct(RB + 2, BLK), int_table), [column_depth, newton], 2, "masks"
-    )
-    raws = gather_x(terms[0])
-    *raws, masks, sweeps = lax.optimization_barrier((*raws, masks, sweeps))
+    raws = gather_x(raw)
     slot_table = jax.ShapeDtypeStruct((NX * RB, NBAND), jnp.int32)
-    slots = call(slots_kernel, (slot_table, slot_table), [terms[0], *raws], 0, "slots")
+    terms = (raw, own, north, south)
+    slots = call(slots_kernel, (slot_table, slot_table), [raw, *raws], 0, "slots")
     for step_index in range(STEPS):
         if step_index:
             raws = gather_x(terms[0])

time: 107 us -> 107 us (level)
    pallas_call x11 -> x10, Pallas kernels: 7.14 us -> 6.82 us  [call(): pl.pallas_call(kernel, out_shape=out_shape, in_specs=[SMEM] * smem + [VME...]
  transfers between devices with their start and end apart: 24 -> 24, of which waited for: 12 -> 12; matrix products, arithmetic and copies ran while one was open for 0% -> 0% of each run, Pallas kernels for 2% -> 1%
where the time goes in v6:
time: 107 us
  blocking collectives  56.7 us (53%)
  starting transfers between devices  23.5 us (22%)
  waiting for transfers between devices  19.9 us (19%)
  Pallas kernels  6.82 us (6%)
    all_to_all x4, blocking collectives, exchange_z(): lax.all_to_all(value, 'cols', 0, 0, axis_index_groups=groups, tiled=True)  56.7 us
    ppermute x12, starting transfers between devices, shift_x(): return lax.ppermute(value, 'cols', pairs)  15 us
    ppermute x12, waiting for transfers between devices, shift_x(): return lax.ppermute(value, 'cols', pairs)  14.4 us
    ppermute x8, starting transfers between devices, ring_lat(): lax.ppermute(value, 'lat', [(i, (i + steps) % N_LAT) for i in range(N_LAT)])  8.1 us
    pallas_call x10, Pallas kernels, call(): pl.pallas_call(kernel, out_shape=out_shape, in_specs=[SMEM] * smem + [VME...  6.82 us
    ppermute x4, waiting for transfers between devices, swap_core(): lax.ppermute(value, 'cols', [(i, i ^ 1) for i in range(NX * NZ * NCORE)])  5.53 us
  transfers between devices with their start and end apart: 24, of which 12 were waited for; matrix products, arithmetic and copies ran while one was open for 0% of the time, Pallas kernels for 1%

profile of v6, /device:TPU:24, one launch (start us, length us, event | category | flops | bytes accessed | tf_op | source)
XLA Modules:
  0.0 107.2 jit_solution(3411476378246453022)
XLA Ops:
  0.0 2.3 %first.1 = (f32[168,128]{1,0:T(8,128)S(1)}, f32[40,128]{1,0:T(8,128)S(1)}, f32[40,128]{1,0:T(8,128)S(1)}, f32[40,128]{1,0:T(8,128)S(1)}, f32[6,128]{1,0:T(8,128)S(1)}, /*index=5*/s32[4,128]{1,0:T(4,128)S(1)}) custom-call(f32[10,512]{1,0:T(8,128)} %field_far.1, s32[4,4]{1,0:T(4,128)} %impl_dest_far.1, s32[4,4]{1,0:T(4,128)} %impl_local_far.1, ...), custom_call_target="tpu_custom_call" | custom-call | bytes 938304 | tf_op jit(solution)/shard_map/first/pallas_call | solution.py:250
  2.3 0.0 copy-start
  2.3 2.8 %collective-permute-start.2 = (f32[168,128]{1,0:T(8,128)S(1)}, f32[168,128]{1,0:T(8,128)S(1)}, u32[]{:S(2)}, u32[]{:S(2)}) collective-permute-start(f32[168,128]{1,0:T(8,128)S(1)} %get-tuple-element.46.raw0), channel_id=1, source_target_pairs={{0,192},{4,196},{8,200},{12,204},{16,208},{20,212},{24,216},{28,22... | collective-permute-start | bytes 258056 | tf_op jit(solution)/shard_map/ppermute | solution.py:48
  5.1 0.8 collective-permute-start.1
  5.9 0.9 collective-permute-start
  6.8 0.2 collective-permute-start.3
  7.0 1.8 %collective-permute-start.4 = (f32[40,128]{1,0:T(8,128)S(1)}, f32[40,128]{1,0:T(8,128)S(1)}, u32[]{:S(2)}, u32[]{:S(2)}) collective-permute-start(f32[40,128]{1,0:T(8,128)S(1)} %get-tuple-element.52), channel_id=1, source_target_pairs={{0,3},{1,0},{2,1},{3,2},{4,7},{5,4},{6,5},{7,6},{8,11},{9,8},{10,9... | collective-permute-start | bytes 61448 | tf_op jit(solution)/shard_map/ppermute | solution.py:56
  8.8 0.0 collective-permute-done.2.raw3
  8.8 2.8 %collective-permute-done.1.raw2 = f32[168,128]{1,0:T(8,128)S(1)} collective-permute-done((f32[168,128]{1,0:T(8,128)S(1)}, f32[168,128]{1,0:T(8,128)S(1)}, u32[]{:S(2)}, u32[]{:S(2)}) %collective-permute-start.1) | collective-permute-done | bytes 86048 | tf_op jit(solution)/shard_map/ppermute | solution.py:48
  11.6 0.9 collective-permute-done.raw1
  12.5 0.4 merge.4
  12.9 0.0 collective-permute-done.3.below_ref
  12.9 0.0 collective-permute-done.4.above_ref
  12.9 0.1 collective-permute-start.5
  13.0 1.4 %collective-permute-done.5 = f32[320,128]{1,0:T(8,128)S(1)} collective-permute-done((f32[320,128]{1,0:T(8,128)S(1)}, f32[320,128]{1,0:T(8,128)S(1)}, u32[]{:S(2)}, u32[]{:S(2)}) %collective-permute-start.5) | collective-permute-done | bytes 163872 | tf_op jit(solution)/shard_map/ppermute | solution.py:52
  14.4 0.0 copy-start.3
  14.4 18.5 %all_to_all.20.slabs_ref = f32[8,40,128]{2,1,0:T(8,128)S(1)} all-to-all(f32[8,40,128]{2,1,0:T(8,128)S(1)} %bitcast.4), channel_id=1, replica_groups={{0,8,16,24,32,40,48,56},{4,12,20,28,36,44,52,60},{64,72,80,88,96,104,11..., dimensions={0} | all-to-all | bytes 327680 | tf_op jit(solution)/shard_map/all_to_all | solution.py:61
  32.9 0.0 copy-done.2
  32.9 1.1 %react.2 = (f32[160,128]{1,0:T(8,128)S(1)}, f32[40,128]{1,0:T(8,128)S(1)}, f32[40,128]{1,0:T(8,128)S(1)}, f32[40,128]{1,0:T(8,128)S(1)}) custom-call(f32[6,128]{1,0:T(8,128)S(1)} %get-tuple-element.45.mask_ref, f32[8,40,128]{2,1,0:T(8,128)S(1)} %all_to_all.20.slabs_ref, f32[40,128]{1,0:T(8,128)S(1)} %get-tuple-element.54.own_in, ...), custom_call_target="tpu_custom_call" | custom-call | bytes 2171904 | tf_op jit(solution)/shard_map/react/pallas_call | solution.py:250
  34.0 1.5 %collective-permute-start.8 = (f32[160,128]{1,0:T(8,128)S(1)}, f32[160,128]{1,0:T(8,128)S(1)}, u32[]{:S(2)}, u32[]{:S(2)}) collective-permute-start(f32[160,128]{1,0:T(8,128)S(1)} %get-tuple-element.58.raw0), channel_id=1, source_target_pairs={{0,192},{4,196},{8,200},{12,204},{16,208},{20,212},{24,216},{28,22... | collective-permute-start | bytes 245768 | tf_op jit(solution)/shard_map/ppermute | solution.py:48
  35.4 1.5 %collective-permute-start.7 = (f32[160,128]{1,0:T(8,128)S(1)}, f32[160,128]{1,0:T(8,128)S(1)}, u32[]{:S(2)}, u32[]{:S(2)}) collective-permute-start(f32[160,128]{1,0:T(8,128)S(1)} %get-tuple-element.58.raw0), channel_id=1, source_target_pairs={{0,128},{4,132},{8,136},{12,140},{16,144},{20,148},{24,152},{28,15... | collective-permute-start | bytes 245768 | tf_op jit(solution)/shard_map/ppermute | solution.py:48
  37.0 0.0 collective-permute-start.6
  37.0 0.4 collective-permute-start.9
  37.3 1.7 %collective-permute-start.10 = (f32[40,128]{1,0:T(8,128)S(1)}, f32[40,128]{1,0:T(8,128)S(1)}, u32[]{:S(2)}, u32[]{:S(2)}) collective-permute-start(f32[40,128]{1,0:T(8,128)S(1)} %get-tuple-element.62), channel_id=1, source_target_pairs={{0,3},{1,0},{2,1},{3,2},{4,7},{5,4},{6,5},{7,6},{8,11},{9,8},{10,9... | collective-permute-start | bytes 61448 | tf_op jit(solution)/shard_map/ppermute | solution.py:56
  39.0 0.0 collective-permute-done.8.raw3
  39.0 2.4 %collective-permute-done.7.raw2 = f32[160,128]{1,0:T(8,128)S(1)} collective-permute-done((f32[160,128]{1,0:T(8,128)S(1)}, f32[160,128]{1,0:T(8,128)S(1)}, u32[]{:S(2)}, u32[]{:S(2)}) %collective-permute-start.7) | collective-permute-done | bytes 81952 | tf_op jit(solution)/shard_map/ppermute | solution.py:48
  41.4 1.2 %collective-permute-done.6.raw1 = f32[160,128]{1,0:T(8,128)S(1)} collective-permute-done((f32[160,128]{1,0:T(8,128)S(1)}, f32[160,128]{1,0:T(8,128)S(1)}, u32[]{:S(2)}, u32[]{:S(2)}) %collective-permute-start.6) | collective-permute-done | bytes 81952 | tf_op jit(solution)/shard_map/ppermute | solution.py:48
  42.6 0.3 merge.5
  43.0 0.0 collective-permute-done.9.below_ref
  43.0 0.0 collective-permute-done.10.above_ref
  43.0 0.1 collective-permute-start.11
  43.1 1.4 %collective-permute-done.11 = f32[320,128]{1,0:T(8,128)S(1)} collective-permute-done((f32[320,128]{1,0:T(8,128)S(1)}, f32[320,128]{1,0:T(8,128)S(1)}, u32[]{:S(2)}, u32[]{:S(2)}) %collective-permute-start.11) | collective-permute-done | bytes 163872 | tf_op jit(solution)/shard_map/ppermute | solution.py:52
  44.5 12.7 %all_to_all.21.slabs_ref = f32[8,40,128]{2,1,0:T(8,128)S(1)} all-to-all(f32[8,40,128]{2,1,0:T(8,128)S(1)} %bitcast.5), channel_id=1, replica_groups={{0,8,16,24,32,40,48,56},{4,12,20,28,36,44,52,60},{64,72,80,88,96,104,11..., dimensions={0} | all-to-all | bytes 327680 | tf_op jit(solution)/shard_map/all_to_all | solution.py:61
  57.2 0.3 step.1
  57.6 2.5 %collective-permute-start.14 = (f32[160,128]{1,0:T(8,128)S(1)}, f32[160,128]{1,0:T(8,128)S(1)}, u32[]{:S(2)}, u32[]{:S(2)}) collective-permute-start(f32[160,128]{1,0:T(8,128)S(1)} %get-tuple-element.67.raw0), channel_id=1, source_target_pairs={{0,192},{4,196},{8,200},{12,204},{16,208},{20,212},{24,216},{28,22... | collective-permute-start | bytes 245768 | tf_op jit(solution)/shard_map/ppermute | solution.py:48
  60.1 0.8 collective-permute-start.13
  60.9 0.5 collective-permute-start.12
  61.4 0.4 collective-permute-start.15
  61.7 1.7 %collective-permute-start.16 = (f32[40,128]{1,0:T(8,128)S(1)}, f32[40,128]{1,0:T(8,128)S(1)}, u32[]{:S(2)}, u32[]{:S(2)}) collective-permute-start(f32[40,128]{1,0:T(8,128)S(1)} %get-tuple-element.71), channel_id=1, source_target_pairs={{0,3},{1,0},{2,1},{3,2},{4,7},{5,4},{6,5},{7,6},{8,11},{9,8},{10,9... | collective-permute-start | bytes 61448 | tf_op jit(solution)/shard_map/ppermute | solution.py:56
  63.4 0.0 collective-permute-done.14.raw3
  63.4 2.7 %collective-permute-done.13.raw2 = f32[160,128]{1,0:T(8,128)S(1)} collective-permute-done((f32[160,128]{1,0:T(8,128)S(1)}, f32[160,128]{1,0:T(8,128)S(1)}, u32[]{:S(2)}, u32[]{:S(2)}) %collective-permute-start.13) | collective-permute-done | bytes 81952 | tf_op jit(solution)/shard_map/ppermute | solution.py:48
  66.1 0.8 collective-permute-done.12.raw1
  66.9 0.4 merge.6
  67.3 0.0 collective-permute-done.15.below_ref
  67.3 0.0 collective-permute-done.16.above_ref
  67.3 0.1 collective-permute-start.17
  67.4 1.4 %collective-permute-done.17 = f32[320,128]{1,0:T(8,128)S(1)} collective-permute-done((f32[320,128]{1,0:T(8,128)S(1)}, f32[320,128]{1,0:T(8,128)S(1)}, u32[]{:S(2)}, u32[]{:S(2)}) %collective-permute-start.17) | collective-permute-done | bytes 163872 | tf_op jit(solution)/shard_map/ppermute | solution.py:52
  68.8 12.7 %all_to_all.22.slabs_ref = f32[8,40,128]{2,1,0:T(8,128)S(1)} all-to-all(f32[8,40,128]{2,1,0:T(8,128)S(1)} %bitcast.6), channel_id=1, replica_groups={{0,8,16,24,32,40,48,56},{4,12,20,28,36,44,52,60},{64,72,80,88,96,104,11..., dimensions={0} | all-to-all | bytes 327680 | tf_op jit(solution)/shard_map/all_to_all | solution.py:61
  81.6 1.1 react.3
  82.6 2.2 %collective-permute-start.20 = (f32[160,128]{1,0:T(8,128)S(1)}, f32[160,128]{1,0:T(8,128)S(1)}, u32[]{:S(2)}, u32[]{:S(2)}) collective-permute-start(f32[160,128]{1,0:T(8,128)S(1)} %get-tuple-element.76.raw0), channel_id=1, source_target_pairs={{0,192},{4,196},{8,200},{12,204},{16,208},{20,212},{24,216},{28,22... | collective-permute-start | bytes 245768 | tf_op jit(solution)/shard_map/ppermute | solution.py:48
  84.8 1.5 %collective-permute-start.19 = (f32[160,128]{1,0:T(8,128)S(1)}, f32[160,128]{1,0:T(8,128)S(1)}, u32[]{:S(2)}, u32[]{:S(2)}) collective-permute-start(f32[160,128]{1,0:T(8,128)S(1)} %get-tuple-element.76.raw0), channel_id=1, source_target_pairs={{0,128},{4,132},{8,136},{12,140},{16,144},{20,148},{24,152},{28,15... | collective-permute-start | bytes 245768 | tf_op jit(solution)/shard_map/ppermute | solution.py:48
  86.3 0.0 collective-permute-start.18
  86.3 0.1 collective-permute-start.21
  86.4 2.0 %collective-permute-start.22 = (f32[40,128]{1,0:T(8,128)S(1)}, f32[40,128]{1,0:T(8,128)S(1)}, u32[]{:S(2)}, u32[]{:S(2)}) collective-permute-start(f32[40,128]{1,0:T(8,128)S(1)} %get-tuple-element.80), channel_id=1, source_target_pairs={{0,3},{1,0},{2,1},{3,2},{4,7},{5,4},{6,5},{7,6},{8,11},{9,8},{10,9... | collective-permute-start | bytes 61448 | tf_op jit(solution)/shard_map/ppermute | solution.py:56
  88.3 0.0 collective-permute-done.20.raw3
  88.3 2.4 %collective-permute-done.19.raw2 = f32[160,128]{1,0:T(8,128)S(1)} collective-permute-done((f32[160,128]{1,0:T(8,128)S(1)}, f32[160,128]{1,0:T(8,128)S(1)}, u32[]{:S(2)}, u32[]{:S(2)}) %collective-permute-start.19) | collective-permute-done | bytes 81952 | tf_op jit(solution)/shard_map/ppermute | solution.py:48
  90.7 1.2 %collective-permute-done.18.raw1 = f32[160,128]{1,0:T(8,128)S(1)} collective-permute-done((f32[160,128]{1,0:T(8,128)S(1)}, f32[160,128]{1,0:T(8,128)S(1)}, u32[]{:S(2)}, u32[]{:S(2)}) %collective-permute-start.18) | collective-permute-done | bytes 81952 | tf_op jit(solution)/shard_map/ppermute | solution.py:48
  92.0 0.3 merge.7
  92.3 0.0 collective-permute-done.21.below_ref
  92.3 0.0 collective-permute-done.22.above_ref
  92.3 0.1 collective-permute-start.23
  92.4 1.4 %collective-permute-done.23 = f32[320,128]{1,0:T(8,128)S(1)} collective-permute-done((f32[320,128]{1,0:T(8,128)S(1)}, f32[320,128]{1,0:T(8,128)S(1)}, u32[]{:S(2)}, u32[]{:S(2)}) %collective-permute-start.23) | collective-permute-done | bytes 163872 | tf_op jit(solution)/shard_map/ppermute | solution.py:52
  93.8 12.7 %all_to_all.23.slabs_ref = f32[8,40,128]{2,1,0:T(8,128)S(1)} all-to-all(f32[8,40,128]{2,1,0:T(8,128)S(1)} %bitcast.7), channel_id=1, replica_groups={{0,8,16,24,32,40,48,56},{4,12,20,28,36,44,52,60},{64,72,80,88,96,104,11..., dimensions={0} | all-to-all | bytes 327680 | tf_op jit(solution)/shard_map/all_to_all | solution.py:61
  106.6 0.6 last.1
  (10 shorter events, 0.1 us)
Async XLA Ops:
  0.0 32.9 %copy-start.2 = (bf16[4,7,128,128]{3,2,1,0:T(8,128)(2,1)S(1)}, bf16[4,7,128,128]{3,2,1,0:T(8,128)(2,1)}, u32[]{:S(2)}) copy-start(bf16[4,7,128,128]{3,2,1,0:T(8,128)(2,1)} %tiles_ref.5) | copy-start | bytes 2752516
  2.3 30.6 %copy-start = (bf16[30,30,512]{2,1,0:T(8,128)(2,1)S(1)}, bf16[30,30,512]{2,1,0:T(8,128)(2,1)}, u32[]{:S(2)}) copy-start(bf16[30,30,512]{2,1,0:T(8,128)(2,1)} %inv_ref.3) | copy-start | bytes 2764804
  2.3 6.6 %collective-permute-start.2 = (f32[168,128]{1,0:T(8,128)S(1)}, f32[168,128]{1,0:T(8,128)S(1)}, u32[]{:S(2)}, u32[]{:S(2)}) collective-permute-start(f32[168,128]{1,0:T(8,128)S(1)} %get-tuple-element.46.raw0), channel_id=1, source_target_pairs={{0,192},{4,196},{8,200},{12,204},{16,208},{20,212},{24,216},{28,22... | collective-permute-start | bytes 258056 | tf_op jit(solution)/shard_map/ppermute | solution.py:48
  5.1 6.5 %collective-permute-start.1 = (f32[168,128]{1,0:T(8,128)S(1)}, f32[168,128]{1,0:T(8,128)S(1)}, u32[]{:S(2)}, u32[]{:S(2)}) collective-permute-start(f32[168,128]{1,0:T(8,128)S(1)} %get-tuple-element.46.raw0), channel_id=1, source_target_pairs={{0,128},{4,132},{8,136},{12,140},{16,144},{20,148},{24,152},{28,15... | collective-permute-start | bytes 258056 | tf_op jit(solution)/shard_map/ppermute | solution.py:48
  5.9 6.5 %collective-permute-start = (f32[168,128]{1,0:T(8,128)S(1)}, f32[168,128]{1,0:T(8,128)S(1)}, u32[]{:S(2)}, u32[]{:S(2)}) collective-permute-start(f32[168,128]{1,0:T(8,128)S(1)} %get-tuple-element.46.raw0), channel_id=1, source_target_pairs={{0,64},{4,68},{8,72},{12,76},{16,80},{20,84},{24,88},{28,92},{32,9... | collective-permute-start | bytes 258056 | tf_op jit(solution)/shard_map/ppermute | solution.py:48
  6.8 6.1 %collective-permute-start.3 = (f32[40,128]{1,0:T(8,128)S(1)}, f32[40,128]{1,0:T(8,128)S(1)}, u32[]{:S(2)}, u32[]{:S(2)}) collective-permute-start(f32[40,128]{1,0:T(8,128)S(1)} %get-tuple-element.51), channel_id=1, source_target_pairs={{0,1},{1,2},{2,3},{3,0},{4,5},{5,6},{6,7},{7,4},{8,9},{9,10},{10,1... | collective-permute-start | bytes 61448 | tf_op jit(solution)/shard_map/ppermute | solution.py:56
  7.0 5.8 %collective-permute-start.4 = (f32[40,128]{1,0:T(8,128)S(1)}, f32[40,128]{1,0:T(8,128)S(1)}, u32[]{:S(2)}, u32[]{:S(2)}) collective-permute-start(f32[40,128]{1,0:T(8,128)S(1)} %get-tuple-element.52), channel_id=1, source_target_pairs={{0,3},{1,0},{2,1},{3,2},{4,7},{5,4},{6,5},{7,6},{8,11},{9,8},{10,9... | collective-permute-start | bytes 61448 | tf_op jit(solution)/shard_map/ppermute | solution.py:56
  12.9 1.5 %collective-permute-start.5 = (f32[320,128]{1,0:T(8,128)S(1)}, f32[320,128]{1,0:T(8,128)S(1)}, u32[]{:S(2)}, u32[]{:S(2)}) collective-permute-start(f32[320,128]{1,0:T(8,128)S(1)} %get-tuple-element.53), channel_id=1, source_target_pairs={{0,4},{4,0},{8,12},{12,8},{16,20},{20,16},{24,28},{28,24},{32,36},... | collective-permute-start | bytes 491528 | tf_op jit(solution)/shard_map/ppermute | solution.py:52
  14.4 18.5 %copy-start.3 = (bf16[10,10,512]{2,1,0:T(8,128)(2,1)S(1)}, bf16[10,10,512]{2,1,0:T(8,128)(2,1)}, u32[]{:S(2)}) copy-start(bf16[10,10,512]{2,1,0:T(8,128)(2,1)} %jac_ref.3) | copy-start | bytes 307204
  33.9 23.3 %copy-start.1 = (bf16[4,7,128,128]{3,2,1,0:T(8,128)(2,1)S(1)}, bf16[4,7,128,128]{3,2,1,0:T(8,128)(2,1)}, u32[]{:S(2)}) copy-start(bf16[4,7,128,128]{3,2,1,0:T(8,128)(2,1)} %tiles_ref.4) | copy-start | bytes 2752516
  34.0 5.0 %collective-permute-start.8 = (f32[160,128]{1,0:T(8,128)S(1)}, f32[160,128]{1,0:T(8,128)S(1)}, u32[]{:S(2)}, u32[]{:S(2)}) collective-permute-start(f32[160,128]{1,0:T(8,128)S(1)} %get-tuple-element.58.raw0), channel_id=1, source_target_pairs={{0,192},{4,196},{8,200},{12,204},{16,208},{20,212},{24,216},{28,22... | collective-permute-start | bytes 245768 | tf_op jit(solution)/shard_map/ppermute | solution.py:48
  35.4 5.9 %collective-permute-start.7 = (f32[160,128]{1,0:T(8,128)S(1)}, f32[160,128]{1,0:T(8,128)S(1)}, u32[]{:S(2)}, u32[]{:S(2)}) collective-permute-start(f32[160,128]{1,0:T(8,128)S(1)} %get-tuple-element.58.raw0), channel_id=1, source_target_pairs={{0,128},{4,132},{8,136},{12,140},{16,144},{20,148},{24,152},{28,15... | collective-permute-start | bytes 245768 | tf_op jit(solution)/shard_map/ppermute | solution.py:48
  37.0 5.7 %collective-permute-start.6 = (f32[160,128]{1,0:T(8,128)S(1)}, f32[160,128]{1,0:T(8,128)S(1)}, u32[]{:S(2)}, u32[]{:S(2)}) collective-permute-start(f32[160,128]{1,0:T(8,128)S(1)} %get-tuple-element.58.raw0), channel_id=1, source_target_pairs={{0,64},{4,68},{8,72},{12,76},{16,80},{20,84},{24,88},{28,92},{32,9... | collective-permute-start | bytes 245768 | tf_op jit(solution)/shard_map/ppermute | solution.py:48
  37.0 6.0 %collective-permute-start.9 = (f32[40,128]{1,0:T(8,128)S(1)}, f32[40,128]{1,0:T(8,128)S(1)}, u32[]{:S(2)}, u32[]{:S(2)}) collective-permute-start(f32[40,128]{1,0:T(8,128)S(1)} %get-tuple-element.61), channel_id=1, source_target_pairs={{0,1},{1,2},{2,3},{3,0},{4,5},{5,6},{6,7},{7,4},{8,9},{9,10},{10,1... | collective-permute-start | bytes 61448 | tf_op jit(solution)/shard_map/ppermute | solution.py:56
  37.3 5.6 %collective-permute-start.10 = (f32[40,128]{1,0:T(8,128)S(1)}, f32[40,128]{1,0:T(8,128)S(1)}, u32[]{:S(2)}, u32[]{:S(2)}) collective-permute-start(f32[40,128]{1,0:T(8,128)S(1)} %get-tuple-element.62), channel_id=1, source_target_pairs={{0,3},{1,0},{2,1},{3,2},{4,7},{5,4},{6,5},{7,6},{8,11},{9,8},{10,9... | collective-permute-start | bytes 61448 | tf_op jit(solution)/shard_map/ppermute | solution.py:56
  43.0 1.5 %collective-permute-start.11 = (f32[320,128]{1,0:T(8,128)S(1)}, f32[320,128]{1,0:T(8,128)S(1)}, u32[]{:S(2)}, u32[]{:S(2)}) collective-permute-start(f32[320,128]{1,0:T(8,128)S(1)} %get-tuple-element.63), channel_id=1, source_target_pairs={{0,4},{4,0},{8,12},{12,8},{16,20},{20,16},{24,28},{28,24},{32,36},... | collective-permute-start | bytes 491528 | tf_op jit(solution)/shard_map/ppermute | solution.py:52
  57.6 5.8 %collective-permute-start.14 = (f32[160,128]{1,0:T(8,128)S(1)}, f32[160,128]{1,0:T(8,128)S(1)}, u32[]{:S(2)}, u32[]{:S(2)}) collective-permute-start(f32[160,128]{1,0:T(8,128)S(1)} %get-tuple-element.67.raw0), channel_id=1, source_target_pairs={{0,192},{4,196},{8,200},{12,204},{16,208},{20,212},{24,216},{28,22... | collective-permute-start | bytes 245768 | tf_op jit(solution)/shard_map/ppermute | solution.py:48
  60.1 6.0 %collective-permute-start.13 = (f32[160,128]{1,0:T(8,128)S(1)}, f32[160,128]{1,0:T(8,128)S(1)}, u32[]{:S(2)}, u32[]{:S(2)}) collective-permute-start(f32[160,128]{1,0:T(8,128)S(1)} %get-tuple-element.67.raw0), channel_id=1, source_target_pairs={{0,128},{4,132},{8,136},{12,140},{16,144},{20,148},{24,152},{28,15... | collective-permute-start | bytes 245768 | tf_op jit(solution)/shard_map/ppermute | solution.py:48
  60.9 6.0 %collective-permute-start.12 = (f32[160,128]{1,0:T(8,128)S(1)}, f32[160,128]{1,0:T(8,128)S(1)}, u32[]{:S(2)}, u32[]{:S(2)}) collective-permute-start(f32[160,128]{1,0:T(8,128)S(1)} %get-tuple-element.67.raw0), channel_id=1, source_target_pairs={{0,64},{4,68},{8,72},{12,76},{16,80},{20,84},{24,88},{28,92},{32,9... | collective-permute-start | bytes 245768 | tf_op jit(solution)/shard_map/ppermute | solution.py:48
  61.4 5.9 %collective-permute-start.15 = (f32[40,128]{1,0:T(8,128)S(1)}, f32[40,128]{1,0:T(8,128)S(1)}, u32[]{:S(2)}, u32[]{:S(2)}) collective-permute-start(f32[40,128]{1,0:T(8,128)S(1)} %get-tuple-element.70), channel_id=1, source_target_pairs={{0,1},{1,2},{2,3},{3,0},{4,5},{5,6},{6,7},{7,4},{8,9},{9,10},{10,1... | collective-permute-start | bytes 61448 | tf_op jit(solution)/shard_map/ppermute | solution.py:56
  61.7 5.5 %collective-permute-start.16 = (f32[40,128]{1,0:T(8,128)S(1)}, f32[40,128]{1,0:T(8,128)S(1)}, u32[]{:S(2)}, u32[]{:S(2)}) collective-permute-start(f32[40,128]{1,0:T(8,128)S(1)} %get-tuple-element.71), channel_id=1, source_target_pairs={{0,3},{1,0},{2,1},{3,2},{4,7},{5,4},{6,5},{7,6},{8,11},{9,8},{10,9... | collective-permute-start | bytes 61448 | tf_op jit(solution)/shard_map/ppermute | solution.py:56
  67.3 1.5 %collective-permute-start.17 = (f32[320,128]{1,0:T(8,128)S(1)}, f32[320,128]{1,0:T(8,128)S(1)}, u32[]{:S(2)}, u32[]{:S(2)}) collective-permute-start(f32[320,128]{1,0:T(8,128)S(1)} %get-tuple-element.72), channel_id=1, source_target_pairs={{0,4},{4,0},{8,12},{12,8},{16,20},{20,16},{24,28},{28,24},{32,36},... | collective-permute-start | bytes 491528 | tf_op jit(solution)/shard_map/ppermute | solution.py:52
  82.6 5.7 %collective-permute-start.20 = (f32[160,128]{1,0:T(8,128)S(1)}, f32[160,128]{1,0:T(8,128)S(1)}, u32[]{:S(2)}, u32[]{:S(2)}) collective-permute-start(f32[160,128]{1,0:T(8,128)S(1)} %get-tuple-element.76.raw0), channel_id=1, source_target_pairs={{0,192},{4,196},{8,200},{12,204},{16,208},{20,212},{24,216},{28,22... | collective-permute-start | bytes 245768 | tf_op jit(solution)/shard_map/ppermute | solution.py:48
  84.8 5.9 %collective-permute-start.19 = (f32[160,128]{1,0:T(8,128)S(1)}, f32[160,128]{1,0:T(8,128)S(1)}, u32[]{:S(2)}, u32[]{:S(2)}) collective-permute-start(f32[160,128]{1,0:T(8,128)S(1)} %get-tuple-element.76.raw0), channel_id=1, source_target_pairs={{0,128},{4,132},{8,136},{12,140},{16,144},{20,148},{24,152},{28,15... | collective-permute-start | bytes 245768 | tf_op jit(solution)/shard_map/ppermute | solution.py:48
  86.3 5.7 %collective-permute-start.18 = (f32[160,128]{1,0:T(8,128)S(1)}, f32[160,128]{1,0:T(8,128)S(1)}, u32[]{:S(2)}, u32[]{:S(2)}) collective-permute-start(f32[160,128]{1,0:T(8,128)S(1)} %get-tuple-element.76.raw0), channel_id=1, source_target_pairs={{0,64},{4,68},{8,72},{12,76},{16,80},{20,84},{24,88},{28,92},{32,9... | collective-permute-start | bytes 245768 | tf_op jit(solution)/shard_map/ppermute | solution.py:48
  86.3 6.0 %collective-permute-start.21 = (f32[40,128]{1,0:T(8,128)S(1)}, f32[40,128]{1,0:T(8,128)S(1)}, u32[]{:S(2)}, u32[]{:S(2)}) collective-permute-start(f32[40,128]{1,0:T(8,128)S(1)} %get-tuple-element.79), channel_id=1, source_target_pairs={{0,1},{1,2},{2,3},{3,0},{4,5},{5,6},{6,7},{7,4},{8,9},{9,10},{10,1... | collective-permute-start | bytes 61448 | tf_op jit(solution)/shard_map/ppermute | solution.py:56
  86.4 5.9 %collective-permute-start.22 = (f32[40,128]{1,0:T(8,128)S(1)}, f32[40,128]{1,0:T(8,128)S(1)}, u32[]{:S(2)}, u32[]{:S(2)}) collective-permute-start(f32[40,128]{1,0:T(8,128)S(1)} %get-tuple-element.80), channel_id=1, source_target_pairs={{0,3},{1,0},{2,1},{3,2},{4,7},{5,4},{6,5},{7,6},{8,11},{9,8},{10,9... | collective-permute-start | bytes 61448 | tf_op jit(solution)/shard_map/ppermute | solution.py:56
  92.3 1.5 %collective-permute-start.23 = (f32[320,128]{1,0:T(8,128)S(1)}, f32[320,128]{1,0:T(8,128)S(1)}, u32[]{:S(2)}, u32[]{:S(2)}) collective-permute-start(f32[320,128]{1,0:T(8,128)S(1)} %get-tuple-element.81), channel_id=1, source_target_pairs={{0,4},{4,0},{8,12},{12,8},{16,20},{20,16},{24,28},{28,24},{32,36},... | collective-permute-start | bytes 491528 | tf_op jit(solution)/shard_map/ppermute | solution.py:52

commit v7 on v6

--- a/solution.py
+++ b/solution.py
@@ -63,8 +63,8 @@
 
 def emit_terms(blocks, tiles_ref, raw_ref, own_ref, north_ref, south_ref, ready=None):
     for r in range(RB):
-        for copy in ready[r] if ready else ():
-            copy.wait()
+        if ready is not None:
+            ready[r].wait()
         padded = jnp.concatenate([blocks[r], jnp.zeros((16 - TR, BLK), F32)], axis=0)
         left = padded.astype(jnp.bfloat16)
         for t in range(NB):
@@ -102,17 +102,11 @@
         )
     ]
     tile_copies = [
-        [
-            pltpu.make_async_copy(tiles_far.at[r, t], tiles_ref.at[r, t], tile_arrivals.at[r, t])
-            for t in range(NB)
-        ]
+        pltpu.make_async_copy(tiles_far.at[r], tiles_ref.at[r], tile_arrivals.at[r])
         for r in range(RB)
     ]
-    for copy in copies:
+    for copy in tile_copies[:1] + copies + tile_copies[1:]:
         copy.start()
-    for row in tile_copies:
-        for copy in row:
-            copy.start()
     raw_ref[TERMS * TR :, :] = jnp.zeros((2 * RB, BLK), F32)
     for copy in copies:
         copy.wait()
@@ -309,7 +303,7 @@
             *[pltpu.SMEM((RB * BLK // LEV,), jnp.int32)] * 2,
             pltpu.VMEM((RB, NB, BLK, BLK), jnp.bfloat16),
             pltpu.SemaphoreType.DMA((7,)),
-            pltpu.SemaphoreType.DMA((RB, NB)),
+            pltpu.SemaphoreType.DMA((RB,)),
         ],
     )
     raws = gather_x(raw)

time: 107 us -> 107 us (level)
  no operation moved by 1% of the time
where the time goes in v7:
time: 107 us
  blocking collectives  56.7 us (53%)
  starting transfers between devices  23.5 us (22%)
  waiting for transfers between devices  19.9 us (19%)
  Pallas kernels  6.54 us (6%)
    all_to_all x4, blocking collectives, exchange_z(): lax.all_to_all(value, 'cols', 0, 0, axis_index_groups=groups, tiled=True)  56.7 us
    ppermute x12, starting transfers between devices, shift_x(): return lax.ppermute(value, 'cols', pairs)  15 us
    ppermute x12, waiting for transfers between devices, shift_x(): return lax.ppermute(value, 'cols', pairs)  14.4 us
    ppermute x8, starting transfers between devices, ring_lat(): lax.ppermute(value, 'lat', [(i, (i + steps) % N_LAT) for i in range(N_LAT)])  8.1 us
    pallas_call x10, Pallas kernels, call(): pl.pallas_call(kernel, out_shape=out_shape, in_specs=[SMEM] * smem + [VME...  6.54 us
    ppermute x4, waiting for transfers between devices, swap_core(): lax.ppermute(value, 'cols', [(i, i ^ 1) for i in range(NX * NZ * NCORE)])  5.53 us
  transfers between devices with their start and end apart: 24, of which 12 were waited for; matrix products, arithmetic and copies ran while one was open for 0% of the time, Pallas kernels for 1%

profile of v7, /device:TPU:24, one launch (start us, length us, event | category | flops | bytes accessed | tf_op | source)
XLA Modules:
  0.0 106.9 jit_solution(3312282087269412198)
XLA Ops:
  0.0 1.9 %first.1 = (f32[168,128]{1,0:T(8,128)S(1)}, f32[40,128]{1,0:T(8,128)S(1)}, f32[40,128]{1,0:T(8,128)S(1)}, f32[40,128]{1,0:T(8,128)S(1)}, f32[6,128]{1,0:T(8,128)S(1)}, /*index=5*/s32[4,128]{1,0:T(4,128)S(1)}) custom-call(f32[10,512]{1,0:T(8,128)} %field_far.1, s32[4,4]{1,0:T(4,128)} %impl_dest_far.1, s32[4,4]{1,0:T(4,128)} %impl_local_far.1, ...), custom_call_target="tpu_custom_call" | custom-call | bytes 938304 | tf_op jit(solution)/shard_map/first/pallas_call | solution.py:244
  1.9 0.0 copy-start
  1.9 2.8 %collective-permute-start.2 = (f32[168,128]{1,0:T(8,128)S(1)}, f32[168,128]{1,0:T(8,128)S(1)}, u32[]{:S(2)}, u32[]{:S(2)}) collective-permute-start(f32[168,128]{1,0:T(8,128)S(1)} %get-tuple-element.46.raw0), channel_id=1, source_target_pairs={{0,192},{4,196},{8,200},{12,204},{16,208},{20,212},{24,216},{28,22... | collective-permute-start | bytes 258056 | tf_op jit(solution)/shard_map/ppermute | solution.py:48
  4.8 0.8 collective-permute-start.1
  5.6 0.9 collective-permute-start
  6.4 0.2 collective-permute-start.3
  6.7 1.8 %collective-permute-start.4 = (f32[40,128]{1,0:T(8,128)S(1)}, f32[40,128]{1,0:T(8,128)S(1)}, u32[]{:S(2)}, u32[]{:S(2)}) collective-permute-start(f32[40,128]{1,0:T(8,128)S(1)} %get-tuple-element.52), channel_id=1, source_target_pairs={{0,3},{1,0},{2,1},{3,2},{4,7},{5,4},{6,5},{7,6},{8,11},{9,8},{10,9... | collective-permute-start | bytes 61448 | tf_op jit(solution)/shard_map/ppermute | solution.py:56
  8.5 0.0 collective-permute-done.2.raw3
  8.5 2.8 %collective-permute-done.1.raw2 = f32[168,128]{1,0:T(8,128)S(1)} collective-permute-done((f32[168,128]{1,0:T(8,128)S(1)}, f32[168,128]{1,0:T(8,128)S(1)}, u32[]{:S(2)}, u32[]{:S(2)}) %collective-permute-start.1) | collective-permute-done | bytes 86048 | tf_op jit(solution)/shard_map/ppermute | solution.py:48
  11.2 0.9 collective-permute-done.raw1
  12.1 0.4 merge.4
  12.5 0.0 collective-permute-done.3.below_ref
  12.5 0.0 collective-permute-done.4.above_ref
  12.5 0.1 collective-permute-start.5
  12.6 1.4 %collective-permute-done.5 = f32[320,128]{1,0:T(8,128)S(1)} collective-permute-done((f32[320,128]{1,0:T(8,128)S(1)}, f32[320,128]{1,0:T(8,128)S(1)}, u32[]{:S(2)}, u32[]{:S(2)}) %collective-permute-start.5) | collective-permute-done | bytes 163872 | tf_op jit(solution)/shard_map/ppermute | solution.py:52
  14.0 0.0 copy-start.3
  14.0 18.5 %all_to_all.20.slabs_ref = f32[8,40,128]{2,1,0:T(8,128)S(1)} all-to-all(f32[8,40,128]{2,1,0:T(8,128)S(1)} %bitcast.4), channel_id=1, replica_groups={{0,8,16,24,32,40,48,56},{4,12,20,28,36,44,52,60},{64,72,80,88,96,104,11..., dimensions={0} | all-to-all | bytes 327680 | tf_op jit(solution)/shard_map/all_to_all | solution.py:61
  32.5 0.0 copy-done.2
  32.5 1.1 %react.2 = (f32[160,128]{1,0:T(8,128)S(1)}, f32[40,128]{1,0:T(8,128)S(1)}, f32[40,128]{1,0:T(8,128)S(1)}, f32[40,128]{1,0:T(8,128)S(1)}) custom-call(f32[6,128]{1,0:T(8,128)S(1)} %get-tuple-element.45.mask_ref, f32[8,40,128]{2,1,0:T(8,128)S(1)} %all_to_all.20.slabs_ref, f32[40,128]{1,0:T(8,128)S(1)} %get-tuple-element.54.own_in, ...), custom_call_target="tpu_custom_call" | custom-call | bytes 2171904 | tf_op jit(solution)/shard_map/react/pallas_call | solution.py:244
  33.6 1.5 %collective-permute-start.8 = (f32[160,128]{1,0:T(8,128)S(1)}, f32[160,128]{1,0:T(8,128)S(1)}, u32[]{:S(2)}, u32[]{:S(2)}) collective-permute-start(f32[160,128]{1,0:T(8,128)S(1)} %get-tuple-element.58.raw0), channel_id=1, source_target_pairs={{0,192},{4,196},{8,200},{12,204},{16,208},{20,212},{24,216},{28,22... | collective-permute-start | bytes 245768 | tf_op jit(solution)/shard_map/ppermute | solution.py:48
  35.1 1.5 %collective-permute-start.7 = (f32[160,128]{1,0:T(8,128)S(1)}, f32[160,128]{1,0:T(8,128)S(1)}, u32[]{:S(2)}, u32[]{:S(2)}) collective-permute-start(f32[160,128]{1,0:T(8,128)S(1)} %get-tuple-element.58.raw0), channel_id=1, source_target_pairs={{0,128},{4,132},{8,136},{12,140},{16,144},{20,148},{24,152},{28,15... | collective-permute-start | bytes 245768 | tf_op jit(solution)/shard_map/ppermute | solution.py:48
  36.6 0.0 collective-permute-start.6
  36.6 0.4 collective-permute-start.9
  37.0 1.7 %collective-permute-start.10 = (f32[40,128]{1,0:T(8,128)S(1)}, f32[40,128]{1,0:T(8,128)S(1)}, u32[]{:S(2)}, u32[]{:S(2)}) collective-permute-start(f32[40,128]{1,0:T(8,128)S(1)} %get-tuple-element.62), channel_id=1, source_target_pairs={{0,3},{1,0},{2,1},{3,2},{4,7},{5,4},{6,5},{7,6},{8,11},{9,8},{10,9... | collective-permute-start | bytes 61448 | tf_op jit(solution)/shard_map/ppermute | solution.py:56
  38.6 0.0 collective-permute-done.8.raw3
  38.6 2.4 %collective-permute-done.7.raw2 = f32[160,128]{1,0:T(8,128)S(1)} collective-permute-done((f32[160,128]{1,0:T(8,128)S(1)}, f32[160,128]{1,0:T(8,128)S(1)}, u32[]{:S(2)}, u32[]{:S(2)}) %collective-permute-start.7) | collective-permute-done | bytes 81952 | tf_op jit(solution)/shard_map/ppermute | solution.py:48
  41.0 1.2 %collective-permute-done.6.raw1 = f32[160,128]{1,0:T(8,128)S(1)} collective-permute-done((f32[160,128]{1,0:T(8,128)S(1)}, f32[160,128]{1,0:T(8,128)S(1)}, u32[]{:S(2)}, u32[]{:S(2)}) %collective-permute-start.6) | collective-permute-done | bytes 81952 | tf_op jit(solution)/shard_map/ppermute | solution.py:48
  42.2 0.4 merge.5
  42.6 0.0 collective-permute-done.9.below_ref
  42.6 0.0 collective-permute-done.10.above_ref
  42.6 0.1 collective-permute-start.11
  42.7 1.4 %collective-permute-done.11 = f32[320,128]{1,0:T(8,128)S(1)} collective-permute-done((f32[320,128]{1,0:T(8,128)S(1)}, f32[320,128]{1,0:T(8,128)S(1)}, u32[]{:S(2)}, u32[]{:S(2)}) %collective-permute-start.11) | collective-permute-done | bytes 163872 | tf_op jit(solution)/shard_map/ppermute | solution.py:52
  44.2 12.7 %all_to_all.21.slabs_ref = f32[8,40,128]{2,1,0:T(8,128)S(1)} all-to-all(f32[8,40,128]{2,1,0:T(8,128)S(1)} %bitcast.5), channel_id=1, replica_groups={{0,8,16,24,32,40,48,56},{4,12,20,28,36,44,52,60},{64,72,80,88,96,104,11..., dimensions={0} | all-to-all | bytes 327680 | tf_op jit(solution)/shard_map/all_to_all | solution.py:61
  56.9 0.3 step.1
  57.2 2.5 %collective-permute-start.14 = (f32[160,128]{1,0:T(8,128)S(1)}, f32[160,128]{1,0:T(8,128)S(1)}, u32[]{:S(2)}, u32[]{:S(2)}) collective-permute-start(f32[160,128]{1,0:T(8,128)S(1)} %get-tuple-element.67.raw0), channel_id=1, source_target_pairs={{0,192},{4,196},{8,200},{12,204},{16,208},{20,212},{24,216},{28,22... | collective-permute-start | bytes 245768 | tf_op jit(solution)/shard_map/ppermute | solution.py:48
  59.7 0.8 collective-permute-start.13
  60.5 0.5 collective-permute-start.12
  61.0 0.4 collective-permute-start.15
  61.4 1.7 %collective-permute-start.16 = (f32[40,128]{1,0:T(8,128)S(1)}, f32[40,128]{1,0:T(8,128)S(1)}, u32[]{:S(2)}, u32[]{:S(2)}) collective-permute-start(f32[40,128]{1,0:T(8,128)S(1)} %get-tuple-element.71), channel_id=1, source_target_pairs={{0,3},{1,0},{2,1},{3,2},{4,7},{5,4},{6,5},{7,6},{8,11},{9,8},{10,9... | collective-permute-start | bytes 61448 | tf_op jit(solution)/shard_map/ppermute | solution.py:56
  63.0 0.0 collective-permute-done.14.raw3
  63.0 2.7 %collective-permute-done.13.raw2 = f32[160,128]{1,0:T(8,128)S(1)} collective-permute-done((f32[160,128]{1,0:T(8,128)S(1)}, f32[160,128]{1,0:T(8,128)S(1)}, u32[]{:S(2)}, u32[]{:S(2)}) %collective-permute-start.13) | collective-permute-done | bytes 81952 | tf_op jit(solution)/shard_map/ppermute | solution.py:48
  65.7 0.8 collective-permute-done.12.raw1
  66.6 0.4 merge.6
  66.9 0.0 collective-permute-done.15.below_ref
  66.9 0.0 collective-permute-done.16.above_ref
  67.0 0.1 collective-permute-start.17
  67.1 1.4 %collective-permute-done.17 = f32[320,128]{1,0:T(8,128)S(1)} collective-permute-done((f32[320,128]{1,0:T(8,128)S(1)}, f32[320,128]{1,0:T(8,128)S(1)}, u32[]{:S(2)}, u32[]{:S(2)}) %collective-permute-start.17) | collective-permute-done | bytes 163872 | tf_op jit(solution)/shard_map/ppermute | solution.py:52
  68.5 12.7 %all_to_all.22.slabs_ref = f32[8,40,128]{2,1,0:T(8,128)S(1)} all-to-all(f32[8,40,128]{2,1,0:T(8,128)S(1)} %bitcast.6), channel_id=1, replica_groups={{0,8,16,24,32,40,48,56},{4,12,20,28,36,44,52,60},{64,72,80,88,96,104,11..., dimensions={0} | all-to-all | bytes 327680 | tf_op jit(solution)/shard_map/all_to_all | solution.py:61
  81.2 1.1 %react.3 = (f32[160,128]{1,0:T(8,128)S(1)}, f32[40,128]{1,0:T(8,128)S(1)}, f32[40,128]{1,0:T(8,128)S(1)}, f32[40,128]{1,0:T(8,128)S(1)}) custom-call(f32[6,128]{1,0:T(8,128)S(1)} %get-tuple-element.45.mask_ref, f32[8,40,128]{2,1,0:T(8,128)S(1)} %all_to_all.22.slabs_ref, f32[40,128]{1,0:T(8,128)S(1)} %get-tuple-element.73.own_in, ...), custom_call_target="tpu_custom_call" | custom-call | bytes 2171904 | tf_op jit(solution)/shard_map/react/pallas_call | solution.py:244
  82.3 2.2 %collective-permute-start.20 = (f32[160,128]{1,0:T(8,128)S(1)}, f32[160,128]{1,0:T(8,128)S(1)}, u32[]{:S(2)}, u32[]{:S(2)}) collective-permute-start(f32[160,128]{1,0:T(8,128)S(1)} %get-tuple-element.76.raw0), channel_id=1, source_target_pairs={{0,192},{4,196},{8,200},{12,204},{16,208},{20,212},{24,216},{28,22... | collective-permute-start | bytes 245768 | tf_op jit(solution)/shard_map/ppermute | solution.py:48
  84.4 1.5 %collective-permute-start.19 = (f32[160,128]{1,0:T(8,128)S(1)}, f32[160,128]{1,0:T(8,128)S(1)}, u32[]{:S(2)}, u32[]{:S(2)}) collective-permute-start(f32[160,128]{1,0:T(8,128)S(1)} %get-tuple-element.76.raw0), channel_id=1, source_target_pairs={{0,128},{4,132},{8,136},{12,140},{16,144},{20,148},{24,152},{28,15... | collective-permute-start | bytes 245768 | tf_op jit(solution)/shard_map/ppermute | solution.py:48
  86.0 0.0 collective-permute-start.18
  86.0 0.1 collective-permute-start.21
  86.0 2.0 %collective-permute-start.22 = (f32[40,128]{1,0:T(8,128)S(1)}, f32[40,128]{1,0:T(8,128)S(1)}, u32[]{:S(2)}, u32[]{:S(2)}) collective-permute-start(f32[40,128]{1,0:T(8,128)S(1)} %get-tuple-element.80), channel_id=1, source_target_pairs={{0,3},{1,0},{2,1},{3,2},{4,7},{5,4},{6,5},{7,6},{8,11},{9,8},{10,9... | collective-permute-start | bytes 61448 | tf_op jit(solution)/shard_map/ppermute | solution.py:56
  88.0 0.0 collective-permute-done.20.raw3
  88.0 2.4 %collective-permute-done.19.raw2 = f32[160,128]{1,0:T(8,128)S(1)} collective-permute-done((f32[160,128]{1,0:T(8,128)S(1)}, f32[160,128]{1,0:T(8,128)S(1)}, u32[]{:S(2)}, u32[]{:S(2)}) %collective-permute-start.19) | collective-permute-done | bytes 81952 | tf_op jit(solution)/shard_map/ppermute | solution.py:48
  90.4 1.2 %collective-permute-done.18.raw1 = f32[160,128]{1,0:T(8,128)S(1)} collective-permute-done((f32[160,128]{1,0:T(8,128)S(1)}, f32[160,128]{1,0:T(8,128)S(1)}, u32[]{:S(2)}, u32[]{:S(2)}) %collective-permute-start.18) | collective-permute-done | bytes 81952 | tf_op jit(solution)/shard_map/ppermute | solution.py:48
  91.6 0.4 merge.7
  92.0 0.0 collective-permute-done.21.below_ref
  92.0 0.0 collective-permute-done.22.above_ref
  92.0 0.1 collective-permute-start.23
  92.1 1.4 %collective-permute-done.23 = f32[320,128]{1,0:T(8,128)S(1)} collective-permute-done((f32[320,128]{1,0:T(8,128)S(1)}, f32[320,128]{1,0:T(8,128)S(1)}, u32[]{:S(2)}, u32[]{:S(2)}) %collective-permute-start.23) | collective-permute-done | bytes 163872 | tf_op jit(solution)/shard_map/ppermute | solution.py:52
  93.5 12.7 %all_to_all.23.slabs_ref = f32[8,40,128]{2,1,0:T(8,128)S(1)} all-to-all(f32[8,40,128]{2,1,0:T(8,128)S(1)} %bitcast.7), channel_id=1, replica_groups={{0,8,16,24,32,40,48,56},{4,12,20,28,36,44,52,60},{64,72,80,88,96,104,11..., dimensions={0} | all-to-all | bytes 327680 | tf_op jit(solution)/shard_map/all_to_all | solution.py:61
  106.3 0.6 last.1
  (10 shorter events, 0.1 us)
Async XLA Ops:
  0.0 32.5 %copy-start.2 = (bf16[4,7,128,128]{3,2,1,0:T(8,128)(2,1)S(1)}, bf16[4,7,128,128]{3,2,1,0:T(8,128)(2,1)}, u32[]{:S(2)}) copy-start(bf16[4,7,128,128]{3,2,1,0:T(8,128)(2,1)} %tiles_ref.5) | copy-start | bytes 2752516
  1.9 30.6 %copy-start = (bf16[30,30,512]{2,1,0:T(8,128)(2,1)S(1)}, bf16[30,30,512]{2,1,0:T(8,128)(2,1)}, u32[]{:S(2)}) copy-start(bf16[30,30,512]{2,1,0:T(8,128)(2,1)} %inv_ref.3) | copy-start | bytes 2764804
  1.9 6.6 %collective-permute-start.2 = (f32[168,128]{1,0:T(8,128)S(1)}, f32[168,128]{1,0:T(8,128)S(1)}, u32[]{:S(2)}, u32[]{:S(2)}) collective-permute-start(f32[168,128]{1,0:T(8,128)S(1)} %get-tuple-element.46.raw0), channel_id=1, source_target_pairs={{0,192},{4,196},{8,200},{12,204},{16,208},{20,212},{24,216},{28,22... | collective-permute-start | bytes 258056 | tf_op jit(solution)/shard_map/ppermute | solution.py:48
  4.8 6.5 %collective-permute-start.1 = (f32[168,128]{1,0:T(8,128)S(1)}, f32[168,128]{1,0:T(8,128)S(1)}, u32[]{:S(2)}, u32[]{:S(2)}) collective-permute-start(f32[168,128]{1,0:T(8,128)S(1)} %get-tuple-element.46.raw0), channel_id=1, source_target_pairs={{0,128},{4,132},{8,136},{12,140},{16,144},{20,148},{24,152},{28,15... | collective-permute-start | bytes 258056 | tf_op jit(solution)/shard_map/ppermute | solution.py:48
  5.6 6.5 %collective-permute-start = (f32[168,128]{1,0:T(8,128)S(1)}, f32[168,128]{1,0:T(8,128)S(1)}, u32[]{:S(2)}, u32[]{:S(2)}) collective-permute-start(f32[168,128]{1,0:T(8,128)S(1)} %get-tuple-element.46.raw0), channel_id=1, source_target_pairs={{0,64},{4,68},{8,72},{12,76},{16,80},{20,84},{24,88},{28,92},{32,9... | collective-permute-start | bytes 258056 | tf_op jit(solution)/shard_map/ppermute | solution.py:48
  6.4 6.1 %collective-permute-start.3 = (f32[40,128]{1,0:T(8,128)S(1)}, f32[40,128]{1,0:T(8,128)S(1)}, u32[]{:S(2)}, u32[]{:S(2)}) collective-permute-start(f32[40,128]{1,0:T(8,128)S(1)} %get-tuple-element.51), channel_id=1, source_target_pairs={{0,1},{1,2},{2,3},{3,0},{4,5},{5,6},{6,7},{7,4},{8,9},{9,10},{10,1... | collective-permute-start | bytes 61448 | tf_op jit(solution)/shard_map/ppermute | solution.py:56
  6.7 5.9 %collective-permute-start.4 = (f32[40,128]{1,0:T(8,128)S(1)}, f32[40,128]{1,0:T(8,128)S(1)}, u32[]{:S(2)}, u32[]{:S(2)}) collective-permute-start(f32[40,128]{1,0:T(8,128)S(1)} %get-tuple-element.52), channel_id=1, source_target_pairs={{0,3},{1,0},{2,1},{3,2},{4,7},{5,4},{6,5},{7,6},{8,11},{9,8},{10,9... | collective-permute-start | bytes 61448 | tf_op jit(solution)/shard_map/ppermute | solution.py:56
  12.5 1.5 %collective-permute-start.5 = (f32[320,128]{1,0:T(8,128)S(1)}, f32[320,128]{1,0:T(8,128)S(1)}, u32[]{:S(2)}, u32[]{:S(2)}) collective-permute-start(f32[320,128]{1,0:T(8,128)S(1)} %get-tuple-element.53), channel_id=1, source_target_pairs={{0,4},{4,0},{8,12},{12,8},{16,20},{20,16},{24,28},{28,24},{32,36},... | collective-permute-start | bytes 491528 | tf_op jit(solution)/shard_map/ppermute | solution.py:52
  14.0 18.5 %copy-start.3 = (bf16[10,10,512]{2,1,0:T(8,128)(2,1)S(1)}, bf16[10,10,512]{2,1,0:T(8,128)(2,1)}, u32[]{:S(2)}) copy-start(bf16[10,10,512]{2,1,0:T(8,128)(2,1)} %jac_ref.3) | copy-start | bytes 307204
  33.6 23.3 %copy-start.1 = (bf16[4,7,128,128]{3,2,1,0:T(8,128)(2,1)S(1)}, bf16[4,7,128,128]{3,2,1,0:T(8,128)(2,1)}, u32[]{:S(2)}) copy-start(bf16[4,7,128,128]{3,2,1,0:T(8,128)(2,1)} %tiles_ref.4) | copy-start | bytes 2752516
  33.6 5.0 %collective-permute-start.8 = (f32[160,128]{1,0:T(8,128)S(1)}, f32[160,128]{1,0:T(8,128)S(1)}, u32[]{:S(2)}, u32[]{:S(2)}) collective-permute-start(f32[160,128]{1,0:T(8,128)S(1)} %get-tuple-element.58.raw0), channel_id=1, source_target_pairs={{0,192},{4,196},{8,200},{12,204},{16,208},{20,212},{24,216},{28,22... | collective-permute-start | bytes 245768 | tf_op jit(solution)/shard_map/ppermute | solution.py:48
  35.1 5.9 %collective-permute-start.7 = (f32[160,128]{1,0:T(8,128)S(1)}, f32[160,128]{1,0:T(8,128)S(1)}, u32[]{:S(2)}, u32[]{:S(2)}) collective-permute-start(f32[160,128]{1,0:T(8,128)S(1)} %get-tuple-element.58.raw0), channel_id=1, source_target_pairs={{0,128},{4,132},{8,136},{12,140},{16,144},{20,148},{24,152},{28,15... | collective-permute-start | bytes 245768 | tf_op jit(solution)/shard_map/ppermute | solution.py:48
  36.6 5.7 %collective-permute-start.6 = (f32[160,128]{1,0:T(8,128)S(1)}, f32[160,128]{1,0:T(8,128)S(1)}, u32[]{:S(2)}, u32[]{:S(2)}) collective-permute-start(f32[160,128]{1,0:T(8,128)S(1)} %get-tuple-element.58.raw0), channel_id=1, source_target_pairs={{0,64},{4,68},{8,72},{12,76},{16,80},{20,84},{24,88},{28,92},{32,9... | collective-permute-start | bytes 245768 | tf_op jit(solution)/shard_map/ppermute | solution.py:48
  36.6 6.0 %collective-permute-start.9 = (f32[40,128]{1,0:T(8,128)S(1)}, f32[40,128]{1,0:T(8,128)S(1)}, u32[]{:S(2)}, u32[]{:S(2)}) collective-permute-start(f32[40,128]{1,0:T(8,128)S(1)} %get-tuple-element.61), channel_id=1, source_target_pairs={{0,1},{1,2},{2,3},{3,0},{4,5},{5,6},{6,7},{7,4},{8,9},{9,10},{10,1... | collective-permute-start | bytes 61448 | tf_op jit(solution)/shard_map/ppermute | solution.py:56
  37.0 5.7 %collective-permute-start.10 = (f32[40,128]{1,0:T(8,128)S(1)}, f32[40,128]{1,0:T(8,128)S(1)}, u32[]{:S(2)}, u32[]{:S(2)}) collective-permute-start(f32[40,128]{1,0:T(8,128)S(1)} %get-tuple-element.62), channel_id=1, source_target_pairs={{0,3},{1,0},{2,1},{3,2},{4,7},{5,4},{6,5},{7,6},{8,11},{9,8},{10,9... | collective-permute-start | bytes 61448 | tf_op jit(solution)/shard_map/ppermute | solution.py:56
  42.6 1.5 %collective-permute-start.11 = (f32[320,128]{1,0:T(8,128)S(1)}, f32[320,128]{1,0:T(8,128)S(1)}, u32[]{:S(2)}, u32[]{:S(2)}) collective-permute-start(f32[320,128]{1,0:T(8,128)S(1)} %get-tuple-element.63), channel_id=1, source_target_pairs={{0,4},{4,0},{8,12},{12,8},{16,20},{20,16},{24,28},{28,24},{32,36},... | collective-permute-start | bytes 491528 | tf_op jit(solution)/shard_map/ppermute | solution.py:52
  57.2 5.8 %collective-permute-start.14 = (f32[160,128]{1,0:T(8,128)S(1)}, f32[160,128]{1,0:T(8,128)S(1)}, u32[]{:S(2)}, u32[]{:S(2)}) collective-permute-start(f32[160,128]{1,0:T(8,128)S(1)} %get-tuple-element.67.raw0), channel_id=1, source_target_pairs={{0,192},{4,196},{8,200},{12,204},{16,208},{20,212},{24,216},{28,22... | collective-permute-start | bytes 245768 | tf_op jit(solution)/shard_map/ppermute | solution.py:48
  59.7 6.0 %collective-permute-start.13 = (f32[160,128]{1,0:T(8,128)S(1)}, f32[160,128]{1,0:T(8,128)S(1)}, u32[]{:S(2)}, u32[]{:S(2)}) collective-permute-start(f32[160,128]{1,0:T(8,128)S(1)} %get-tuple-element.67.raw0), channel_id=1, source_target_pairs={{0,128},{4,132},{8,136},{12,140},{16,144},{20,148},{24,152},{28,15... | collective-permute-start | bytes 245768 | tf_op jit(solution)/shard_map/ppermute | solution.py:48
  60.5 6.0 %collective-permute-start.12 = (f32[160,128]{1,0:T(8,128)S(1)}, f32[160,128]{1,0:T(8,128)S(1)}, u32[]{:S(2)}, u32[]{:S(2)}) collective-permute-start(f32[160,128]{1,0:T(8,128)S(1)} %get-tuple-element.67.raw0), channel_id=1, source_target_pairs={{0,64},{4,68},{8,72},{12,76},{16,80},{20,84},{24,88},{28,92},{32,9... | collective-permute-start | bytes 245768 | tf_op jit(solution)/shard_map/ppermute | solution.py:48
  61.0 5.9 %collective-permute-start.15 = (f32[40,128]{1,0:T(8,128)S(1)}, f32[40,128]{1,0:T(8,128)S(1)}, u32[]{:S(2)}, u32[]{:S(2)}) collective-permute-start(f32[40,128]{1,0:T(8,128)S(1)} %get-tuple-element.70), channel_id=1, source_target_pairs={{0,1},{1,2},{2,3},{3,0},{4,5},{5,6},{6,7},{7,4},{8,9},{9,10},{10,1... | collective-permute-start | bytes 61448 | tf_op jit(solution)/shard_map/ppermute | solution.py:56
  61.4 5.6 %collective-permute-start.16 = (f32[40,128]{1,0:T(8,128)S(1)}, f32[40,128]{1,0:T(8,128)S(1)}, u32[]{:S(2)}, u32[]{:S(2)}) collective-permute-start(f32[40,128]{1,0:T(8,128)S(1)} %get-tuple-element.71), channel_id=1, source_target_pairs={{0,3},{1,0},{2,1},{3,2},{4,7},{5,4},{6,5},{7,6},{8,11},{9,8},{10,9... | collective-permute-start | bytes 61448 | tf_op jit(solution)/shard_map/ppermute | solution.py:56
  67.0 1.5 %collective-permute-start.17 = (f32[320,128]{1,0:T(8,128)S(1)}, f32[320,128]{1,0:T(8,128)S(1)}, u32[]{:S(2)}, u32[]{:S(2)}) collective-permute-start(f32[320,128]{1,0:T(8,128)S(1)} %get-tuple-element.72), channel_id=1, source_target_pairs={{0,4},{4,0},{8,12},{12,8},{16,20},{20,16},{24,28},{28,24},{32,36},... | collective-permute-start | bytes 491528 | tf_op jit(solution)/shard_map/ppermute | solution.py:52
  82.3 5.7 %collective-permute-start.20 = (f32[160,128]{1,0:T(8,128)S(1)}, f32[160,128]{1,0:T(8,128)S(1)}, u32[]{:S(2)}, u32[]{:S(2)}) collective-permute-start(f32[160,128]{1,0:T(8,128)S(1)} %get-tuple-element.76.raw0), channel_id=1, source_target_pairs={{0,192},{4,196},{8,200},{12,204},{16,208},{20,212},{24,216},{28,22... | collective-permute-start | bytes 245768 | tf_op jit(solution)/shard_map/ppermute | solution.py:48
  84.4 5.9 %collective-permute-start.19 = (f32[160,128]{1,0:T(8,128)S(1)}, f32[160,128]{1,0:T(8,128)S(1)}, u32[]{:S(2)}, u32[]{:S(2)}) collective-permute-start(f32[160,128]{1,0:T(8,128)S(1)} %get-tuple-element.76.raw0), channel_id=1, source_target_pairs={{0,128},{4,132},{8,136},{12,140},{16,144},{20,148},{24,152},{28,15... | collective-permute-start | bytes 245768 | tf_op jit(solution)/shard_map/ppermute | solution.py:48
  86.0 5.7 %collective-permute-start.18 = (f32[160,128]{1,0:T(8,128)S(1)}, f32[160,128]{1,0:T(8,128)S(1)}, u32[]{:S(2)}, u32[]{:S(2)}) collective-permute-start(f32[160,128]{1,0:T(8,128)S(1)} %get-tuple-element.76.raw0), channel_id=1, source_target_pairs={{0,64},{4,68},{8,72},{12,76},{16,80},{20,84},{24,88},{28,92},{32,9... | collective-permute-start | bytes 245768 | tf_op jit(solution)/shard_map/ppermute | solution.py:48
  86.0 6.0 %collective-permute-start.21 = (f32[40,128]{1,0:T(8,128)S(1)}, f32[40,128]{1,0:T(8,128)S(1)}, u32[]{:S(2)}, u32[]{:S(2)}) collective-permute-start(f32[40,128]{1,0:T(8,128)S(1)} %get-tuple-element.79), channel_id=1, source_target_pairs={{0,1},{1,2},{2,3},{3,0},{4,5},{5,6},{6,7},{7,4},{8,9},{9,10},{10,1... | collective-permute-start | bytes 61448 | tf_op jit(solution)/shard_map/ppermute | solution.py:56
  86.0 6.0 %collective-permute-start.22 = (f32[40,128]{1,0:T(8,128)S(1)}, f32[40,128]{1,0:T(8,128)S(1)}, u32[]{:S(2)}, u32[]{:S(2)}) collective-permute-start(f32[40,128]{1,0:T(8,128)S(1)} %get-tuple-element.80), channel_id=1, source_target_pairs={{0,3},{1,0},{2,1},{3,2},{4,7},{5,4},{6,5},{7,6},{8,11},{9,8},{10,9... | collective-permute-start | bytes 61448 | tf_op jit(solution)/shard_map/ppermute | solution.py:56
  92.0 1.5 %collective-permute-start.23 = (f32[320,128]{1,0:T(8,128)S(1)}, f32[320,128]{1,0:T(8,128)S(1)}, u32[]{:S(2)}, u32[]{:S(2)}) collective-permute-start(f32[320,128]{1,0:T(8,128)S(1)} %get-tuple-element.81), channel_id=1, source_target_pairs={{0,4},{4,0},{8,12},{12,8},{16,20},{20,16},{24,28},{28,24},{32,36},... | collective-permute-start | bytes 491528 | tf_op jit(solution)/shard_map/ppermute | solution.py:52
